TPU v7x, 32 devices: a whole 2x2x4 slice. The times are simulated.
32 devices in a mesh: mom: 8 (over z, y), tm: 4 (over x, core).
Axes of the slice: x: 2, y: 2, z: 4, core: 2. Of those that a mesh axis runs over, the one named last changes fastest.
Arguments:
- hist_lesser: float32 [2, 256, 16, 2048], P(None, 'mom', None, 'tm'), may hold values from -2 to 6
- hist_retarded: float32 [2, 256, 16, 2048], P(None, 'mom', None, 'tm'), may hold values from -4 to 4
- propagator: float32 [2, 256, 16, 16], P(None, 'mom'), may hold values from -0.5 to 1.5
- coupling: float32 [256], replicated, may hold values from 0.15 to 0.4
- mf_weight: float32 [256], replicated, may hold values from 0.5 to 2
- lag_weight: float32 [8], replicated, may hold values from 0.05 to 0.2
Outputs:
- new_slice: float32 [2, 256, 16, 2048], P(None, 'mom', None, 'tm')
All inputs are finite; a program needn't handle non-finite values.
Results may differ from a plain program's by a relative error of at most 0.0003.
Values sent between devices are 32-bit elements; how exact they have to be, the bound alone decides.
No kernel may reach another device: no remote copies, remote signals or barrier semaphores. Data moves between devices by JAX's collectives and lax.ppermute only.
A program may use at most 128 MiB of HBM per device.

v0:
```python
import math

import jax
import jax.numpy as jnp
from jax import lax
from jax.sharding import PartitionSpec as P

KX = 16
KY = 16
ORB = 16
W = 8
PASSES = 3


HIGHEST = lax.Precision.HIGHEST


def shifted(x, axis, by):
    peers = lax.axis_size(axis)
    pairs = [(i, i + by) for i in range(peers) if 0 <= i + by < peers]
    return lax.ppermute(x, axis, pairs)


def broadcast(x, axis, root):
    mine = lax.axis_index(axis) == root
    return lax.psum(jnp.where(mine, x, jnp.zeros_like(x)), axis)


def momentum_tables():
    index = jnp.arange(KX * KY, dtype=jnp.int32)
    first = index // KY
    second = index % KY
    turn_x = first[:, None] * first[None, :] % KX
    turn_y = second[:, None] * second[None, :] % KY
    phase = 2.0 * math.pi * (turn_x.astype(jnp.float32) / KX + turn_y.astype(jnp.float32) / KY)
    scale = 1.0 / math.sqrt(KX * KY)
    return (jnp.cos(phase) * scale, jnp.sin(phase) * scale)


def complex_product(pattern, first, second):
    real = jnp.einsum(pattern, first[0], second[0], precision=HIGHEST) - jnp.einsum(
        pattern, first[1], second[1], precision=HIGHEST
    )
    imaginary = jnp.einsum(pattern, first[0], second[1], precision=HIGHEST) + jnp.einsum(
        pattern, first[1], second[0], precision=HIGHEST
    )
    return jnp.stack([real, imaginary])


def back_to_momenta(real, imaginary, cosine, sine):
    out_real = jnp.dot(cosine, real, precision=HIGHEST) + jnp.dot(
        sine, imaginary, precision=HIGHEST
    )
    out_imag = jnp.dot(cosine, imaginary, precision=HIGHEST) - jnp.dot(
        sine, real, precision=HIGHEST
    )
    return jnp.stack([out_real, out_imag])


def local_products(arrived, cosine, sine, strength, lag_mark):
    lag_count = lag_mark.shape[0]
    space_real = jnp.dot(cosine, arrived[0], precision=HIGHEST) - jnp.dot(
        sine, arrived[1], precision=HIGHEST
    )
    space_imag = jnp.dot(cosine, arrived[1], precision=HIGHEST) + jnp.dot(
        sine, arrived[0], precision=HIGHEST
    )
    column_strength = jnp.repeat(strength, lag_count)
    magnitude = column_strength * (space_real * space_real + space_imag * space_imag)
    lesser_real = magnitude * space_real
    lesser_imag = magnitude * space_imag
    pair_real = column_strength * (space_real * space_real - space_imag * space_imag)
    pair_imag = column_strength * 2.0 * space_real * space_imag
    return (
        back_to_momenta(lesser_real, lesser_imag, cosine, sine),
        back_to_momenta(pair_real, pair_imag, cosine, sine),
    )


def self_energies(window, cosine, sine, strength, mf_weight, last_mark):
    momenta_here = window.shape[1]
    outgoing = window.reshape(2, momenta_here, ORB * ORB * W)
    arrived = lax.all_to_all(outgoing, "mom", split_axis=2, concat_axis=1, tiled=True)
    lesser_r, pair_r = local_products(arrived, cosine, sine, strength, last_mark)
    back_lesser, back_pair = (
        lax.all_to_all(lesser_r, "mom", split_axis=1, concat_axis=2, tiled=True),
        lax.all_to_all(pair_r, "mom", split_axis=1, concat_axis=2, tiled=True),
    )
    sigma = back_lesser.reshape(2, momenta_here, ORB, ORB, W)
    pair_k = back_pair.reshape(2, momenta_here, ORB, ORB, W)
    own_total = jnp.sum(window[..., W - 1], axis=1)
    occupation = lax.psum(own_total, "mom") / (KX * KY)
    sigma = sigma + (mf_weight.reshape(ORB, ORB) * occupation)[:, None, :, :, None] * last_mark
    return (sigma, pair_k)


def collide(sigma, pair_k, lag_weight, padded_r, padded_l, first, count):
    weighted_sigma = sigma * lag_weight
    weighted_pair = pair_k * lag_weight

    def ladder(padded):
        region = lax.dynamic_slice_in_dim(padded, first * ORB, (count + W - 1) * ORB, 3)
        return jnp.stack(
            [region[..., offset * ORB : (offset + count) * ORB] for offset in range(W)], axis=3
        )

    return complex_product("kabm,kbmx->kax", weighted_sigma, ladder(padded_r)) + complex_product(
        "kabm,kbmx->kax", weighted_pair, ladder(padded_l)
    )


def on_device(hist_lesser, hist_retarded, propagator, coupling, mf_weight, lag_weight):
    momenta_here = hist_lesser.shape[1]
    times_here = hist_lesser.shape[3] // ORB
    cosine, sine = momentum_tables()
    lesser = hist_lesser.reshape(2, momenta_here, ORB, times_here, ORB)
    start = complex_product("kab,kbjc->kajc", propagator, lesser).reshape(
        2, momenta_here, ORB, times_here * ORB
    )
    rim_width = (W - 1) * ORB
    rim_retarded, rim_lesser = shifted(
        (
            hist_retarded[..., times_here * ORB - rim_width :],
            hist_lesser[..., times_here * ORB - rim_width :],
        ),
        "tm",
        1,
    )
    padded_r = jnp.concatenate([rim_retarded, hist_retarded], axis=3)
    padded_l = jnp.concatenate([rim_lesser, hist_lesser], axis=3)
    block = min(32, times_here)
    count_blocks = times_here // block
    window_start = (times_here - W) * ORB
    pair_count = ORB * ORB // lax.axis_size("mom")
    strength = lax.dynamic_slice_in_dim(
        coupling * coupling, lax.axis_index("mom") * pair_count, pair_count, 0
    )
    last_mark = (jnp.arange(W) == W - 1).astype(jnp.float32)
    owner = lax.axis_size("tm") - 1
    current = start[..., window_start:]
    full_slice = start
    for sweep in range(PASSES):
        shared = broadcast(current, "tm", owner)
        window = jnp.transpose(shared.reshape(2, momenta_here, ORB, W, ORB), (0, 1, 2, 4, 3))
        sigma, pair_k = self_energies(window, cosine, sine, strength, mf_weight, last_mark)
        if sweep + 1 < PASSES:
            collision = collide(sigma, pair_k, lag_weight, padded_r, padded_l, times_here - W, W)
            current = start[..., window_start:] + jnp.stack([collision[1], -collision[0]])
        else:
            blocks_out = lax.map(
                lambda number: collide(
                    sigma, pair_k, lag_weight, padded_r, padded_l, number * block, block
                ),
                jnp.arange(count_blocks, dtype=jnp.int32),
            )
            collision = jnp.moveaxis(blocks_out, 0, 3).reshape(
                2, momenta_here, ORB, times_here * ORB
            )
            full_slice = start + jnp.stack([collision[1], -collision[0]])
            current = full_slice[..., window_start:]
    return full_slice


def solution(mesh):
    return jax.shard_map(
        on_device,
        mesh=mesh,
        in_specs=(
            P(None, "mom", None, "tm"),
            P(None, "mom", None, "tm"),
            P(None, "mom", None, None),
            P(),
            P(),
            P(),
        ),
        out_specs=P(None, "mom", None, "tm"),
        check_vma=False,
    )
```

profile of v0, /device:TPU:0, one launch (start us, length us, event | category | flops | bytes accessed | tf_op | source)
XLA Modules:
  0.0 890.7 jit_solution(3552777212641367255)
XLA Ops:
  11.1 6.5 copy.116
  20.6 6.5 copy.113
  27.2 5.5 fusion.136
  32.7 5.2 fusion.138
  37.9 5.1 convolution_add_fusion
  43.0 5.9 copy.120
  52.2 9.2 %convolution_subtract_fusion = f32[32,16,32,16]{2,1,3,0:T(8,128)} fusion(f32[32,16,32,16]{2,1,3,0:T(8,128)} %fusion.138, f32[32,16,32,16]{2,1,3,0:T(8,128)} %copy.116, f32[1,32,16,16]{3,2,1,0:T(8,128)S(1)} %copy.208), kind=kOutput, calls=%fused_computation.43 | convolution fusion | flops 50593792 | bytes 3178496 | tf_op jit(solution)/shard_map/kab,kbjc->kajc/dot_general | solution.py:41
  61.4 5.9 copy.117
  87.6 42.6 %all-reduce.4.cloned.1.call-done = f32[2,32,16,16,8]{1,3,4,2,0:T(8,128)} async-done(((f32[2,32,16,16,8]{1,3,4,2,0:T(8,128)}), f32[2,32,16,16,8]{1,3,4,2,0:T(8,128)}) %all-reduce.4.cloned.1.call-update) | async-done | bytes 524304 | tf_op jit(solution)/shard_map/psum | solution.py:26
  132.7 9.0 %copy.215 = f32[2,32,2048]{1,0,2:T(2,128)} copy(f32[2,32,2048]{1,2,0:T(8,128)S(1)} %bitcast.679) | data formatting | bytes 1048576 | tf_op jit(solution)/shard_map/reshape | solution.py:82
  141.6 4.3 reshape.183
  145.9 5.5 all-to-all-start
  154.6 11.4 %all-to-all-done = f32[8,1,16384]{2,1,0:T(1,128)} async-done(((f32[8,1,16384]{2,1,0:T(1,128)}), f32[8,1,16384]{2,1,0:T(1,128)}, u32[]{:S(2)}, u32[]{:S(2)}) %all-to-all-start) | async-done | bytes 524320 | tf_op jit(solution)/shard_map/all_to_all | solution.py:83
  192.6 4.1 all-to-all-start.2
  206.7 4.4 all-to-all-done.2
  211.0 4.1 all-to-all-start.1
  217.2 37.5 %psum.43 = f32[2,16,16]{2,1,0:T(8,128)S(1)} all-reduce(f32[2,16,16]{2,1,0:T(8,128)S(1)} %slice_reduce_fusion.2), channel_id=1, replica_groups=mesh['mom'=8,'tm'=4] {'mom'}, use_global_device_ids=true, to_apply=%region_2.3 | all-reduce | flops 512 | bytes 4096 | tf_op jit(solution)/shard_map/psum | solution.py:92
  259.7 5.6 copy.136
  270.2 5.8 copy.132
  275.9 4.7 broadcast_multiply_fusion.2
  280.6 4.2 fusion.106
  284.9 4.3 fusion.105
  289.1 4.5 fusion.102
  293.6 4.3 fusion.101
  297.9 4.2 fusion.110
  302.1 4.6 fusion.112
  306.8 4.3 fusion.114
  311.0 4.2 fusion.116
  323.5 48.3 %all-reduce.6.cloned.1.call-done = f32[2,32,16,16,8]{1,3,4,2,0:T(8,128)} async-done(((f32[2,32,16,16,8]{1,3,4,2,0:T(8,128)}), f32[2,32,16,16,8]{1,3,4,2,0:T(8,128)}) %all-reduce.6.cloned.1.call-update) | async-done | bytes 524304 | tf_op jit(solution)/shard_map/psum | solution.py:26
  374.3 8.7 copy.214
  383.1 4.3 reshape.185
  387.4 5.5 all-to-all-start.3
  435.0 5.9 all-to-all-start.5
  450.8 5.4 all-to-all-done.5
  456.2 4.1 all-to-all-start.4
  471.6 37.4 %psum.45 = f32[2,16,16]{2,1,0:T(8,128)S(1)} all-reduce(f32[2,16,16]{2,1,0:T(8,128)S(1)} %slice_reduce_fusion.1), channel_id=1, replica_groups=mesh['mom'=8,'tm'=4] {'mom'}, use_global_device_ids=true, to_apply=%region_5.6 | all-reduce | flops 512 | bytes 4096 | tf_op jit(solution)/shard_map/psum | solution.py:92
  514.0 5.6 copy.150
  524.4 5.9 copy.146
  530.4 4.7 broadcast_multiply_fusion.1
  535.1 4.2 fusion.98
  539.3 4.3 fusion.97
  543.6 4.4 fusion.94
  548.0 4.3 fusion.93
  552.3 4.2 fusion.118
  556.5 4.5 fusion.120
  561.0 4.3 fusion.122
  565.2 4.2 fusion.124
  579.5 41.4 %all-reduce.8.cloned.1.call-done = f32[2,32,16,16,8]{1,3,4,2,0:T(8,128)} async-done(((f32[2,32,16,16,8]{1,3,4,2,0:T(8,128)}), f32[2,32,16,16,8]{1,3,4,2,0:T(8,128)}) %all-reduce.8.cloned.1.call-update) | async-done | bytes 524304 | tf_op jit(solution)/shard_map/psum | solution.py:26
  623.4 9.0 %copy.213 = f32[2,32,2048]{1,0,2:T(2,128)} copy(f32[2,32,2048]{1,2,0:T(8,128)S(1)} %bitcast.681) | data formatting | bytes 1048576 | tf_op jit(solution)/shard_map/reshape | solution.py:82
  632.3 4.3 reshape.187
  636.6 5.5 all-to-all-start.6
  682.6 5.4 all-to-all-start.8
  711.9 38.0 %psum.47 = f32[2,16,16]{2,1,0:T(8,128)S(1)} all-reduce(f32[2,16,16]{2,1,0:T(8,128)S(1)} %slice_reduce_fusion), channel_id=1, replica_groups=mesh['mom'=8,'tm'=4] {'mom'}, use_global_device_ids=true, to_apply=%region_8.9 | all-reduce | flops 512 | bytes 4096 | tf_op jit(solution)/shard_map/psum | solution.py:92
  753.5 4.5 copy.170
  761.5 4.5 copy.160
  766.1 4.5 broadcast_multiply_fusion
  770.6 13.7 %fusion.72 = f32[32,16,512]{2,1,0:T(8,128)S(1)} fusion(f32[2,32,16,8,512]{4,2,3,1,0:T(8,128)} %bitcast_dynamic-update-slice_fusion.1, f32[2,32,16,16,8]{3,2,4,1,0:T(8,128)S(1)} %get-tuple-element.43), kind=kOutput, calls=%fused_computation.132 | convolution fusion | flops 402653184 | bytes 11534336 | tf_op jit(solution)/shard_map/while/body/eval_jaxpr/kabm,kbmx->kax/dot_general | solution.py:44
  784.3 13.7 %fusion.69 = f32[32,16,512]{2,1,0:T(8,128)S(1)} fusion(f32[2,32,16,8,512]{4,2,3,1,0:T(8,128)} %bitcast_dynamic-update-slice_fusion.1, f32[2,32,16,16,8]{3,2,4,1,0:T(8,128)S(1)} %get-tuple-element.43), kind=kOutput, calls=%fused_computation.129 | convolution fusion | flops 402653184 | bytes 11534336 | tf_op jit(solution)/shard_map/while/body/eval_jaxpr/kabm,kbmx->kax/dot_general | solution.py:41
  798.0 13.9 %fusion.68 = f32[32,16,512]{2,1,0:T(8,128)S(1)} fusion(f32[2,32,16,8,512]{4,2,3,1,0:T(8,128)} %bitcast_dynamic-update-slice_fusion, f32[2,32,16,16,8]{3,2,4,1,0:T(8,128)S(1)} %get-tuple-element.42), kind=kOutput, calls=%fused_computation.128 | convolution fusion | flops 402653184 | bytes 11534336 | tf_op jit(solution)/shard_map/while/body/eval_jaxpr/kabm,kbmx->kax/dot_general | solution.py:44
  811.9 13.5 %fusion.65 = f32[32,16,512]{2,1,0:T(8,128)S(1)} fusion(f32[2,32,16,8,512]{4,2,3,1,0:T(8,128)} %bitcast_dynamic-update-slice_fusion, f32[2,32,16,16,8]{3,2,4,1,0:T(8,128)S(1)} %get-tuple-element.42), kind=kOutput, calls=%fused_computation.125 | convolution fusion | flops 402653184 | bytes 11534336 | tf_op jit(solution)/shard_map/while/body/eval_jaxpr/kabm,kbmx->kax/dot_general | solution.py:41
  825.5 13.7 %fusion.76 = f32[1,32,16,512]{3,2,1,0:T(8,128)S(1)} fusion(f32[32,16,512]{2,1,0:T(8,128)S(1)} %fusion.72, f32[2,32,16,8,512]{4,2,3,1,0:T(8,128)} %bitcast_dynamic-update-slice_fusion.1, f32[2,32,16,16,8]{3,2,4,1,0:T(8,128)S(1)} %get-tuple-element.43), kind=kOutput, calls=%fused_computation.136 | convolution fusion | flops 402915328 | bytes 12582912 | tf_op jit(solution)/shard_map/while/body/eval_jaxpr/kabm,kbmx->kax/dot_general | solution.py:44
  839.2 14.0 %fusion.74 = f32[1,32,16,512]{3,2,1,0:T(8,128)S(1)} fusion(f32[32,16,512]{2,1,0:T(8,128)S(1)} %fusion.69, f32[2,32,16,8,512]{4,2,3,1,0:T(8,128)} %bitcast_dynamic-update-slice_fusion.1, f32[2,32,16,16,8]{3,2,4,1,0:T(8,128)S(1)} %get-tuple-element.43), kind=kOutput, calls=%fused_computation.134 | convolution fusion | flops 402915328 | bytes 12582912 | tf_op jit(solution)/shard_map/while/body/eval_jaxpr/kabm,kbmx->kax/dot_general | solution.py:41
  853.2 13.8 %fusion.80 = f32[1,32,16,512]{3,2,1,0:T(8,128)S(1)} fusion(f32[32,16,512]{2,1,0:T(8,128)S(1)} %fusion.68, f32[2,32,16,8,512]{4,2,3,1,0:T(8,128)} %bitcast_dynamic-update-slice_fusion, f32[2,32,16,16,8]{3,2,4,1,0:T(8,128)S(1)} %get-tuple-element.42), kind=kOutput, calls=%fused_computation.140 | convolution fusion | flops 402915328 | bytes 12582912 | tf_op jit(solution)/shard_map/while/body/eval_jaxpr/kabm,kbmx->kax/dot_general | solution.py:44
  867.0 13.9 %fusion.78 = f32[1,32,16,512]{3,2,1,0:T(8,128)S(1)} fusion(f32[32,16,512]{2,1,0:T(8,128)S(1)} %fusion.65, f32[2,32,16,8,512]{4,2,3,1,0:T(8,128)} %bitcast_dynamic-update-slice_fusion, f32[2,32,16,16,8]{3,2,4,1,0:T(8,128)S(1)} %get-tuple-element.42), kind=kOutput, calls=%fused_computation.138 | convolution fusion | flops 402915328 | bytes 12582912 | tf_op jit(solution)/shard_map/while/body/eval_jaxpr/kabm,kbmx->kax/dot_general | solution.py:41
  (232 shorter events, 255.2 us)
Async XLA Ops:
  6.5 123.7 %all-reduce.4.cloned.1.call-start = ((), (), s32[]{:S(2)}) async-start(), calls=%async_computation.9 | async-start | bytes 4194304 | tf_op jit(solution)/shard_map/psum | solution.py:26
  11.1 6.5 copy-start.14
  27.2 5.5 copy-start.10
  71.0 4.9 copy-start
  76.0 5.4 copy-start.1
  77.0 7.2 copy-start.16
  82.3 2.0 copy-start.7
  132.7 18.8 %copy-start.17 = (f32[256]{0:T(256)S(1)}, f32[256]{0:T(256)}, u32[]{:S(2)}) copy-start(f32[256]{0:T(256)} %param.10) | copy-start | bytes 3076
  145.9 20.0 %all-to-all-start = ((f32[8,1,16384]{2,1,0:T(1,128)}), f32[8,1,16384]{2,1,0:T(1,128)}, u32[]{:S(2)}, u32[]{:S(2)}) async-start(f32[8,1,16384]{2,1,0:T(1,128)} %reshape.183), calls=%async_computation | async-start | bytes 1048576 | tf_op jit(solution)/shard_map/all_to_all | solution.py:83
  182.9 6.4 copy-start.22
  184.5 6.8 copy-start.26
  192.6 18.4 %all-to-all-start.2 = ((f32[2,256,256]{2,0,1:T(2,128)}), f32[2,256,256]{2,0,1:T(2,128)}, u32[]{:S(2)}, u32[]{:S(2)}) async-start(f32[2,256,256]{2,0,1:T(2,128)} %copy.133), calls=%async_computation.2 | async-start | bytes 1048576 | tf_op jit(solution)/shard_map/all_to_all | solution.py:87
  196.7 5.4 copy-start.23
  196.7 5.4 copy-start.27
  211.0 54.3 %all-to-all-start.1 = ((f32[2,256,256]{2,0,1:T(2,128)}), f32[2,256,256]{2,0,1:T(2,128)}, u32[]{:S(2)}, u32[]{:S(2)}) async-start(f32[2,256,256]{2,0,1:T(2,128)} %copy.129), calls=%async_computation.1 | async-start | bytes 1048576 | tf_op jit(solution)/shard_map/all_to_all | solution.py:86
  215.2 156.7 %all-reduce.6.cloned.1.call-start = ((), (), s32[]{:S(2)}) async-start(), calls=%async_computation.10 | async-start | bytes 4194304 | tf_op jit(solution)/shard_map/psum | solution.py:26
  267.2 8.8 copy-start.15
  275.9 4.7 copy-start.8
  280.6 8.5 copy-start.5
  311.0 4.4 copy-start.11
  321.4 74.7 %collective-permute-start = (f32[2,32,16,112]{3,2,1,0:T(8,128)}, f32[2,32,16,112]{3,2,1,0:T(8,128)}, u32[]{:S(2)}, u32[]{:S(2)}) collective-permute-start(f32[2,32,16,112]{3,2,1,0:T(8,128)} %slice.370), channel_id=1, source_target_pairs={{0,1},{1,2},{2,3},{4,5},{5,6},{6,7},{8,9},{9,10},{10,11},{12,13},{... | collective-permute-start | bytes 1376264 | tf_op jit(solution)/shard_map/ppermute | solution.py:21
  387.4 21.5 %all-to-all-start.3 = ((f32[8,1,16384]{2,1,0:T(1,128)}), f32[8,1,16384]{2,1,0:T(1,128)}, u32[]{:S(2)}, u32[]{:S(2)}) async-start(f32[8,1,16384]{2,1,0:T(1,128)} %reshape.185), calls=%async_computation.3 | async-start | bytes 1048576 | tf_op jit(solution)/shard_map/all_to_all | solution.py:83
  392.9 6.8 copy-start.2
  393.9 179.6 %collective-permute-start.1 = (f32[2,32,16,112]{3,2,1,0:T(8,128)}, f32[2,32,16,112]{3,2,1,0:T(8,128)}, u32[]{:S(2)}, u32[]{:S(2)}) collective-permute-start(f32[2,32,16,112]{3,2,1,0:T(8,128)} %slice.382), channel_id=1, source_target_pairs={{0,1},{1,2},{2,3},{4,5},{5,6},{6,7},{8,9},{9,10},{10,11},{12,13},{... | collective-permute-start | bytes 1376264 | tf_op jit(solution)/shard_map/ppermute | solution.py:21
  425.6 6.4 copy-start.24
  427.1 6.6 copy-start.28
  435.0 21.2 %all-to-all-start.5 = ((f32[2,256,256]{2,0,1:T(2,128)}), f32[2,256,256]{2,0,1:T(2,128)}, u32[]{:S(2)}, u32[]{:S(2)}) async-start(f32[2,256,256]{2,0,1:T(2,128)} %copy.147), calls=%async_computation.5 | async-start | bytes 1048576 | tf_op jit(solution)/shard_map/all_to_all | solution.py:87
  440.9 5.4 copy-start.25
  440.9 5.4 copy-start.29
  456.2 63.3 %all-to-all-start.4 = ((f32[2,256,256]{2,0,1:T(2,128)}), f32[2,256,256]{2,0,1:T(2,128)}, u32[]{:S(2)}, u32[]{:S(2)}) async-start(f32[2,256,256]{2,0,1:T(2,128)} %copy.143), calls=%async_computation.4 | async-start | bytes 1048576 | tf_op jit(solution)/shard_map/all_to_all | solution.py:86
  460.4 160.5 %all-reduce.8.cloned.1.call-start = ((), (), s32[]{:S(2)}) async-start(), calls=%async_computation.11 | async-start | bytes 4194304 | tf_op jit(solution)/shard_map/psum | solution.py:26
  460.4 3.9 copy-start.3
  530.4 4.7 copy-start.9
  535.1 8.5 copy-start.6
  565.2 4.4 copy-start.12
  636.6 20.0 %all-to-all-start.6 = ((f32[8,1,16384]{2,1,0:T(1,128)}), f32[8,1,16384]{2,1,0:T(1,128)}, u32[]{:S(2)}, u32[]{:S(2)}) async-start(f32[8,1,16384]{2,1,0:T(1,128)} %reshape.187), calls=%async_computation.6 | async-start | bytes 1048576 | tf_op jit(solution)/shard_map/all_to_all | solution.py:83
  648.3 6.3 copy-start.4
  673.1 6.4 copy-start.18
  674.7 6.7 copy-start.20
  682.6 19.4 %all-to-all-start.8 = ((f32[2,256,256]{2,0,1:T(2,128)}), f32[2,256,256]{2,0,1:T(2,128)}, u32[]{:S(2)}, u32[]{:S(2)}) async-start(f32[2,256,256]{2,0,1:T(2,128)} %copy.167), calls=%async_computation.8 | async-start | bytes 1048576 | tf_op jit(solution)/shard_map/all_to_all | solution.py:87
  688.0 5.4 copy-start.19
  688.0 5.4 copy-start.21
  702.0 56.0 %all-to-all-start.7 = ((f32[2,256,256]{2,0,1:T(2,128)}), f32[2,256,256]{2,0,1:T(2,128)}, u32[]{:S(2)}, u32[]{:S(2)}) async-start(f32[2,256,256]{2,0,1:T(2,128)} %copy.157), calls=%async_computation.7 | async-start | bytes 1048576 | tf_op jit(solution)/shard_map/all_to_all | solution.py:86
  880.9 1.2 copy-start.13
Sparse Core Ops, SparseCore 0:
  76.1 54.0 all-reduce.3
  319.4 52.3 all-reduce.5
  573.6 47.2 all-reduce.7
where the time goes:
time: 902 us; the launch traced here: 891 us
  matrix products  269 us (30%)
  local copies, waits for them, and re-layouts  208 us (23%)
  waiting for transfers between devices  158 us (18%)
  blocking collectives  113 us (13%)
  other arithmetic  79.3 us (9%)
  starting transfers between devices  48.7 us (5%)
  between operations  14.5 us (2%)
    psum x3, waiting for transfers between devices, broadcast(): return lax.psum(jnp.where(mine, x, jnp.zeros_like(x)), axis)  132 us
    psum x3, blocking collectives, self_energies(): occupation = lax.psum(own_total, 'mom') / (KX * KY)  113 us
    dot_general x7, matrix products, complex_product(): jnp.einsum(pattern, first[1], second[1], precision=HIGHEST)  53.4 us
    dot_general x7, matrix products, complex_product(): jnp.einsum(pattern, first[0], second[0], precision=HIGHEST)  50.6 us
    dot_general x7, matrix products, complex_product(): jnp.einsum(pattern, first[1], second[0], precision=HIGHEST)  50.1 us
    dot_general x7, matrix products, complex_product(): jnp.einsum(pattern, first[0], second[1], precision=HIGHEST)  50 us
    unnamed x84, local copies, waits for them, and re-layouts  45.9 us
    unnamed x14, other arithmetic  44.2 us
  transfers between devices with their start and end apart: 14, of which 8 were waited for; matrix products, arithmetic and copies ran while one was open for 25% of the time, Pallas kernels for 0%

commit v1 on v0

--- a/solution.py
+++ b/solution.py
@@ -1,8 +1,12 @@
+import functools
 import math
 
 import jax
 import jax.numpy as jnp
+import numpy as np
 from jax import lax
+from jax.experimental import pallas as pl
+from jax.experimental.pallas import tpu as pltpu
 from jax.sharding import PartitionSpec as P
 
 KX = 16
@@ -109,7 +113,7 @@
     )
 
 
-def on_device(hist_lesser, hist_retarded, propagator, coupling, mf_weight, lag_weight):
+def on_device_any(hist_lesser, hist_retarded, propagator, coupling, mf_weight, lag_weight):
     momenta_here = hist_lesser.shape[1]
     times_here = hist_lesser.shape[3] // ORB
     cosine, sine = momentum_tables()
@@ -161,6 +165,290 @@
     return full_slice
 
 
+VMEM = pl.BlockSpec(memory_space=pltpu.VMEM)
+HALF = W * ORB // 2
+TILE = W * ORB
+PARAMS = pltpu.CompilerParams(vmem_limit_bytes=48 * 1024 * 1024)
+
+
+def halves(x):
+    high = x.astype(jnp.bfloat16)
+    return high, (x - high.astype(jnp.float32)).astype(jnp.bfloat16)
+
+
+def matmul(first, second):
+    return jnp.dot(first, second, preferred_element_type=jnp.float32)
+
+
+def fourier_tables():
+    index = np.arange(KX * KY)
+    turn = np.outer(index // KY, index // KY) / KX + np.outer(index % KY, index % KY) / KY
+    phase = 2.0 * np.pi * (turn % 1.0)
+    table = np.concatenate([np.cos(phase), np.sin(phase)]) / math.sqrt(KX * KY)
+    high = table.astype(jnp.bfloat16)
+    low = (table - high.astype(np.float64)).astype(jnp.bfloat16)
+    return jnp.asarray(high), jnp.asarray(low)
+
+
+def lower_lanes(shape):
+    return lax.broadcasted_iota(jnp.int32, shape, 1) < HALF
+
+
+def store_window(send_ref, k, own, real, imag):
+    lower = lower_lanes(real.shape)
+    turned_real = pltpu.roll(real, HALF, 1)
+    turned_imag = pltpu.roll(imag, HALF, 1)
+    send_ref[pl.ds(k, ORB, stride=2 * own), :] = jnp.where(lower, real, turned_imag)
+    send_ref[pl.ds(own + k, ORB, stride=2 * own), :] = jnp.where(lower, turned_real, imag)
+
+
+def first_window_kernel(own, propagator_ref, lesser_ref, send_ref):
+    for k in range(own):
+        left = jnp.concatenate([propagator_ref[0, k], propagator_ref[1, k]], axis=0)
+        right = jnp.concatenate([lesser_ref[0, k], lesser_ref[1, k]], axis=1)
+        both = jnp.dot(left, right, precision=HIGHEST, preferred_element_type=jnp.float32)
+        real = both[:ORB, :TILE] - both[ORB:, TILE:]
+        imag = both[:ORB, TILE:] + both[ORB:, :TILE]
+        store_window(send_ref, k, own, real, imag)
+
+
+def fourier_kernel(arrived_ref, high_ref, low_ref, strength_ref, mean_ref, out_ref):
+    count = KX * KY
+    x_high, x_low = halves(arrived_ref[...])
+    main = matmul(high_ref[...], jnp.concatenate([x_high, x_low], axis=1))
+    turned = main[:, :TILE] + main[:, TILE:] + matmul(low_ref[...], x_high)
+    lower = lower_lanes((count, TILE))
+    sine_part = pltpu.roll(turned[count:], HALF, 1)
+    here = turned[:count] + jnp.where(lower, -sine_part, sine_part)
+    swapped = pltpu.roll(here, HALF, 1)
+    real = jnp.where(lower, here, swapped)
+    imag = jnp.where(lower, swapped, here)
+    real_square = real * real
+    imag_square = imag * imag
+    size = real_square + imag_square
+    strength = strength_ref[...]
+    out_real = strength * jnp.where(lower, size * real, real_square - imag_square)
+    out_imag = strength * jnp.where(lower, size * imag, 2.0 * real * imag)
+    origin = (lax.broadcasted_iota(jnp.int32, (count, TILE), 0) == 0).astype(jnp.float32)
+    mean = origin * mean_ref[...]
+    out_real = out_real + mean * real
+    out_imag = out_imag + mean * imag
+    real_high, real_low = halves(out_real)
+    imag_high, imag_low = halves(out_imag)
+    y_high = jnp.concatenate([real_high, imag_high], axis=1)
+    y_low = jnp.concatenate([real_low, imag_low], axis=1)
+    back = matmul(high_ref[...], y_high) + matmul(low_ref[...], y_high) + matmul(high_ref[...], y_low)
+    devices, rows, _ = out_ref.shape
+    own = rows // 2
+    out_ref[:, :own] = (back[:count, :TILE] + back[count:, TILE:]).reshape(devices, own, TILE)
+    out_ref[:, own:] = (back[:count, TILE:] - back[count:, :TILE]).reshape(devices, own, TILE)
+
+
+def coefficients(arrived_ref, start_ref, k, k_start, own):
+    def piece(part, half):
+        return arrived_ref[pl.ds((2 * half + part) * own + k, ORB, stride=4 * own), :]
+
+    rows = [
+        jnp.concatenate([piece(part, 0), piece(part, 1) + start_ref[part, k_start]], axis=1) for part in range(2)
+    ]
+    return halves(jnp.concatenate(rows, axis=0))
+
+
+def ladder(regions, width):
+    rows = []
+    for half in range(2):
+        for kind in range(2):
+            for lag in range(W // 2):
+                offset = ORB * (1 + half * (W // 2) + lag)
+                rows.append(jnp.concatenate([x[:, offset : offset + width] for x in regions[kind]], axis=1))
+    return jnp.concatenate(rows, axis=0)
+
+
+def contract(left_high, left_low, right_high, right_low, width):
+    rows = 2 * ORB
+    main = matmul(jnp.concatenate([left_high, left_low], axis=0), right_high)
+    both = main[:rows] + main[rows:] + matmul(left_high, right_low)
+    real = both[:ORB, :width] - both[ORB:, width:]
+    imag = both[:ORB, width:] + both[ORB:, :width]
+    return imag, -real
+
+
+def window_ladder_kernel(own, retarded_ref, lesser_ref, high_ref, low_ref):
+    for k in range(own):
+        regions = [[ref[part, k] for part in range(2)] for ref in (retarded_ref, lesser_ref)]
+        high_ref[k], low_ref[k] = halves(ladder(regions, TILE))
+
+
+def window_kernel(own, arrived_ref, start_ref, high_ref, low_ref, send_ref):
+    for k in range(own):
+        left_high, left_low = coefficients(arrived_ref, start_ref, k, k, own)
+        real, imag = contract(left_high, left_low, high_ref[k], low_ref[k], TILE)
+        store_window(send_ref, k, own, real, imag)
+
+
+def final_kernel(own, tm_ref, arrived_ref, start_ref, retarded_ref, lesser_ref, rim_retarded_ref, rim_lesser_ref, out_ref):
+    width = retarded_ref.shape[3]
+
+    def step(k, carry):
+        left_high, left_low = coefficients(arrived_ref.at[0], start_ref, k, k, own)
+        regions = [
+            [jnp.concatenate([rim[part, k], ref[part, k]], axis=1) for part in range(2)]
+            for rim, ref in ((rim_retarded_ref, retarded_ref), (rim_lesser_ref, lesser_ref))
+        ]
+        right_high, right_low = halves(ladder(regions, width))
+        out_ref[0, k], out_ref[1, k] = contract(left_high, left_low, right_high, right_low, width)
+        return carry
+
+    lax.fori_loop(0, own, step, 0)
+
+
+def own_block(x, own, axis):
+    return lax.dynamic_slice_in_dim(x, lax.axis_index("tm") * own, own, axis)
+
+
+def scatter(x, own):
+    peers = lax.axis_size("tm")
+    parts = [lax.ppermute(x[:, t * own : (t + 1) * own], "tm", [(peers - 1, t)]) for t in range(peers - 1)]
+    mine = x[:, (peers - 1) * own :]
+    arrived = functools.reduce(jnp.add, parts)
+    return jnp.where(lax.axis_index("tm") == peers - 1, mine, arrived)
+
+
+def on_device_tiled(hist_lesser, hist_retarded, propagator, coupling, mf_weight, lag_weight):
+    both_axes = ("mom", "tm")
+    momenta_here = hist_lesser.shape[1]
+    columns = hist_lesser.shape[3]
+    peers = lax.axis_size("tm")
+    devices = lax.axis_size("mom") * peers
+    own = momenta_here // peers
+    count = KX * KY
+
+    first = scatter(hist_lesser[..., columns - TILE :], own)
+    rest = scatter(
+        jnp.concatenate(
+            [
+                hist_retarded[..., columns - 2 * TILE : columns - TILE],
+                hist_retarded[..., columns - TILE :],
+                hist_lesser[..., columns - 2 * TILE : columns - TILE],
+            ],
+            axis=0,
+        ),
+        own,
+    )
+    near_retarded = jnp.concatenate([rest[0:2], rest[2:4]], axis=3)
+    near_lesser = jnp.concatenate([rest[4:6], first], axis=3)
+    rim_retarded, rim_lesser = shifted(
+        (hist_retarded[..., columns - TILE :], hist_lesser[..., columns - TILE :]), "tm", 1
+    )
+
+    me = lax.axis_index("mom") * peers + lax.axis_index("tm")
+    last_mark = (jnp.arange(W) == W - 1).astype(jnp.float32)
+    strong = (coupling * coupling).reshape(ORB, 1, ORB) * lag_weight[:, None]
+    mean = mf_weight.reshape(ORB, 1, ORB) * (lag_weight * last_mark)[:, None]
+    strong = lax.dynamic_slice_in_dim(strong.reshape(devices, HALF), me, 1, 0)
+    mean = lax.dynamic_slice_in_dim(mean.reshape(devices, HALF), me, 1, 0)
+    strength = jnp.concatenate([strong, strong], axis=1)
+    mean = jnp.concatenate([mean, jnp.zeros_like(mean)], axis=1)
+    start = jnp.pad(
+        jnp.stack([-propagator[1], propagator[0]]), ((0, 0), (0, 0), (0, 0), (TILE - ORB, 0))
+    )
+    start_own = own_block(start, own, 1)
+    table_high, table_low = fourier_tables()
+
+    def call(kernel, shapes, *operands):
+        return pl.pallas_call(
+            kernel,
+            out_shape=shapes,
+            in_specs=[VMEM] * len(operands),
+            out_specs=jax.tree.map(lambda _: VMEM, shapes),
+            compiler_params=PARAMS,
+        )(*operands)
+
+    f32 = functools.partial(jax.ShapeDtypeStruct, dtype=jnp.float32)
+    bf16 = functools.partial(jax.ShapeDtypeStruct, dtype=jnp.bfloat16)
+    send = call(
+        functools.partial(first_window_kernel, own), f32((count, TILE)), own_block(propagator, own, 1), first
+    )
+    rungs = bf16((own, 2 * TILE, 2 * TILE))
+    rungs_high, rungs_low = call(
+        functools.partial(window_ladder_kernel, own), (rungs, rungs), near_retarded, near_lesser
+    )
+    for sweep in range(PASSES):
+        arrived = lax.all_to_all(send.reshape(devices, own, TILE), both_axes, 0, 0, tiled=True)
+        back = call(
+            fourier_kernel,
+            f32((devices, 2 * own, TILE)),
+            arrived.reshape(count, TILE),
+            table_high,
+            table_low,
+            strength,
+            mean,
+        )
+        arrived = lax.all_to_all(back, both_axes, 0, 0, tiled=True).reshape(2 * count, TILE)
+        if sweep + 1 < PASSES:
+            send = call(
+                functools.partial(window_kernel, own),
+                f32((count, TILE)),
+                arrived,
+                start_own,
+                rungs_high,
+                rungs_low,
+            )
+
+    blocks = [arrived]
+    distance = peers // 2
+    gathered = {0: arrived}
+    while distance:
+        for known in list(gathered):
+            gathered[known ^ distance] = lax.ppermute(
+                gathered[known], "tm", [(t, t ^ distance) for t in range(peers)]
+            )
+        distance //= 2
+    blocks = jnp.stack([gathered[s] for s in range(peers)])
+
+    def momenta(s, tm_ref):
+        return (0, tm_ref[0] ^ s, 0, 0)
+
+    def spec(width):
+        return pl.BlockSpec((2, own, ORB, width), momenta)
+
+    return pl.pallas_call(
+        functools.partial(final_kernel, own),
+        out_shape=f32(hist_lesser.shape),
+        grid_spec=pltpu.PrefetchScalarGridSpec(
+            num_scalar_prefetch=1,
+            grid=(peers,),
+            in_specs=[
+                pl.BlockSpec((1, 2 * count, TILE), lambda s, tm_ref: (s, 0, 0)),
+                spec(TILE),
+                spec(columns),
+                spec(columns),
+                spec(TILE),
+                spec(TILE),
+            ],
+            out_specs=spec(columns),
+        ),
+        compiler_params=PARAMS,
+    )(
+        lax.axis_index("tm").reshape(1).astype(jnp.int32),
+        blocks,
+        start,
+        hist_retarded,
+        hist_lesser,
+        rim_retarded,
+        rim_lesser,
+    )
+
+
+def on_device(hist_lesser, *others):
+    peers = lax.axis_size("tm")
+    devices = lax.axis_size("mom") * peers
+    own, rest = divmod(hist_lesser.shape[1], peers)
+    fits = devices == 2 * ORB and rest == 0 and own % 8 == 0 and peers & (peers - 1) == 0
+    fits = fits and hist_lesser.shape[3] >= 2 * TILE and hist_lesser.shape[3] % TILE == 0
+    return (on_device_tiled if fits else on_device_any)(hist_lesser, *others)
+
+
 def solution(mesh):
     return jax.shard_map(
         on_device,

time: 902 us -> 139 us (0.15)
  the two profiles are of different devices: /device:TPU:0 before, /device:TPU:1 now
where the time goes in v1:
time: 139 us; the launch traced here: 138 us
  blocking collectives  45.5 us (33%)
  waiting for transfers between devices  31.8 us (23%)
  Pallas kernels  28.1 us (20%)
  starting transfers between devices  24.1 us (17%)
  local copies, waits for them, and re-layouts  6.34 us (5%)
  other arithmetic  2.24 us (2%)
    all_to_all x2, blocking collectives, on_device_tiled(): lax.all_to_all(back, both_axes, 0, 0, tiled=True).reshape(2 * count, TILE)  24.1 us
    all_to_all x2, blocking collectives, on_device_tiled(): lax.all_to_all(send.reshape(devices, own, TILE), both_axes, 0, 0, tiled=T...  21.4 us
    pallas_call x1, Pallas kernels, on_device_tiled(): pl.pallas_call(functools.partial(final_kernel, own), out_shape=f32(hist_l...  21 us
    ppermute x2, waiting for transfers between devices, shifted(): return lax.ppermute(x, axis, pairs)  8.03 us
    all_to_all x1, waiting for transfers between devices, on_device_tiled(): lax.all_to_all(back, both_axes, 0, 0, tiled=True).reshape(2 * count, TILE)  7.79 us
    all_to_all x1, waiting for transfers between devices, on_device_tiled(): lax.all_to_all(send.reshape(devices, own, TILE), both_axes, 0, 0, tiled=T...  7.49 us
    pallas_call x7, Pallas kernels, call(): pl.pallas_call(kernel, out_shape=shapes, in_specs=[VMEM] * len(operands),...  7.07 us
    all_to_all x1, starting transfers between devices, on_device_tiled(): lax.all_to_all(send.reshape(devices, own, TILE), both_axes, 0, 0, tiled=T...  6.78 us
  transfers between devices with their start and end apart: 13, of which 7 were waited for; matrix products, arithmetic and copies ran while one was open for 3% of the time, Pallas kernels for 3%

profile of v1, /device:TPU:1, one launch (start us, length us, event | category | flops | bytes accessed | tf_op | source)
XLA Modules:
  0.0 138.4 jit_solution(11460326747121497653)
XLA Ops:
  0.0 1.4 %fusion.1 = (f32[2,32,16,128]{3,2,1,0:T(8,128)S(1)}, f32[2,32,16,128]{3,2,1,0:T(8,128)S(1)}) fusion(f32[2,32,16,512]{3,2,1,0:T(8,128)} %retarded_ref.1), kind=kLoop, calls=%fused_computation.17 | loop fusion | bytes 2097152 | tf_op jit(solution)/shard_map/slice | solution.py:330
  1.4 0.5 copy-done.3
  1.9 1.0 fusion
  2.9 0.2 pad_maximum_fusion
  3.1 0.0 copy-start.4
  3.1 0.0 copy-start.10
  3.1 0.0 copy-start.12
  3.1 0.0 copy-start.11
  3.1 0.0 copy-start.7
  3.2 1.0 fusion.3
  4.2 1.4 %collective-permute-start.3 = (f32[6,8,16,128]{3,2,1,0:T(8,128)}, f32[6,8,16,128]{3,2,1,0:T(8,128)}, u32[]{:S(2)}, u32[]{:S(2)}) collective-permute-start(f32[6,8,16,128]{3,2,1,0:T(8,128)} %get-tuple-element.18), channel_id=1, source_target_pairs={{3,0},{7,4},{11,8},{15,12},{19,16},{23,20},{27,24},{31,28}} | collective-permute-start | bytes 1179656 | tf_op jit(solution)/shard_map/ppermute | solution.py:311
  5.6 1.3 collective-permute-start.4
  6.9 0.7 fusion.2
  7.6 0.7 collective-permute-start
  8.3 1.3 collective-permute-start.1
  9.6 0.7 collective-permute-start.2
  10.3 0.1 mul.53
  10.4 0.1 broadcast_multiply_fusion.1
  10.5 0.1 mul.59
  10.5 0.7 fusion.5
  11.2 0.1 broadcast_multiply_fusion
  11.3 0.1 constant_dynamic-slice_fusion.3
  11.4 0.1 copy.12.propagator_ref
  11.6 0.1 mul.57
  11.7 0.1 mul.64
  11.8 0.0 collective-permute-done
  11.8 1.4 %collective-permute-start.5 = (f32[6,8,16,128]{3,2,1,0:T(8,128)}, f32[6,8,16,128]{3,2,1,0:T(8,128)}, u32[]{:S(2)}, u32[]{:S(2)}) collective-permute-start(f32[6,8,16,128]{3,2,1,0:T(8,128)} %get-tuple-element.17), channel_id=1, source_target_pairs={{3,2},{7,6},{11,10},{15,14},{19,18},{23,22},{27,26},{31,30}} | collective-permute-start | bytes 1179656 | tf_op jit(solution)/shard_map/ppermute | solution.py:311
  13.2 6.7 %collective-permute-done.1 = f32[2,8,16,128]{3,2,1,0:T(8,128)S(1)} collective-permute-done((f32[2,8,16,128]{3,2,1,0:T(8,128)S(1)}, f32[2,8,16,128]{3,2,1,0:T(8,128)S(1)}, u32[]{:S(2)}, u32[]{:S(2)}) %collective-permute-start.1) | collective-permute-done | bytes 131104 | tf_op jit(solution)/shard_map/ppermute | solution.py:311
  19.9 0.0 copy-start.1
  20.0 0.0 copy-start.2
  20.0 1.1 shard_map.82
  21.0 6.8 %all-to-all-start = ((f32[32,8,128]{2,1,0:T(8,128)}), f32[32,8,128]{2,1,0:T(8,128)S(1)}, u32[]{:S(2)}, u32[]{:S(2)}) async-start(f32[32,8,128]{2,1,0:T(8,128)} %bitcast.1), calls=%async_computation | async-start | bytes 262144 | tf_op jit(solution)/shard_map/all_to_all | solution.py:377
  27.8 0.1 pad_maximum_fusion.4.strength_ref
  27.9 0.2 copy.13
  28.1 0.2 copy.14
  28.3 0.2 select_maximum_fusion.start_ref
  28.5 7.5 %all-to-all-done = f32[32,8,128]{2,1,0:T(8,128)S(1)} async-done(((f32[32,8,128]{2,1,0:T(8,128)}), f32[32,8,128]{2,1,0:T(8,128)S(1)}, u32[]{:S(2)}, u32[]{:S(2)}) %all-to-all-start) | async-done | bytes 131104 | tf_op jit(solution)/shard_map/all_to_all | solution.py:377
  36.0 1.8 %shard_map.83 = f32[32,16,128]{2,1,0:T(8,128)} custom-call(f32[256,128]{1,0:T(8,128)S(1)} %bitcast.18, bf16[512,256]{1,0:T(8,128)(2,1)S(1)} %copy-done.1, bf16[512,256]{1,0:T(8,128)(2,1)S(1)} %copy-done.2, f32[1,128]{1,0:T(1,128)S(1)} %pad_maximum_fusion.4.strength_ref, f32[1,128]{1,0:T(1,128)S(1)} %concatenate.16.mean_ref), custom_call_target="tpu_custom_call" | custom-call | tf_op jit(solution)/shard_map/pallas_call | solution.py:359
  37.8 2.5 %all-to-all-start.1 = ((f32[32,16,128]{2,1,0:T(8,128)}), f32[32,16,128]{2,1,0:T(8,128)S(1)}, u32[]{:S(2)}, u32[]{:S(2)}) async-start(f32[32,16,128]{2,1,0:T(8,128)} %shard_map.83), calls=%async_computation.1 | async-start | bytes 524288 | tf_op jit(solution)/shard_map/all_to_all | solution.py:387
  40.3 0.0 collective-permute-done.4
  40.3 0.0 collective-permute-done.5
  40.3 1.5 %slice_select_fusion = f32[6,8,16,128]{3,2,1,0:T(8,128)S(1)} fusion(f32[6,32,16,128]{3,2,1,0:T(8,128)} %copy-done.4, f32[6,8,16,128]{3,2,1,0:T(8,128)} %collective-permute-done.5, f32[6,8,16,128]{3,2,1,0:T(8,128)} %collective-permute-done.3, f32[6,8,16,128]{3,2,1,0:T(8,128)} %collective-permute-done.4, pred[]{:T(512)S(6)} %eq.7), kind=kLoop, calls=%fused_computation.4 | loop fusion | flops 294912 | bytes 1966081 | tf_op jit(solution)/shard_map/jit(_where)/select_n | solution.py:314
  41.9 1.0 shard_map.84
  42.9 7.8 %all-to-all-done.1 = f32[32,16,128]{2,1,0:T(8,128)S(1)} async-done(((f32[32,16,128]{2,1,0:T(8,128)}), f32[32,16,128]{2,1,0:T(8,128)S(1)}, u32[]{:S(2)}, u32[]{:S(2)}) %all-to-all-start.1) | async-done | bytes 262176 | tf_op jit(solution)/shard_map/all_to_all | solution.py:387
  50.7 0.5 shard_map.85
  51.2 10.6 %all_to_all.30 = f32[32,8,128]{2,1,0:T(8,128)S(1)} all-to-all(f32[32,8,128]{2,1,0:T(8,128)S(1)} %bitcast.17), channel_id=1, replica_groups=mesh['mom'=8,'tm'=4] {'mom','tm'}, dimensions={0} | all-to-all | bytes 262144 | tf_op jit(solution)/shard_map/all_to_all | solution.py:377
  61.9 1.1 shard_map.86
  63.0 12.1 %all_to_all.31 = f32[32,16,128]{2,1,0:T(8,128)S(1)} all-to-all(f32[32,16,128]{2,1,0:T(8,128)S(1)} %shard_map.86), channel_id=1, replica_groups=mesh['mom'=8,'tm'=4] {'mom','tm'}, dimensions={0} | all-to-all | bytes 524288 | tf_op jit(solution)/shard_map/all_to_all | solution.py:387
  75.0 0.5 shard_map.87
  75.6 10.7 %all_to_all.32 = f32[32,8,128]{2,1,0:T(8,128)S(1)} all-to-all(f32[32,8,128]{2,1,0:T(8,128)S(1)} %bitcast.16), channel_id=1, replica_groups=mesh['mom'=8,'tm'=4] {'mom','tm'}, dimensions={0} | all-to-all | bytes 262144 | tf_op jit(solution)/shard_map/all_to_all | solution.py:377
  86.3 1.1 shard_map.88
  87.4 12.1 %all_to_all.33 = f32[32,16,128]{2,1,0:T(8,128)S(1)} all-to-all(f32[32,16,128]{2,1,0:T(8,128)S(1)} %shard_map.88), channel_id=1, replica_groups=mesh['mom'=8,'tm'=4] {'mom','tm'}, dimensions={0} | all-to-all | bytes 524288 | tf_op jit(solution)/shard_map/all_to_all | solution.py:387
  99.5 0.6 collective-permute-start.7
  100.1 3.5 %collective-permute-start.9 = (f32[2,32,16,128]{3,2,1,0:T(8,128)S(1)}, f32[2,32,16,128]{3,2,1,0:T(8,128)S(1)}, u32[]{:S(2)}, u32[]{:S(2)}) collective-permute-start(f32[2,32,16,128]{3,2,1,0:T(8,128)S(1)} %copy-done.6), channel_id=1, source_target_pairs={{0,1},{1,2},{2,3},{4,5},{5,6},{6,7},{8,9},{9,10},{10,11},{12,13},{... | collective-permute-start | bytes 1572872 | tf_op jit(solution)/shard_map/ppermute | solution.py:25
  103.6 1.9 %collective-permute-start.10 = (f32[2,32,16,128]{3,2,1,0:T(8,128)S(1)}, f32[2,32,16,128]{3,2,1,0:T(8,128)S(1)}, u32[]{:S(2)}, u32[]{:S(2)}) collective-permute-start(f32[2,32,16,128]{3,2,1,0:T(8,128)S(1)} %copy-done.9), channel_id=1, source_target_pairs={{0,1},{1,2},{2,3},{4,5},{5,6},{6,7},{8,9},{9,10},{10,11},{12,13},{... | collective-permute-start | bytes 1572872 | tf_op jit(solution)/shard_map/ppermute | solution.py:25
  105.5 0.6 collective-permute-start.6
  106.1 0.6 collective-permute-done.7
  106.7 1.5 %collective-permute-start.8 = (f32[512,128]{1,0:T(8,128)S(1)}, f32[512,128]{1,0:T(8,128)S(1)}, u32[]{:S(2)}, u32[]{:S(2)}) collective-permute-start(f32[512,128]{1,0:T(8,128)S(1)} %collective-permute-done.7), channel_id=1, source_target_pairs={{0,1},{1,0},{2,3},{3,2},{4,5},{5,4},{6,7},{7,6},{8,9},{9,8},{10,11... | collective-permute-start | bytes 786440 | tf_op jit(solution)/shard_map/ppermute | solution.py:403
  108.2 0.0 collective-permute-done.6
  108.2 1.2 collective-permute-done.8
  109.3 0.1 pad_maximum_fusion.1.arrived_ref
  109.4 2.4 %collective-permute-done.9.rim_retarded_ref = f32[2,32,16,128]{3,2,1,0:T(8,128)S(1)} collective-permute-done((f32[2,32,16,128]{3,2,1,0:T(8,128)S(1)}, f32[2,32,16,128]{3,2,1,0:T(8,128)S(1)}, u32[]{:S(2)}, u32[]{:S(2)}) %collective-permute-start.9) | collective-permute-done | bytes 524320 | tf_op jit(solution)/shard_map/ppermute | solution.py:25
  111.8 5.6 %collective-permute-done.10.rim_lesser_ref = f32[2,32,16,128]{3,2,1,0:T(8,128)S(1)} collective-permute-done((f32[2,32,16,128]{3,2,1,0:T(8,128)S(1)}, f32[2,32,16,128]{3,2,1,0:T(8,128)S(1)}, u32[]{:S(2)}, u32[]{:S(2)}) %collective-permute-start.10) | collective-permute-done | bytes 524320 | tf_op jit(solution)/shard_map/ppermute | solution.py:25
  117.5 21.0 %shard_map.89 = f32[2,32,16,512]{3,2,1,0:T(8,128)} custom-call(s32[1]{0:T(128)} %bitcast.tm_ref, f32[4,512,128]{2,1,0:T(8,128)S(1)} %pad_maximum_fusion.1.arrived_ref, f32[2,32,16,128]{3,2,1,0:T(8,128)S(1)} %select_maximum_fusion.start_ref, f32[2,32,16,512]{3,2,1,0:T(8,128)S(1)} %copy-done, f32[2,32,16,512]{3,2,1,0:T(8,128)} %lesser_ref.1, ...), custom_call_target="tpu_custom_call" | custom-call | tf_op jit(solution)/shard_map/pallas_call | solution.py:415
  (30 shorter events, 0.2 us)
Async XLA Ops:
  0.0 1.9 %copy-start.3 = (f32[2,32,16,512]{3,2,1,0:T(8,128)S(1)}, f32[2,32,16,512]{3,2,1,0:T(8,128)}, u32[]{:S(2)}) copy-start(f32[2,32,16,512]{3,2,1,0:T(8,128)} %lesser_ref.1) | copy-start | bytes 6291460
  1.9 1.2 copy-start.5
  3.1 4.5 %copy-start.4 = (f32[6,32,16,128]{3,2,1,0:T(8,128)}, f32[6,32,16,128]{3,2,1,0:T(8,128)S(1)}, u32[]{:S(2)}) copy-start(f32[6,32,16,128]{3,2,1,0:T(8,128)S(1)} %pad_maximum_fusion) | copy-start | bytes 4718596
  3.1 7.2 %copy-start.10 = (f32[256]{0:T(256)S(1)}, f32[256]{0:T(256)}, u32[]{:S(2)}) copy-start(f32[256]{0:T(256)} %param.11) | copy-start | bytes 3076
  3.1 7.2 %copy-start.12 = (f32[8]{0:T(128)S(1)}, f32[8]{0:T(128)}, u32[]{:S(2)}) copy-start(f32[8]{0:T(128)} %param.13) | copy-start | bytes 100
  3.1 7.3 %copy-start.11 = (f32[256]{0:T(256)S(1)}, f32[256]{0:T(256)}, u32[]{:S(2)}) copy-start(f32[256]{0:T(256)} %param.12) | copy-start | bytes 3076
  3.1 7.4 %copy-start.7 = (f32[2,32,16,16]{1,3,2,0:T(8,128)S(1)}, f32[2,32,16,16]{1,3,2,0:T(8,128)}, u32[]{:S(2)}) copy-start(f32[2,32,16,16]{1,3,2,0:T(8,128)} %param.10) | copy-start | bytes 196612
  4.2 36.1 %collective-permute-start.3 = (f32[6,8,16,128]{3,2,1,0:T(8,128)}, f32[6,8,16,128]{3,2,1,0:T(8,128)}, u32[]{:S(2)}, u32[]{:S(2)}) collective-permute-start(f32[6,8,16,128]{3,2,1,0:T(8,128)} %get-tuple-element.18), channel_id=1, source_target_pairs={{3,0},{7,4},{11,8},{15,12},{19,16},{23,20},{27,24},{31,28}} | collective-permute-start | bytes 1179656 | tf_op jit(solution)/shard_map/ppermute | solution.py:311
  5.6 34.7 %collective-permute-start.4 = (f32[6,8,16,128]{3,2,1,0:T(8,128)}, f32[6,8,16,128]{3,2,1,0:T(8,128)}, u32[]{:S(2)}, u32[]{:S(2)}) collective-permute-start(f32[6,8,16,128]{3,2,1,0:T(8,128)} %get-tuple-element.16), channel_id=1, source_target_pairs={{3,1},{7,5},{11,9},{15,13},{19,17},{23,21},{27,25},{31,29}} | collective-permute-start | bytes 1179656 | tf_op jit(solution)/shard_map/ppermute | solution.py:311
  7.6 4.1 %collective-permute-start = (f32[2,8,16,128]{3,2,1,0:T(8,128)}, f32[2,8,16,128]{3,2,1,0:T(8,128)S(1)}, u32[]{:S(2)}, u32[]{:S(2)}) collective-permute-start(f32[2,8,16,128]{3,2,1,0:T(8,128)} %get-tuple-element.15), channel_id=1, source_target_pairs={{3,0},{7,4},{11,8},{15,12},{19,16},{23,20},{27,24},{31,28}} | collective-permute-start | bytes 393224 | tf_op jit(solution)/shard_map/ppermute | solution.py:311
  8.3 11.6 %collective-permute-start.1 = (f32[2,8,16,128]{3,2,1,0:T(8,128)S(1)}, f32[2,8,16,128]{3,2,1,0:T(8,128)S(1)}, u32[]{:S(2)}, u32[]{:S(2)}) collective-permute-start(f32[2,8,16,128]{3,2,1,0:T(8,128)S(1)} %get-tuple-element.13), channel_id=1, source_target_pairs={{3,1},{7,5},{11,9},{15,13},{19,17},{23,21},{27,25},{31,29}} | collective-permute-start | bytes 393224 | tf_op jit(solution)/shard_map/ppermute | solution.py:311
  9.6 10.3 %collective-permute-start.2 = (f32[2,8,16,128]{3,2,1,0:T(8,128)S(1)}, f32[2,8,16,128]{3,2,1,0:T(8,128)S(1)}, u32[]{:S(2)}, u32[]{:S(2)}) collective-permute-start(f32[2,8,16,128]{3,2,1,0:T(8,128)S(1)} %get-tuple-element.14), channel_id=1, source_target_pairs={{3,2},{7,6},{11,10},{15,14},{19,18},{23,22},{27,26},{31,30}} | collective-permute-start | bytes 393224 | tf_op jit(solution)/shard_map/ppermute | solution.py:311
  11.6 16.3 %copy-start.8 = (f32[1,32,16,16]{1,3,2,0:T(8,128)S(1)}, f32[1,32,16,16]{1,3,2,0:T(8,128)}, u32[]{:S(2)}) copy-start(f32[1,32,16,16]{1,3,2,0:T(8,128)} %get-tuple-element.22) | copy-start | bytes 98308
  11.8 28.5 %collective-permute-start.5 = (f32[6,8,16,128]{3,2,1,0:T(8,128)}, f32[6,8,16,128]{3,2,1,0:T(8,128)}, u32[]{:S(2)}, u32[]{:S(2)}) collective-permute-start(f32[6,8,16,128]{3,2,1,0:T(8,128)} %get-tuple-element.17), channel_id=1, source_target_pairs={{3,2},{7,6},{11,10},{15,14},{19,18},{23,22},{27,26},{31,30}} | collective-permute-start | bytes 1179656 | tf_op jit(solution)/shard_map/ppermute | solution.py:311
  19.9 16.1 %copy-start.1 = (bf16[512,256]{1,0:T(8,128)(2,1)S(1)}, bf16[512,256]{1,0:T(8,128)(2,1)}, u32[]{:S(2)}) copy-start(bf16[512,256]{1,0:T(8,128)(2,1)} %constant.29.clone.high_ref) | copy-start | bytes 786436
  20.0 16.1 %copy-start.2 = (bf16[512,256]{1,0:T(8,128)(2,1)S(1)}, bf16[512,256]{1,0:T(8,128)(2,1)}, u32[]{:S(2)}) copy-start(bf16[512,256]{1,0:T(8,128)(2,1)} %constant.30.clone.low_ref) | copy-start | bytes 786436
  21.0 15.0 %all-to-all-start = ((f32[32,8,128]{2,1,0:T(8,128)}), f32[32,8,128]{2,1,0:T(8,128)S(1)}, u32[]{:S(2)}, u32[]{:S(2)}) async-start(f32[32,8,128]{2,1,0:T(8,128)} %bitcast.1), calls=%async_computation | async-start | bytes 262144 | tf_op jit(solution)/shard_map/all_to_all | solution.py:377
  37.8 12.9 %all-to-all-start.1 = ((f32[32,16,128]{2,1,0:T(8,128)}), f32[32,16,128]{2,1,0:T(8,128)S(1)}, u32[]{:S(2)}, u32[]{:S(2)}) async-start(f32[32,16,128]{2,1,0:T(8,128)} %shard_map.83), calls=%async_computation.1 | async-start | bytes 524288 | tf_op jit(solution)/shard_map/all_to_all | solution.py:387
  75.0 25.1 %copy-start.6 = (f32[2,32,16,128]{3,2,1,0:T(8,128)S(1)}, f32[2,32,16,128]{3,2,1,0:T(8,128)}, u32[]{:S(2)}) copy-start(f32[2,32,16,128]{3,2,1,0:T(8,128)} %copy-done.5) | copy-start | bytes 1572868
  75.0 28.6 %copy-start.9 = (f32[2,32,16,128]{3,2,1,0:T(8,128)S(1)}, f32[2,32,16,128]{3,2,1,0:T(8,128)}, u32[]{:S(2)}) copy-start(f32[2,32,16,128]{3,2,1,0:T(8,128)} %get-tuple-element.9) | copy-start | bytes 1572868
  86.3 31.1 %copy-start = (f32[2,32,16,512]{3,2,1,0:T(8,128)S(1)}, f32[2,32,16,512]{3,2,1,0:T(8,128)}, u32[]{:S(2)}) copy-start(f32[2,32,16,512]{3,2,1,0:T(8,128)} %retarded_ref.1) | copy-start | bytes 6291460
  99.5 7.3 %collective-permute-start.7 = (f32[512,128]{1,0:T(8,128)S(1)}, f32[512,128]{1,0:T(8,128)S(1)}, u32[]{:S(2)}, u32[]{:S(2)}) collective-permute-start(f32[512,128]{1,0:T(8,128)S(1)} %bitcast.21), channel_id=1, source_target_pairs={{0,2},{1,3},{2,0},{3,1},{4,6},{5,7},{6,4},{7,5},{8,10},{9,11},{10,... | collective-permute-start | bytes 786440 | tf_op jit(solution)/shard_map/ppermute | solution.py:403
  100.1 11.7 %collective-permute-start.9 = (f32[2,32,16,128]{3,2,1,0:T(8,128)S(1)}, f32[2,32,16,128]{3,2,1,0:T(8,128)S(1)}, u32[]{:S(2)}, u32[]{:S(2)}) collective-permute-start(f32[2,32,16,128]{3,2,1,0:T(8,128)S(1)} %copy-done.6), channel_id=1, source_target_pairs={{0,1},{1,2},{2,3},{4,5},{5,6},{6,7},{8,9},{9,10},{10,11},{12,13},{... | collective-permute-start | bytes 1572872 | tf_op jit(solution)/shard_map/ppermute | solution.py:25
  103.6 13.8 %collective-permute-start.10 = (f32[2,32,16,128]{3,2,1,0:T(8,128)S(1)}, f32[2,32,16,128]{3,2,1,0:T(8,128)S(1)}, u32[]{:S(2)}, u32[]{:S(2)}) collective-permute-start(f32[2,32,16,128]{3,2,1,0:T(8,128)S(1)} %copy-done.9), channel_id=1, source_target_pairs={{0,1},{1,2},{2,3},{4,5},{5,6},{6,7},{8,9},{9,10},{10,11},{12,13},{... | collective-permute-start | bytes 1572872 | tf_op jit(solution)/shard_map/ppermute | solution.py:25
  105.5 2.7 %collective-permute-start.6 = (f32[512,128]{1,0:T(8,128)S(1)}, f32[512,128]{1,0:T(8,128)S(1)}, u32[]{:S(2)}, u32[]{:S(2)}) collective-permute-start(f32[512,128]{1,0:T(8,128)S(1)} %bitcast.22), channel_id=1, source_target_pairs={{0,1},{1,0},{2,3},{3,2},{4,5},{5,4},{6,7},{7,6},{8,9},{9,8},{10,11... | collective-permute-start | bytes 786440 | tf_op jit(solution)/shard_map/ppermute | solution.py:403
  106.7 2.6 %collective-permute-start.8 = (f32[512,128]{1,0:T(8,128)S(1)}, f32[512,128]{1,0:T(8,128)S(1)}, u32[]{:S(2)}, u32[]{:S(2)}) collective-permute-start(f32[512,128]{1,0:T(8,128)S(1)} %collective-permute-done.7), channel_id=1, source_target_pairs={{0,1},{1,0},{2,3},{3,2},{4,5},{5,4},{6,7},{7,6},{8,9},{9,8},{10,11... | collective-permute-start | bytes 786440 | tf_op jit(solution)/shard_map/ppermute | solution.py:403

commit v2 on v0

--- a/solution.py
+++ b/solution.py
@@ -1,8 +1,12 @@
+import functools
 import math
 
 import jax
 import jax.numpy as jnp
+import numpy as np
 from jax import lax
+from jax.experimental import pallas as pl
+from jax.experimental.pallas import tpu as pltpu
 from jax.sharding import PartitionSpec as P
 
 KX = 16
@@ -109,7 +113,7 @@
     )
 
 
-def on_device(hist_lesser, hist_retarded, propagator, coupling, mf_weight, lag_weight):
+def on_device_any(hist_lesser, hist_retarded, propagator, coupling, mf_weight, lag_weight):
     momenta_here = hist_lesser.shape[1]
     times_here = hist_lesser.shape[3] // ORB
     cosine, sine = momentum_tables()
@@ -161,6 +165,472 @@
     return full_slice
 
 
+VMEM = pl.BlockSpec(memory_space=pltpu.VMEM)
+SMEM = pl.BlockSpec(memory_space=pltpu.SMEM)
+IN_HBM = pl.BlockSpec(memory_space=pltpu.HBM)
+HALF = W * ORB // 2
+TILE = W * ORB
+
+
+def limit(mebibytes):
+    return pltpu.CompilerParams(vmem_limit_bytes=mebibytes * 1024 * 1024)
+
+
+def halves(x):
+    high = x.astype(jnp.bfloat16)
+    return high, (x - high.astype(jnp.float32)).astype(jnp.bfloat16)
+
+
+def matmul(first, second):
+    return jnp.dot(first, second, preferred_element_type=jnp.float32)
+
+
+def fourier_tables():
+    index = np.arange(KX * KY)
+    turn = np.outer(index // KY, index // KY) / KX + np.outer(index % KY, index % KY) / KY
+    phase = 2.0 * np.pi * (turn % 1.0)
+    table = np.concatenate([np.cos(phase), np.sin(phase)]) / math.sqrt(KX * KY)
+    high = table.astype(jnp.bfloat16)
+    low = (table - high.astype(np.float64)).astype(jnp.bfloat16)
+    return jnp.asarray(high), jnp.asarray(low)
+
+
+def lower_lanes(shape):
+    return lax.broadcasted_iota(jnp.int32, shape, 1) < HALF
+
+
+def store_window(send_ref, k, own, real, imag):
+    lower = lower_lanes(real.shape)
+    turned_real = pltpu.roll(real, HALF, 1)
+    turned_imag = pltpu.roll(imag, HALF, 1)
+    send_ref[pl.ds(k, ORB, stride=2 * own), :] = jnp.where(lower, real, turned_imag)
+    send_ref[pl.ds(own + k, ORB, stride=2 * own), :] = jnp.where(lower, turned_real, imag)
+
+
+def start_all(copies):
+    for copy in copies:
+        copy.start()
+    return copies
+
+
+def wait_all(copies):
+    for copy in copies:
+        copy.wait()
+
+
+def first_window_kernel(
+    own, propagator_ref, retarded_ref, lesser_ref, low_ref, high_ref, near0_ref, near1_ref, window_ref, arrive, pass_on
+):
+    momenta, columns = lesser_ref.shape[1], lesser_ref.shape[3]
+    half = momenta // 2
+    fetches = start_all(
+        [
+            pltpu.make_async_copy(
+                lesser_ref.at[:, first : first + own, :, columns - TILE :],
+                window_ref.at[:, first : first + own],
+                arrive.at[number],
+            )
+            for number, first in enumerate(range(0, momenta, own))
+        ]
+    )
+    copies = start_all(
+        [
+            pltpu.make_async_copy(
+                ref.at[:, tm * own : (tm + 1) * own, :, columns - 2 * TILE :],
+                near_ref.at[2 * kind : 2 * kind + 2],
+                pass_on.at[tm, kind],
+            )
+            for tm, near_ref in enumerate((near0_ref, near1_ref))
+            for kind, ref in enumerate((retarded_ref, lesser_ref))
+        ]
+    )
+    for number, fetch in enumerate(fetches):
+        fetch.wait()
+        for k in range(number * own, (number + 1) * own):
+            left = jnp.concatenate([propagator_ref[0, k], propagator_ref[1, k]], axis=0)
+            right = jnp.concatenate([window_ref[0, k], window_ref[1, k]], axis=1)
+            imag, real = contract(*halves(left), *halves(right), TILE)
+            store_window(low_ref if k < half else high_ref, k % half, half, -real, imag)
+    wait_all(copies)
+
+
+def fourier_kernel(arrived_ref, high_ref, low_ref, strength_ref, mean_ref, out_ref):
+    count = KX * KY
+    useful = count // (arrived_ref.shape[0] * arrived_ref.shape[2])
+    x_high, x_low = halves(arrived_ref[:, arrived_ref.shape[1] - useful :].reshape(count, TILE))
+    main = matmul(high_ref[...], jnp.concatenate([x_high, x_low], axis=1))
+    turned = main[:, :TILE] + main[:, TILE:] + matmul(low_ref[...], x_high)
+    lower = lower_lanes((count, TILE))
+    sine_part = pltpu.roll(turned[count:], HALF, 1)
+    here = turned[:count] + jnp.where(lower, -sine_part, sine_part)
+    swapped = pltpu.roll(here, HALF, 1)
+    real = jnp.where(lower, here, swapped)
+    imag = jnp.where(lower, swapped, here)
+    real_square = real * real
+    imag_square = imag * imag
+    size = real_square + imag_square
+    strength = strength_ref[...]
+    out_real = strength * jnp.where(lower, size * real, real_square - imag_square)
+    out_imag = strength * jnp.where(lower, size * imag, 2.0 * real * imag)
+    origin = (lax.broadcasted_iota(jnp.int32, (count, TILE), 0) == 0).astype(jnp.float32)
+    mean = origin * mean_ref[...]
+    out_real = out_real + mean * real
+    out_imag = out_imag + mean * imag
+    real_high, real_low = halves(out_real)
+    imag_high, imag_low = halves(out_imag)
+    y_high = jnp.concatenate([real_high, imag_high], axis=1)
+    y_low = jnp.concatenate([real_low, imag_low], axis=1)
+    back = matmul(high_ref[...], y_high) + matmul(low_ref[...], y_high) + matmul(high_ref[...], y_low)
+    devices, rows, _ = out_ref.shape
+    own = rows // 2
+    out_ref[:, :own] = (back[:count, :TILE] + back[count:, TILE:]).reshape(devices, own, TILE)
+    out_ref[:, own:] = (back[:count, TILE:] - back[count:, :TILE]).reshape(devices, own, TILE)
+
+
+def coefficients(arrived_ref, propagator_ref, k, own):
+    pieces = []
+    for part, start in enumerate((-propagator_ref[1], propagator_ref[0])):
+        first, second = (
+            arrived_ref[pl.ds((2 * half + part) * own + k, ORB, stride=4 * own), :] for half in range(2)
+        )
+        start = jnp.concatenate([jnp.zeros((ORB, TILE - ORB), jnp.float32), start], axis=1)
+        pieces.append((first, second + start))
+    return pieces
+
+
+def ladder(regions, width):
+    rows = []
+    for half in range(2):
+        for kind in range(2):
+            for lag in range(W // 2):
+                offset = ORB * (1 + half * (W // 2) + lag)
+                rows.append(jnp.concatenate([x[:, offset : offset + width] for x in regions[kind]], axis=1))
+    return jnp.concatenate(rows, axis=0)
+
+
+def contract(left_high, left_low, right_high, right_low, width):
+    rows = left_high.shape[0]
+    main = matmul(jnp.concatenate([left_high, left_low], axis=0), right_high)
+    both = main[:rows] + main[rows:] + matmul(left_high, right_low)
+    half = rows // 2
+    real = both[:half, :width] - both[half:, width:]
+    imag = both[:half, width:] + both[half:, :width]
+    return imag, -real
+
+
+def window_ladder_kernel(own, near_ref, high_ref, low_ref):
+    for k in range(own):
+        regions = [[near_ref[2 * kind + part, k] for part in range(2)] for kind in range(2)]
+        high_ref[k], low_ref[k] = halves(ladder(regions, TILE))
+
+
+def window_kernel(own, arrived_ref, propagator_ref, high_ref, low_ref, send_ref):
+    for k in range(own):
+        pieces = coefficients(arrived_ref, propagator_ref.at[:, k], k, own)
+        left_high, left_low = halves(jnp.concatenate([jnp.concatenate(pair, axis=1) for pair in pieces], axis=0))
+        real, imag = contract(left_high, left_low, high_ref[k], low_ref[k], TILE)
+        store_window(send_ref, k, own, real, imag)
+
+
+def trade(tiles):
+    group = lax.broadcasted_iota(jnp.int32, tiles[0].shape, 1) // ORB
+    for bit in (2, 1):
+        first = (group & bit) == 0
+        shift = bit * ORB
+        traded = list(tiles)
+        for i in range(4):
+            if not i & bit:
+                x, y = tiles[i], tiles[i | bit]
+                traded[i] = jnp.where(first, x, pltpu.roll(y, shift, 1))
+                traded[i | bit] = jnp.where(first, pltpu.roll(x, TILE - shift, 1), y)
+        tiles = traded
+    return tiles
+
+
+def final_ladder_kernel(tm_ref, retarded_ref, lesser_ref, rim_ref, high_out, low_out, region_ref, high_ref, low_ref, arrive, leave):
+    own = high_ref.shape[0]
+    momenta = pl.ds(tm_ref[0] * own, own)
+    fetches = []
+    for kind, ref in enumerate((retarded_ref, lesser_ref)):
+        both = pl.ds(2 * kind, 2)
+        fetches += start_all(
+            [
+                pltpu.make_async_copy(
+                    ref.at[:, momenta], region_ref.at[both, :, :, pl.ds(TILE, ref.shape[3])], arrive.at[kind, 0]
+                ),
+                pltpu.make_async_copy(
+                    rim_ref.at[both, momenta], region_ref.at[both, :, :, pl.ds(0, TILE)], arrive.at[kind, 1]
+                ),
+            ]
+        )
+    wait_all(fetches)
+
+    def leaving(k):
+        return [
+            pltpu.make_async_copy(ref.at[k], out.at[k], leave.at[k, which])
+            for which, (ref, out) in enumerate(((high_ref, high_out), (low_ref, low_out)))
+        ]
+
+    def one(k, carry):
+        for part in range(2):
+            region = jnp.concatenate([region_ref[2 * kind + part, k] for kind in range(2)], axis=0)
+            lanes = pl.ds(part * TILE, TILE)
+            for turn in range(3):
+                from_lane = turn * 4 * ORB
+                tiles = trade([region[:, from_lane + t * TILE : from_lane + (t + 1) * TILE] for t in range(4)])
+                for step in range(4 * turn - 1, 4 * turn + 3):
+                    if step >= 0:
+                        high, low = halves(tiles[step - 4 * turn + 1])
+                        for kind in range(2):
+                            rows = pl.ds(step // 4 * TILE + kind * HALF + step % 4 * ORB, ORB)
+                            high_ref[k, rows, lanes] = high[kind * ORB : (kind + 1) * ORB]
+                            low_ref[k, rows, lanes] = low[kind * ORB : (kind + 1) * ORB]
+            for kind in range(2):
+                rows = pl.ds(2 * TILE + kind * HALF + 3 * ORB, ORB)
+                high_ref[k, rows, lanes] = jnp.zeros((ORB, TILE), jnp.bfloat16)
+                low_ref[k, rows, lanes] = jnp.zeros((ORB, TILE), jnp.bfloat16)
+        start_all(leaving(k))
+        return carry
+
+    lax.fori_loop(0, own, one, 0)
+    lax.fori_loop(0, own, lambda k, c: (wait_all(leaving(k)), c)[1], 0)
+
+
+def stepped(pair):
+    first, second = pair
+    place = lax.broadcasted_iota(jnp.int32, first.shape, 1) // ORB % 4
+    rows = [jnp.concatenate([first, second, jnp.zeros_like(first)], axis=1)]
+    for s in range(1, 4):
+        stay = place >= s
+        up, over = s * ORB, TILE + (s - 4) * ORB
+        rows.append(
+            jnp.concatenate(
+                [
+                    jnp.where(stay, pltpu.roll(first, up, 1), 0.0),
+                    jnp.where(stay, pltpu.roll(second, up, 1), pltpu.roll(first, over, 1)),
+                    jnp.where(stay, 0.0, pltpu.roll(second, over, 1)),
+                ],
+                axis=1,
+            )
+        )
+    return jnp.concatenate(rows, axis=0)
+
+
+def final_kernel(own, before, tm_ref, arrived_ref, propagator_ref, high_ref, low_ref, *others):
+    out_ref, high_here, low_here, out_here, arrive, leave = others[before:]
+    base = tm_ref[0] * own
+
+    group = own // 2
+
+    def arriving(number):
+        momenta = pl.ds(number * group, group)
+        return [
+            pltpu.make_async_copy(ref.at[momenta], here.at[momenta], arrive.at[number, which])
+            for which, (ref, here) in enumerate(((high_ref, high_here), (low_ref, low_here)))
+        ]
+
+    def leaving(number):
+        return [
+            pltpu.make_async_copy(
+                out_here.at[:, pl.ds(number * group, group)],
+                out_ref.at[:, pl.ds(base + number * group, group)],
+                leave.at[number],
+            )
+        ]
+
+    def one(number, carry):
+        wait_all(arriving(number))
+        for n in range(group):
+            k = number * group + n
+            pieces = coefficients(arrived_ref, propagator_ref.at[:, base + k], k, own)
+            left_high, left_low = halves(jnp.concatenate([stepped(pair) for pair in pieces], axis=0))
+            parts = contract(left_high, left_low, high_here[k], low_here[k], TILE)
+            for part, value in enumerate(parts):
+                tiles = trade([value[s * ORB : (s + 1) * ORB] for s in range(4)])
+                for t, tile in enumerate(tiles):
+                    out_here[part, k, :, t * TILE : (t + 1) * TILE] = tile
+        start_all(leaving(number))
+        return carry
+
+    for number in range(own // group):
+        start_all(arriving(number))
+    lax.fori_loop(0, own // group, one, 0)
+    for number in range(own // group):
+        wait_all(leaving(number))
+
+
+def own_block(x, own, axis):
+    return lax.dynamic_slice_in_dim(x, lax.axis_index("tm") * own, own, axis)
+
+
+def on_device_tiled(hist_lesser, hist_retarded, propagator, coupling, mf_weight, lag_weight):
+    both_axes = ("mom", "tm")
+    momenta_here = hist_lesser.shape[1]
+    columns = hist_lesser.shape[3]
+    peers = lax.axis_size("tm")
+    devices = lax.axis_size("mom") * peers
+    own = momenta_here // peers
+    count = KX * KY
+
+    f32 = functools.partial(jax.ShapeDtypeStruct, dtype=jnp.float32)
+    bf16 = functools.partial(jax.ShapeDtypeStruct, dtype=jnp.bfloat16)
+
+    def call(kernel, shapes, *operands):
+        return pl.pallas_call(
+            kernel,
+            out_shape=shapes,
+            in_specs=[VMEM] * len(operands),
+            out_specs=jax.tree.map(lambda _: VMEM, shapes),
+            compiler_params=limit(12),
+        )(*operands)
+
+    half = momenta_here // 2
+    sent = f32((devices * half, TILE))
+    near_shape = f32((4, own, ORB, 2 * TILE))
+    low, high, *near = pl.pallas_call(
+        functools.partial(first_window_kernel, own),
+        out_shape=(sent, sent, near_shape, near_shape),
+        in_specs=[VMEM, IN_HBM, IN_HBM],
+        out_specs=(VMEM,) * 4,
+        scratch_shapes=[
+            pltpu.VMEM((2, momenta_here, ORB, TILE), jnp.float32),
+            pltpu.SemaphoreType.DMA((momenta_here // own,)),
+            pltpu.SemaphoreType.DMA((2, 2)),
+        ],
+        compiler_params=limit(8),
+    )(propagator, *(pltpu.with_memory_space_constraint(x, pltpu.HBM) for x in (hist_retarded, hist_lesser)))
+    here = lax.axis_index("tm")
+    last = here == peers - 1
+    low = lax.ppermute(low, "tm", [(3, 2)])
+    near = [lax.ppermute(block, "tm", [(3, tm)]) for tm, block in enumerate(near)]
+    send = jnp.where(last, high, low).reshape(devices, half, TILE)
+    send, hist_lesser, hist_retarded, coupling, mf_weight, lag_weight = lax.optimization_barrier(
+        (send, hist_lesser, hist_retarded, coupling, mf_weight, lag_weight)
+    )
+
+    def near_of(tm):
+        momenta = slice(tm * own, (tm + 1) * own)
+        return jnp.concatenate([x[:, momenta, :, columns - 2 * TILE :] for x in (hist_retarded, hist_lesser)], axis=0)
+
+    near.append(lax.ppermute(near_of(2), "tm", [(3, 2)]))
+    rim = jnp.concatenate([x[..., columns - TILE :] for x in (hist_retarded, hist_lesser)], axis=0)
+    rim = shifted(rim, "tm", 1)
+
+    me = lax.axis_index("mom") * peers + lax.axis_index("tm")
+    last_mark = (jnp.arange(W) == W - 1).astype(jnp.float32)
+    strong = (coupling * coupling).reshape(ORB, 1, ORB) * lag_weight[:, None]
+    mean = mf_weight.reshape(ORB, 1, ORB) * (lag_weight * last_mark)[:, None]
+    strong = lax.dynamic_slice_in_dim(strong.reshape(devices, HALF), me, 1, 0)
+    mean = lax.dynamic_slice_in_dim(mean.reshape(devices, HALF), me, 1, 0)
+    strength = jnp.concatenate([strong, strong], axis=1)
+    mean = jnp.concatenate([mean, jnp.zeros_like(mean)], axis=1)
+    table_high, table_low = fourier_tables()
+
+    ladders = []
+    ladder_shape = (own, 3 * TILE, 2 * TILE)
+
+    def beside(arrived, sent):
+        _, retarded, lesser, edge = lax.optimization_barrier((sent, hist_retarded, hist_lesser, rim))
+        momenta = (here ^ len(ladders)).reshape(1).astype(jnp.int32)
+        ladder = pl.pallas_call(
+            final_ladder_kernel,
+            out_shape=(pltpu.HBM(ladder_shape, jnp.bfloat16),) * 2,
+            in_specs=[SMEM, IN_HBM, IN_HBM, IN_HBM],
+            out_specs=(IN_HBM, IN_HBM),
+            scratch_shapes=[
+                pltpu.VMEM((4, own, ORB, TILE + columns), jnp.float32),
+                pltpu.VMEM(ladder_shape, jnp.bfloat16),
+                pltpu.VMEM(ladder_shape, jnp.bfloat16),
+                pltpu.SemaphoreType.DMA((2, 2)),
+                pltpu.SemaphoreType.DMA((own, 2)),
+            ],
+            compiler_params=limit(6),
+        )(momenta, *(pltpu.with_memory_space_constraint(x, pltpu.HBM) for x in (retarded, lesser, edge)))
+        arrived, *ladder = lax.optimization_barrier((arrived, *ladder))
+        ladders.append(ladder)
+        return arrived
+
+    for sweep in range(PASSES):
+        arrived = lax.all_to_all(send, both_axes, 0, 0, tiled=True)
+        if sweep == 0:
+            arrived, *near[:2] = lax.optimization_barrier((arrived, *near[:2]))
+        else:
+            arrived = beside(arrived, send)
+        back = call(
+            fourier_kernel,
+            f32((devices, 2 * own, TILE)),
+            arrived.reshape(devices // peers, peers, -1, TILE),
+            table_high,
+            table_low,
+            strength,
+            mean,
+        )
+        if sweep == 0:
+            near[2], _ = lax.optimization_barrier((near[2], back))
+            mine = near_of(peers - 1)
+            for tm, received in enumerate(near):
+                mine = jnp.where(here == tm, received, mine)
+            rungs = bf16((own, 2 * TILE, 2 * TILE))
+            rungs = call(functools.partial(window_ladder_kernel, own), (rungs, rungs), mine)
+            rim, *rungs = lax.optimization_barrier((rim, *rungs))
+            propagator_own = own_block(propagator, own, 1)
+        arrived = lax.all_to_all(back, both_axes, 0, 0, tiled=True)
+        if sweep:
+            arrived = beside(arrived, back)
+        arrived = arrived.reshape(2 * count, TILE)
+        if sweep + 1 < PASSES:
+            send = call(
+                functools.partial(window_kernel, own),
+                f32((count, TILE)),
+                arrived,
+                propagator_own,
+                *rungs,
+            ).reshape(devices, own, TILE)
+
+    def finish(new_slice, coefficients_of, step):
+        before = () if new_slice is None else (new_slice,)
+        return pl.pallas_call(
+            functools.partial(final_kernel, own, len(before)),
+            out_shape=pltpu.HBM(hist_lesser.shape, jnp.float32),
+            in_specs=[SMEM, VMEM, VMEM] + [IN_HBM] * (2 + len(before)),
+            out_specs=IN_HBM,
+            scratch_shapes=[
+                pltpu.VMEM(ladder_shape, jnp.bfloat16),
+                pltpu.VMEM(ladder_shape, jnp.bfloat16),
+                pltpu.VMEM((2, own, ORB, columns), jnp.float32),
+                pltpu.SemaphoreType.DMA((own, 2)),
+                pltpu.SemaphoreType.DMA((own,)),
+            ],
+            input_output_aliases={5: 0} if before else {},
+            compiler_params=limit(6),
+        )(
+            (here ^ step).reshape(1).astype(jnp.int32),
+            coefficients_of,
+            propagator,
+            *[pltpu.with_memory_space_constraint(x, pltpu.HBM) for x in ladders[step]],
+            *before,
+        )
+
+    def exchange(x, step):
+        return lax.ppermute(x, "tm", [(t, t ^ step) for t in range(peers)])
+
+    across = exchange(arrived, 2)
+    beside_me = exchange(arrived, 1)
+    new_slice = finish(None, arrived, 0)
+    new_slice = finish(new_slice, beside_me, 1)
+    across, new_slice = lax.optimization_barrier((across, new_slice))
+    beyond = exchange(across, 1)
+    new_slice = finish(new_slice, across, 2)
+    return finish(new_slice, beyond, 3)
+
+
+def on_device(hist_lesser, *others):
+    peers = lax.axis_size("tm")
+    devices = lax.axis_size("mom") * peers
+    fits = devices == 2 * ORB and peers == 4 and hist_lesser.shape[1:] == (2 * ORB, ORB, 4 * TILE)
+    return (on_device_tiled if fits else on_device_any)(hist_lesser, *others)
+
+
 def solution(mesh):
     return jax.shard_map(
         on_device,

time: 902 us -> 120 us (0.13)
  the two profiles are of different devices: /device:TPU:0 before, /device:TPU:1 now
where the time goes in v2:
time: 120 us; the launch traced here: 119 us
  Pallas kernels  48.2 us (40%)
  starting transfers between devices  35.4 us (30%)
  waiting for transfers between devices  24.6 us (20%)
  local copies, waits for them, and re-layouts  6.59 us (5%)
  other arithmetic  4.14 us (3%)
    pallas_call x4, Pallas kernels, beside(): pl.pallas_call(final_ladder_kernel, out_shape=(pltpu.HBM(ladder_shape, jn...  23.2 us
    pallas_call x4, Pallas kernels, finish(): pl.pallas_call(functools.partial(final_kernel, own, len(before)), out_sha...  16 us
    all_to_all x3, waiting for transfers between devices, on_device_tiled(): arrived = lax.all_to_all(back, both_axes, 0, 0, tiled=True)  15.6 us
    all_to_all x3, starting transfers between devices, on_device_tiled(): arrived = lax.all_to_all(send, both_axes, 0, 0, tiled=True)  15.4 us
    all_to_all x3, starting transfers between devices, on_device_tiled(): arrived = lax.all_to_all(back, both_axes, 0, 0, tiled=True)  9.93 us
    all_to_all x3, waiting for transfers between devices, on_device_tiled(): arrived = lax.all_to_all(send, both_axes, 0, 0, tiled=True)  7.76 us
    pallas_call x6, Pallas kernels, call(): pl.pallas_call(kernel, out_shape=shapes, in_specs=[VMEM] * len(operands),...  6.71 us
    unnamed x27, local copies, waits for them, and re-layouts  4.18 us
  transfers between devices with their start and end apart: 14, of which 7 were waited for; matrix products, arithmetic and copies ran while one was open for 5% of the time, Pallas kernels for 32%

profile of v2, /device:TPU:1, one launch (start us, length us, event | category | flops | bytes accessed | tf_op | source)
XLA Modules:
  0.0 119.4 jit_solution(2181722140066078546)
XLA Ops:
  0.0 1.2 %copy.12.propagator_ref = f32[2,32,16,16]{3,2,1,0:T(8,128)S(1)} copy(f32[2,32,16,16]{1,3,2,0:T(8,128)} %param.10) | data formatting | bytes 131072 | tf_op args[2]
  1.2 2.4 %shard_map.82 = (f32[512,128]{1,0:T(8,128)S(1)}, f32[512,128]{1,0:T(8,128)S(1)}, f32[4,8,16,256]{3,2,1,0:T(8,128)S(1)}, f32[4,8,16,256]{3,2,1,0:T(8,128)S(1)}) custom-call(f32[2,32,16,16]{3,2,1,0:T(8,128)S(1)} %copy.12.propagator_ref, f32[2,32,16,512]{3,2,1,0:T(8,128)} %retarded_ref.5, f32[2,32,16,512]{3,2,1,0:T(8,128)} %lesser_ref.5), custom_call_target="tpu_custom_call" | custom-call | tf_op jit(solution)/shard_map/pallas_call | solution.py:490
  3.6 0.7 collective-permute-start
  4.3 1.5 %collective-permute-start.1 = (f32[4,8,16,256]{3,2,1,0:T(8,128)S(1)}, f32[4,8,16,256]{3,2,1,0:T(8,128)}, u32[]{:S(2)}, u32[]{:S(2)}) collective-permute-start(f32[4,8,16,256]{3,2,1,0:T(8,128)S(1)} %get-tuple-element.61), channel_id=1, source_target_pairs={{3,0},{7,4},{11,8},{15,12},{19,16},{23,20},{27,24},{31,28}} | collective-permute-start | bytes 1572872 | tf_op jit(solution)/shard_map/ppermute | solution.py:505
  5.8 1.3 %collective-permute-start.2 = (f32[4,8,16,256]{3,2,1,0:T(8,128)S(1)}, f32[4,8,16,256]{3,2,1,0:T(8,128)}, u32[]{:S(2)}, u32[]{:S(2)}) collective-permute-start(f32[4,8,16,256]{3,2,1,0:T(8,128)S(1)} %get-tuple-element.62), channel_id=1, source_target_pairs={{3,1},{7,5},{11,9},{15,13},{19,17},{23,21},{27,25},{31,29}} | collective-permute-start | bytes 1572872 | tf_op jit(solution)/shard_map/ppermute | solution.py:505
  7.1 0.0 copy-start.5
  7.1 0.0 collective-permute-done
  7.1 0.7 broadcast_select_fusion
  7.8 0.9 copy-done.5
  8.8 2.1 %fusion.2 = (f32[2,8,16,256]{3,2,1,0:T(8,128)}, f32[2,8,16,256]{3,2,1,0:T(8,128)}, f32[2,8,16,256]{3,2,1,0:T(8,128)}, f32[2,8,16,256]{3,2,1,0:T(8,128)}) fusion(f32[2,32,16,512]{3,2,1,0:T(8,128)S(1)} %copy-done.5, f32[2,32,16,512]{3,2,1,0:T(8,128)} %lesser_ref.5), kind=kLoop, calls=%fused_computation.13 | loop fusion | bytes 2097152 | tf_op jit(solution)/shard_map/slice | solution.py:513
  10.8 0.0 copy-start.1
  10.9 0.1 mul.51
  10.9 9.9 %all-to-all-start = ((f32[32,16,128]{2,1,0:T(8,128)}), f32[32,16,128]{2,1,0:T(8,128)S(1)}, u32[]{:S(2)}, u32[]{:S(2)}) async-start(f32[32,16,128]{2,1,0:T(8,128)} %bitcast.23), calls=%async_computation | async-start | bytes 524288 | tf_op jit(solution)/shard_map/all_to_all | solution.py:554
  20.8 0.1 broadcast_multiply_fusion.1
  20.9 1.0 pad_maximum_fusion
  22.0 3.7 %collective-permute-start.3 = (f32[4,32,16,128]{3,2,1,0:T(8,128)}, f32[4,32,16,128]{3,2,1,0:T(8,128)}, u32[]{:S(2)}, u32[]{:S(2)}) collective-permute-start(f32[4,32,16,128]{3,2,1,0:T(8,128)} %pad_maximum_fusion), channel_id=1, source_target_pairs={{0,1},{1,2},{2,3},{4,5},{5,6},{6,7},{8,9},{9,10},{10,11},{12,13},{... | collective-permute-start | bytes 3145736 | tf_op jit(solution)/shard_map/ppermute | solution.py:25
  25.7 0.9 pad_maximum_fusion.1
  26.5 0.1 mul.57
  26.6 1.5 %collective-permute-start.4 = (f32[4,8,16,256]{3,2,1,0:T(8,128)}, f32[4,8,16,256]{3,2,1,0:T(8,128)}, u32[]{:S(2)}, u32[]{:S(2)}) collective-permute-start(f32[4,8,16,256]{3,2,1,0:T(8,128)} %pad_maximum_fusion.1), channel_id=1, source_target_pairs={{3,2},{7,6},{11,10},{15,14},{19,18},{23,22},{27,26},{31,30}} | collective-permute-start | bytes 1572872 | tf_op jit(solution)/shard_map/ppermute | solution.py:515
  28.1 0.1 broadcast_multiply_fusion
  28.1 0.1 mul.62
  28.2 0.1 mul.55
  28.3 0.1 pad_maximum_fusion.2.strength_ref
  28.4 0.0 collective-permute-done.1
  28.4 0.0 collective-permute-done.2
  28.4 2.7 %all-to-all-done = f32[32,16,128]{2,1,0:T(8,128)S(1)} async-done(((f32[32,16,128]{2,1,0:T(8,128)}), f32[32,16,128]{2,1,0:T(8,128)S(1)}, u32[]{:S(2)}, u32[]{:S(2)}) %all-to-all-start) | async-done | bytes 262176 | tf_op jit(solution)/shard_map/all_to_all | solution.py:554
  31.1 1.8 %shard_map.83 = f32[32,16,128]{2,1,0:T(8,128)} custom-call(f32[8,4,16,128]{3,2,1,0:T(8,128)S(1)} %bitcast.13, bf16[512,256]{1,0:T(8,128)(2,1)S(1)} %copy-done.1, bf16[512,256]{1,0:T(8,128)(2,1)S(1)} %copy-done, f32[1,128]{1,0:T(1,128)S(1)} %pad_maximum_fusion.2.strength_ref, f32[1,128]{1,0:T(1,128)S(1)} %concatenate.16.mean_ref), custom_call_target="tpu_custom_call" | custom-call | tf_op jit(solution)/shard_map/pallas_call | solution.py:479
  32.9 3.1 %all-to-all-start.1 = ((f32[32,16,128]{2,1,0:T(8,128)}), f32[32,16,128]{2,1,0:T(8,128)S(1)}, u32[]{:S(2)}, u32[]{:S(2)}) async-start(f32[32,16,128]{2,1,0:T(8,128)} %shard_map.83), calls=%async_computation.1 | async-start | bytes 524288 | tf_op jit(solution)/shard_map/all_to_all | solution.py:577
  36.0 0.0 collective-permute-done.4
  36.0 1.3 %fusion.1.near_ref = f32[4,8,16,256]{3,2,1,0:T(8,128)S(1)} fusion(f32[4,8,16,256]{3,2,1,0:T(8,128)} %collective-permute-done.4, f32[4,8,16,256]{3,2,1,0:T(8,128)} %collective-permute-done.2, f32[4,8,16,256]{3,2,1,0:T(8,128)} %collective-permute-done.1, f32[2,8,16,256]{3,2,1,0:T(8,128)S(1)} %copy-done.9, f32[2,8,16,256]{3,2,1,0:T(8,128)S(1)} %copy-done.8, ...), kind=kLoop, calls=%fused_computation.4 | loop fusion | flops 524288 | bytes 2621443 | tf_op jit(solution)/shard_map/jit(_where)/select_n | solution.py:572
  37.3 1.0 shard_map.84
  38.3 1.2 %collective-permute-done.3.rim_ref = f32[4,32,16,128]{3,2,1,0:T(8,128)} collective-permute-done((f32[4,32,16,128]{3,2,1,0:T(8,128)}, f32[4,32,16,128]{3,2,1,0:T(8,128)}, u32[]{:S(2)}, u32[]{:S(2)}) %collective-permute-start.3) | collective-permute-done | bytes 1048608 | tf_op jit(solution)/shard_map/ppermute | solution.py:25
  39.5 6.7 %all-to-all-done.1 = f32[32,16,128]{2,1,0:T(8,128)S(1)} async-done(((f32[32,16,128]{2,1,0:T(8,128)}), f32[32,16,128]{2,1,0:T(8,128)S(1)}, u32[]{:S(2)}, u32[]{:S(2)}) %all-to-all-start.1) | async-done | bytes 262176 | tf_op jit(solution)/shard_map/all_to_all | solution.py:577
  46.2 0.5 shard_map.85
  46.7 0.0 copy-start.4
  46.7 0.6 copy-done.4
  47.4 2.8 %all-to-all-start.2 = ((f32[32,8,128]{2,1,0:T(8,128)}), f32[32,8,128]{2,1,0:T(8,128)S(1)}, u32[]{:S(2)}, u32[]{:S(2)}) async-start(f32[32,8,128]{2,1,0:T(8,128)} %bitcast.20), calls=%async_computation.2 | async-start | bytes 262144 | tf_op jit(solution)/shard_map/all_to_all | solution.py:554
  50.2 5.8 %shard_map.86 = (bf16[8,384,256]{2,1,0:T(8,128)(2,1)}, bf16[8,384,256]{2,1,0:T(8,128)(2,1)}) custom-call(s32[1]{0:T(128)} %bitcast.5.tm_ref, f32[2,32,16,512]{3,2,1,0:T(8,128)} %retarded_ref.5, f32[2,32,16,512]{3,2,1,0:T(8,128)} %lesser_ref.5, f32[4,32,16,128]{3,2,1,0:T(8,128)} %collective-permute-done.3.rim_ref), custom_call_target="tpu_custom_call" | custom-call | tf_op jit(solution)/shard_map/pallas_call | solution.py:535
  56.0 2.5 %all-to-all-done.2 = f32[32,8,128]{2,1,0:T(8,128)S(1)} async-done(((f32[32,8,128]{2,1,0:T(8,128)}), f32[32,8,128]{2,1,0:T(8,128)S(1)}, u32[]{:S(2)}, u32[]{:S(2)}) %all-to-all-start.2) | async-done | bytes 131104 | tf_op jit(solution)/shard_map/all_to_all | solution.py:554
  58.5 1.1 shard_map.87
  59.6 0.0 copy-start.2
  59.6 0.7 copy-done.2
  60.3 3.4 %all-to-all-start.3 = ((f32[32,16,128]{2,1,0:T(8,128)}), f32[32,16,128]{2,1,0:T(8,128)S(1)}, u32[]{:S(2)}, u32[]{:S(2)}) async-start(f32[32,16,128]{2,1,0:T(8,128)} %copy-done.2), calls=%async_computation.3 | async-start | bytes 524288 | tf_op jit(solution)/shard_map/all_to_all | solution.py:577
  63.7 5.8 %shard_map.88 = (bf16[8,384,256]{2,1,0:T(8,128)(2,1)}, bf16[8,384,256]{2,1,0:T(8,128)(2,1)}) custom-call(s32[1]{0:T(128)} %bitcast.7.tm_ref, f32[2,32,16,512]{3,2,1,0:T(8,128)} %retarded_ref.5, f32[2,32,16,512]{3,2,1,0:T(8,128)} %lesser_ref.5, f32[4,32,16,128]{3,2,1,0:T(8,128)} %collective-permute-done.3.rim_ref), custom_call_target="tpu_custom_call" | custom-call | tf_op jit(solution)/shard_map/pallas_call | solution.py:535
  69.5 4.4 %all-to-all-done.3 = f32[32,16,128]{2,1,0:T(8,128)S(1)} async-done(((f32[32,16,128]{2,1,0:T(8,128)}), f32[32,16,128]{2,1,0:T(8,128)S(1)}, u32[]{:S(2)}, u32[]{:S(2)}) %all-to-all-start.3) | async-done | bytes 262176 | tf_op jit(solution)/shard_map/all_to_all | solution.py:577
  74.0 0.5 shard_map.89
  74.5 0.0 copy-start.3
  74.6 0.6 copy-done.3
  75.2 2.8 %all-to-all-start.4 = ((f32[32,8,128]{2,1,0:T(8,128)}), f32[32,8,128]{2,1,0:T(8,128)S(1)}, u32[]{:S(2)}, u32[]{:S(2)}) async-start(f32[32,8,128]{2,1,0:T(8,128)} %bitcast.19), calls=%async_computation.4 | async-start | bytes 262144 | tf_op jit(solution)/shard_map/all_to_all | solution.py:554
  78.0 5.8 %shard_map.90 = (bf16[8,384,256]{2,1,0:T(8,128)(2,1)}, bf16[8,384,256]{2,1,0:T(8,128)(2,1)}) custom-call(s32[1]{0:T(128)} %bitcast.10.tm_ref, f32[2,32,16,512]{3,2,1,0:T(8,128)} %retarded_ref.5, f32[2,32,16,512]{3,2,1,0:T(8,128)} %lesser_ref.5, f32[4,32,16,128]{3,2,1,0:T(8,128)} %collective-permute-done.3.rim_ref), custom_call_target="tpu_custom_call" | custom-call | tf_op jit(solution)/shard_map/pallas_call | solution.py:535
  83.8 2.5 %all-to-all-done.4 = f32[32,8,128]{2,1,0:T(8,128)S(1)} async-done(((f32[32,8,128]{2,1,0:T(8,128)}), f32[32,8,128]{2,1,0:T(8,128)S(1)}, u32[]{:S(2)}, u32[]{:S(2)}) %all-to-all-start.4) | async-done | bytes 131104 | tf_op jit(solution)/shard_map/all_to_all | solution.py:554
  86.3 1.8 %shard_map.91 = f32[32,16,128]{2,1,0:T(8,128)} custom-call(f32[8,4,8,128]{3,2,1,0:T(8,128)S(1)} %bitcast.21, bf16[512,256]{1,0:T(8,128)(2,1)S(1)} %copy-done.1, bf16[512,256]{1,0:T(8,128)(2,1)S(1)} %copy-done, f32[1,128]{1,0:T(1,128)S(1)} %pad_maximum_fusion.2.strength_ref, f32[1,128]{1,0:T(1,128)S(1)} %concatenate.16.mean_ref), custom_call_target="tpu_custom_call" | custom-call | tf_op jit(solution)/shard_map/pallas_call | solution.py:479
  88.1 3.4 %all-to-all-start.5 = ((f32[32,16,128]{2,1,0:T(8,128)}), f32[32,16,128]{2,1,0:T(8,128)S(1)}, u32[]{:S(2)}, u32[]{:S(2)}) async-start(f32[32,16,128]{2,1,0:T(8,128)} %shard_map.91), calls=%async_computation.5 | async-start | bytes 524288 | tf_op jit(solution)/shard_map/all_to_all | solution.py:577
  91.5 5.8 %shard_map.92 = (bf16[8,384,256]{2,1,0:T(8,128)(2,1)}, bf16[8,384,256]{2,1,0:T(8,128)(2,1)}) custom-call(s32[1]{0:T(128)} %bitcast.tm_ref, f32[2,32,16,512]{3,2,1,0:T(8,128)} %retarded_ref.5, f32[2,32,16,512]{3,2,1,0:T(8,128)} %lesser_ref.5, f32[4,32,16,128]{3,2,1,0:T(8,128)} %collective-permute-done.3.rim_ref), custom_call_target="tpu_custom_call" | custom-call | tf_op jit(solution)/shard_map/pallas_call | solution.py:535
  97.3 4.5 %all-to-all-done.5 = f32[32,16,128]{2,1,0:T(8,128)S(1)} async-done(((f32[32,16,128]{2,1,0:T(8,128)}), f32[32,16,128]{2,1,0:T(8,128)S(1)}, u32[]{:S(2)}, u32[]{:S(2)}) %all-to-all-start.5) | async-done | bytes 262176 | tf_op jit(solution)/shard_map/all_to_all | solution.py:577
  101.8 0.6 collective-permute-start.6
  102.4 0.0 collective-permute-start.5
  102.4 4.0 %shard_map.93.others_0_ = f32[2,32,16,512]{3,2,1,0:T(8,128)} custom-call(s32[1]{0:T(128)} %bitcast.5.tm_ref, f32[512,128]{1,0:T(8,128)S(1)} %bitcast.17, f32[2,32,16,16]{3,2,1,0:T(8,128)S(1)} %copy.12.propagator_ref, bf16[8,384,256]{2,1,0:T(8,128)(2,1)} %get-tuple-element.103.high_ref, bf16[8,384,256]{2,1,0:T(8,128)(2,1)} %get-tuple-element.104.low_ref), custom_call_target="tpu_custom_call" | custom-call | tf_op jit(solution)/shard_map/pallas_call | solution.py:592
  106.4 0.0 collective-permute-done.6.arrived_ref
  106.5 4.0 %shard_map.94.others_0_ = f32[2,32,16,512]{3,2,1,0:T(8,128)} custom-call(s32[1]{0:T(128)} %bitcast.7.tm_ref, f32[512,128]{1,0:T(8,128)S(1)} %collective-permute-done.6.arrived_ref, f32[2,32,16,16]{3,2,1,0:T(8,128)S(1)} %copy.12.propagator_ref, bf16[8,384,256]{2,1,0:T(8,128)(2,1)} %get-tuple-element.101.high_ref, ...), custom_call_target="tpu_custom_call", output_to_operand_aliasing={{}: (5, {})} | custom-call | tf_op jit(solution)/shard_map/pallas_call | solution.py:592
  110.5 0.0 collective-permute-done.5.arrived_ref
  110.5 0.9 collective-permute-start.7
  111.3 4.0 %shard_map.95.others_0_ = f32[2,32,16,512]{3,2,1,0:T(8,128)} custom-call(s32[1]{0:T(128)} %bitcast.10.tm_ref, f32[512,128]{1,0:T(8,128)S(1)} %collective-permute-done.5.arrived_ref, f32[2,32,16,16]{3,2,1,0:T(8,128)S(1)} %copy.12.propagator_ref, bf16[8,384,256]{2,1,0:T(8,128)(2,1)} %get-tuple-element.108.high_ref, ...), custom_call_target="tpu_custom_call", output_to_operand_aliasing={{}: (5, {})} | custom-call | tf_op jit(solution)/shard_map/pallas_call | solution.py:592
  115.4 4.0 %shard_map.96 = f32[2,32,16,512]{3,2,1,0:T(8,128)} custom-call(s32[1]{0:T(128)} %bitcast.tm_ref, f32[512,128]{1,0:T(8,128)S(1)} %collective-permute-done.7.arrived_ref, f32[2,32,16,16]{3,2,1,0:T(8,128)S(1)} %copy.12.propagator_ref, bf16[8,384,256]{2,1,0:T(8,128)(2,1)} %get-tuple-element.106.high_ref, ...), custom_call_target="tpu_custom_call", output_to_operand_aliasing={{}: (5, {})} | custom-call | tf_op jit(solution)/shard_map/pallas_call | solution.py:592
  (27 shorter events, 0.1 us)
Async XLA Ops:
  3.6 3.5 %collective-permute-start = (f32[512,128]{1,0:T(8,128)S(1)}, f32[512,128]{1,0:T(8,128)S(1)}, u32[]{:S(2)}, u32[]{:S(2)}) collective-permute-start(f32[512,128]{1,0:T(8,128)S(1)} %get-tuple-element.59), channel_id=1, source_target_pairs={{3,2},{7,6},{11,10},{15,14},{19,18},{23,22},{27,26},{31,30}} | collective-permute-start | bytes 786440 | tf_op jit(solution)/shard_map/ppermute | solution.py:504
  4.3 24.1 %collective-permute-start.1 = (f32[4,8,16,256]{3,2,1,0:T(8,128)S(1)}, f32[4,8,16,256]{3,2,1,0:T(8,128)}, u32[]{:S(2)}, u32[]{:S(2)}) collective-permute-start(f32[4,8,16,256]{3,2,1,0:T(8,128)S(1)} %get-tuple-element.61), channel_id=1, source_target_pairs={{3,0},{7,4},{11,8},{15,12},{19,16},{23,20},{27,24},{31,28}} | collective-permute-start | bytes 1572872 | tf_op jit(solution)/shard_map/ppermute | solution.py:505
  5.8 22.6 %collective-permute-start.2 = (f32[4,8,16,256]{3,2,1,0:T(8,128)S(1)}, f32[4,8,16,256]{3,2,1,0:T(8,128)}, u32[]{:S(2)}, u32[]{:S(2)}) collective-permute-start(f32[4,8,16,256]{3,2,1,0:T(8,128)S(1)} %get-tuple-element.62), channel_id=1, source_target_pairs={{3,1},{7,5},{11,9},{15,13},{19,17},{23,21},{27,25},{31,29}} | collective-permute-start | bytes 1572872 | tf_op jit(solution)/shard_map/ppermute | solution.py:505
  7.1 1.7 %copy-start.5 = (f32[2,32,16,512]{3,2,1,0:T(8,128)S(1)}, f32[2,32,16,512]{3,2,1,0:T(8,128)}, u32[]{:S(2)}) copy-start(f32[2,32,16,512]{3,2,1,0:T(8,128)} %retarded_ref.5) | copy-start | bytes 6291460
  7.8 3.0 %copy-start.12 = (f32[8]{0:T(128)S(1)}, f32[8]{0:T(128)}, u32[]{:S(2)}) copy-start(f32[8]{0:T(128)} %param.13) | copy-start | bytes 100
  7.8 3.0 %copy-start.10 = (f32[256]{0:T(256)S(1)}, f32[256]{0:T(256)}, u32[]{:S(2)}) copy-start(f32[256]{0:T(256)} %param.11) | copy-start | bytes 3076
  7.8 13.1 %slice-start = ((f32[2,32,16,512]{3,2,1,0:T(8,128)}), f32[2,32,16,128]{3,2,1,0:T(8,128)S(1)}, s32[]{:S(2)}) async-start(f32[2,32,16,512]{3,2,1,0:T(8,128)} %retarded_ref.5), calls=%async_computation.6 | async-start | bytes 1048576 | tf_op jit(solution)/shard_map/slice | solution.py:516
  7.8 13.1 %slice-start.1 = ((f32[2,32,16,512]{3,2,1,0:T(8,128)}), f32[2,32,16,128]{3,2,1,0:T(8,128)S(1)}, s32[]{:S(2)}) async-start(f32[2,32,16,512]{3,2,1,0:T(8,128)} %lesser_ref.5), calls=%async_computation.7 | async-start | bytes 1048576 | tf_op jit(solution)/shard_map/slice | solution.py:516
  10.8 15.7 %copy-start.11 = (f32[256]{0:T(256)S(1)}, f32[256]{0:T(256)}, u32[]{:S(2)}) copy-start(f32[256]{0:T(256)} %param.12) | copy-start | bytes 3076
  10.8 20.3 %copy-start = (bf16[512,256]{1,0:T(8,128)(2,1)S(1)}, bf16[512,256]{1,0:T(8,128)(2,1)}, u32[]{:S(2)}) copy-start(bf16[512,256]{1,0:T(8,128)(2,1)} %constant.33.clone.low_ref) | copy-start | bytes 786436
  10.8 20.3 %copy-start.1 = (bf16[512,256]{1,0:T(8,128)(2,1)S(1)}, bf16[512,256]{1,0:T(8,128)(2,1)}, u32[]{:S(2)}) copy-start(bf16[512,256]{1,0:T(8,128)(2,1)} %constant.32.clone.high_ref) | copy-start | bytes 786436
  10.9 20.1 %all-to-all-start = ((f32[32,16,128]{2,1,0:T(8,128)}), f32[32,16,128]{2,1,0:T(8,128)S(1)}, u32[]{:S(2)}, u32[]{:S(2)}) async-start(f32[32,16,128]{2,1,0:T(8,128)} %bitcast.23), calls=%async_computation | async-start | bytes 524288 | tf_op jit(solution)/shard_map/all_to_all | solution.py:554
  20.8 4.8 %copy-start.6 = (f32[2,8,16,256]{3,2,1,0:T(8,128)S(1)}, f32[2,8,16,256]{3,2,1,0:T(8,128)}, u32[]{:S(2)}) copy-start(f32[2,8,16,256]{3,2,1,0:T(8,128)} %get-tuple-element.112) | copy-start | bytes 786436
  20.8 4.8 %copy-start.7 = (f32[2,8,16,256]{3,2,1,0:T(8,128)S(1)}, f32[2,8,16,256]{3,2,1,0:T(8,128)}, u32[]{:S(2)}) copy-start(f32[2,8,16,256]{3,2,1,0:T(8,128)} %get-tuple-element.115) | copy-start | bytes 786436
  22.0 14.0 %copy-start.8 = (f32[2,8,16,256]{3,2,1,0:T(8,128)S(1)}, f32[2,8,16,256]{3,2,1,0:T(8,128)}, u32[]{:S(2)}) copy-start(f32[2,8,16,256]{3,2,1,0:T(8,128)} %get-tuple-element.111) | copy-start | bytes 786436
  22.0 14.0 %copy-start.9 = (f32[2,8,16,256]{3,2,1,0:T(8,128)S(1)}, f32[2,8,16,256]{3,2,1,0:T(8,128)}, u32[]{:S(2)}) copy-start(f32[2,8,16,256]{3,2,1,0:T(8,128)} %get-tuple-element.116) | copy-start | bytes 786436
  22.0 17.5 %collective-permute-start.3 = (f32[4,32,16,128]{3,2,1,0:T(8,128)}, f32[4,32,16,128]{3,2,1,0:T(8,128)}, u32[]{:S(2)}, u32[]{:S(2)}) collective-permute-start(f32[4,32,16,128]{3,2,1,0:T(8,128)} %pad_maximum_fusion), channel_id=1, source_target_pairs={{0,1},{1,2},{2,3},{4,5},{5,6},{6,7},{8,9},{9,10},{10,11},{12,13},{... | collective-permute-start | bytes 3145736 | tf_op jit(solution)/shard_map/ppermute | solution.py:25
  26.6 9.4 %collective-permute-start.4 = (f32[4,8,16,256]{3,2,1,0:T(8,128)}, f32[4,8,16,256]{3,2,1,0:T(8,128)}, u32[]{:S(2)}, u32[]{:S(2)}) collective-permute-start(f32[4,8,16,256]{3,2,1,0:T(8,128)} %pad_maximum_fusion.1), channel_id=1, source_target_pairs={{3,2},{7,6},{11,10},{15,14},{19,18},{23,22},{27,26},{31,30}} | collective-permute-start | bytes 1572872 | tf_op jit(solution)/shard_map/ppermute | solution.py:515
  32.9 13.3 %all-to-all-start.1 = ((f32[32,16,128]{2,1,0:T(8,128)}), f32[32,16,128]{2,1,0:T(8,128)S(1)}, u32[]{:S(2)}, u32[]{:S(2)}) async-start(f32[32,16,128]{2,1,0:T(8,128)} %shard_map.83), calls=%async_computation.1 | async-start | bytes 524288 | tf_op jit(solution)/shard_map/all_to_all | solution.py:577
  46.7 0.7 copy-start.4
  47.4 11.1 %all-to-all-start.2 = ((f32[32,8,128]{2,1,0:T(8,128)}), f32[32,8,128]{2,1,0:T(8,128)S(1)}, u32[]{:S(2)}, u32[]{:S(2)}) async-start(f32[32,8,128]{2,1,0:T(8,128)} %bitcast.20), calls=%async_computation.2 | async-start | bytes 262144 | tf_op jit(solution)/shard_map/all_to_all | solution.py:554
  59.6 0.7 copy-start.2
  60.3 13.7 %all-to-all-start.3 = ((f32[32,16,128]{2,1,0:T(8,128)}), f32[32,16,128]{2,1,0:T(8,128)S(1)}, u32[]{:S(2)}, u32[]{:S(2)}) async-start(f32[32,16,128]{2,1,0:T(8,128)} %copy-done.2), calls=%async_computation.3 | async-start | bytes 524288 | tf_op jit(solution)/shard_map/all_to_all | solution.py:577
  74.5 0.7 copy-start.3
  75.2 11.1 %all-to-all-start.4 = ((f32[32,8,128]{2,1,0:T(8,128)}), f32[32,8,128]{2,1,0:T(8,128)S(1)}, u32[]{:S(2)}, u32[]{:S(2)}) async-start(f32[32,8,128]{2,1,0:T(8,128)} %bitcast.19), calls=%async_computation.4 | async-start | bytes 262144 | tf_op jit(solution)/shard_map/all_to_all | solution.py:554
  88.1 13.7 %all-to-all-start.5 = ((f32[32,16,128]{2,1,0:T(8,128)}), f32[32,16,128]{2,1,0:T(8,128)S(1)}, u32[]{:S(2)}, u32[]{:S(2)}) async-start(f32[32,16,128]{2,1,0:T(8,128)} %shard_map.91), calls=%async_computation.5 | async-start | bytes 524288 | tf_op jit(solution)/shard_map/all_to_all | solution.py:577
  101.8 4.7 %collective-permute-start.6 = (f32[512,128]{1,0:T(8,128)S(1)}, f32[512,128]{1,0:T(8,128)S(1)}, u32[]{:S(2)}, u32[]{:S(2)}) collective-permute-start(f32[512,128]{1,0:T(8,128)S(1)} %bitcast.15), channel_id=1, source_target_pairs={{0,1},{1,0},{2,3},{3,2},{4,5},{5,4},{6,7},{7,6},{8,9},{9,8},{10,11... | collective-permute-start | bytes 786440 | tf_op jit(solution)/shard_map/ppermute | solution.py:615
  102.4 8.1 %collective-permute-start.5 = (f32[512,128]{1,0:T(8,128)S(1)}, f32[512,128]{1,0:T(8,128)S(1)}, u32[]{:S(2)}, u32[]{:S(2)}) collective-permute-start(f32[512,128]{1,0:T(8,128)S(1)} %bitcast.16), channel_id=1, source_target_pairs={{0,2},{1,3},{2,0},{3,1},{4,6},{5,7},{6,4},{7,5},{8,10},{9,11},{10,... | collective-permute-start | bytes 786440 | tf_op jit(solution)/shard_map/ppermute | solution.py:615
  110.5 4.9 %collective-permute-start.7 = (f32[512,128]{1,0:T(8,128)S(1)}, f32[512,128]{1,0:T(8,128)S(1)}, u32[]{:S(2)}, u32[]{:S(2)}) collective-permute-start(f32[512,128]{1,0:T(8,128)S(1)} %collective-permute-done.5.arrived_ref), channel_id=1, source_target_pairs={{0,1},{1,0},{2,3},{3,2},{4,5},{5,4},{6,7},{7,6},{8,9},{9,8},{10,11... | collective-permute-start | bytes 786440 | tf_op jit(solution)/shard_map/ppermute | solution.py:615

commit v3 on v2

--- a/solution.py
+++ b/solution.py
@@ -218,9 +218,8 @@
         copy.wait()
 
 
-def first_window_kernel(
-    own, propagator_ref, retarded_ref, lesser_ref, low_ref, high_ref, near0_ref, near1_ref, window_ref, arrive, pass_on
-):
+def first_window_kernel(own, propagator_ref, retarded_ref, lesser_ref, low_ref, high_ref, *others):
+    *near_refs, rim_ref, window_ref, arrive, pass_on = others
     momenta, columns = lesser_ref.shape[1], lesser_ref.shape[3]
     half = momenta // 2
     fetches = start_all(
@@ -233,17 +232,16 @@
             for number, first in enumerate(range(0, momenta, own))
         ]
     )
-    copies = start_all(
-        [
-            pltpu.make_async_copy(
-                ref.at[:, tm * own : (tm + 1) * own, :, columns - 2 * TILE :],
-                near_ref.at[2 * kind : 2 * kind + 2],
-                pass_on.at[tm, kind],
-            )
-            for tm, near_ref in enumerate((near0_ref, near1_ref))
-            for kind, ref in enumerate((retarded_ref, lesser_ref))
-        ]
-    )
+    copies = []
+    for kind, ref in enumerate((retarded_ref, lesser_ref)):
+        both = pl.ds(2 * kind, 2)
+        for tm, near_ref in enumerate(near_refs):
+            source = ref.at[:, tm * own : (tm + 1) * own, :, columns - 2 * TILE :]
+            copies.append(pltpu.make_async_copy(source, near_ref.at[both], pass_on.at[kind, tm]))
+        copies.append(
+            pltpu.make_async_copy(ref.at[:, :, :, columns - TILE :], rim_ref.at[both], pass_on.at[kind, len(near_refs)])
+        )
+    start_all(copies)
     for number, fetch in enumerate(fetches):
         fetch.wait()
         for k in range(number * own, (number + 1) * own):
@@ -487,35 +485,29 @@
     half = momenta_here // 2
     sent = f32((devices * half, TILE))
     near_shape = f32((4, own, ORB, 2 * TILE))
-    low, high, *near = pl.pallas_call(
+    low, high, *near, rim = pl.pallas_call(
         functools.partial(first_window_kernel, own),
-        out_shape=(sent, sent, near_shape, near_shape),
+        out_shape=(sent, sent, *[near_shape] * peers, f32((4, momenta_here, ORB, TILE))),
         in_specs=[VMEM, IN_HBM, IN_HBM],
-        out_specs=(VMEM,) * 4,
+        out_specs=(VMEM,) * (peers + 3),
         scratch_shapes=[
             pltpu.VMEM((2, momenta_here, ORB, TILE), jnp.float32),
-            pltpu.SemaphoreType.DMA((momenta_here // own,)),
-            pltpu.SemaphoreType.DMA((2, 2)),
+            pltpu.SemaphoreType.DMA((peers,)),
+            pltpu.SemaphoreType.DMA((2, peers + 1)),
         ],
         compiler_params=limit(8),
     )(propagator, *(pltpu.with_memory_space_constraint(x, pltpu.HBM) for x in (hist_retarded, hist_lesser)))
     here = lax.axis_index("tm")
     last = here == peers - 1
     low = lax.ppermute(low, "tm", [(3, 2)])
-    near = [lax.ppermute(block, "tm", [(3, tm)]) for tm, block in enumerate(near)]
+    mine = near.pop()
+    near[:2] = [lax.ppermute(block, "tm", [(3, tm)]) for tm, block in enumerate(near[:2])]
     send = jnp.where(last, high, low).reshape(devices, half, TILE)
-    send, hist_lesser, hist_retarded, coupling, mf_weight, lag_weight = lax.optimization_barrier(
-        (send, hist_lesser, hist_retarded, coupling, mf_weight, lag_weight)
-    )
-
-    def near_of(tm):
-        momenta = slice(tm * own, (tm + 1) * own)
-        return jnp.concatenate([x[:, momenta, :, columns - 2 * TILE :] for x in (hist_retarded, hist_lesser)], axis=0)
-
-    near.append(lax.ppermute(near_of(2), "tm", [(3, 2)]))
-    rim = jnp.concatenate([x[..., columns - TILE :] for x in (hist_retarded, hist_lesser)], axis=0)
+    send, near[2], rim, hist_lesser, hist_retarded, coupling, mf_weight, lag_weight = lax.optimization_barrier(
+        (send, near[2], rim, hist_lesser, hist_retarded, coupling, mf_weight, lag_weight)
+    )
+    near[2] = lax.ppermute(near[2], "tm", [(3, 2)])
     rim = shifted(rim, "tm", 1)
-
     me = lax.axis_index("mom") * peers + lax.axis_index("tm")
     last_mark = (jnp.arange(W) == W - 1).astype(jnp.float32)
     strong = (coupling * coupling).reshape(ORB, 1, ORB) * lag_weight[:, None]
@@ -567,7 +559,6 @@
         )
         if sweep == 0:
             near[2], _ = lax.optimization_barrier((near[2], back))
-            mine = near_of(peers - 1)
             for tm, received in enumerate(near):
                 mine = jnp.where(here == tm, received, mine)
             rungs = bf16((own, 2 * TILE, 2 * TILE))
@@ -575,7 +566,7 @@
             rim, *rungs = lax.optimization_barrier((rim, *rungs))
             propagator_own = own_block(propagator, own, 1)
         arrived = lax.all_to_all(back, both_axes, 0, 0, tiled=True)
-        if sweep:
+        if sweep + 1 < PASSES:
             arrived = beside(arrived, back)
         arrived = arrived.reshape(2 * count, TILE)
         if sweep + 1 < PASSES:
@@ -607,7 +598,7 @@
             (here ^ step).reshape(1).astype(jnp.int32),
             coefficients_of,
             propagator,
-            *[pltpu.with_memory_space_constraint(x, pltpu.HBM) for x in ladders[step]],
+            *[pltpu.with_memory_space_constraint(x, pltpu.HBM) if step == 0 else x for x in ladders[step]],
             *before,
         )
 

time: 120 us -> 116 us (0.967)
  blocking collectives: 0 us -> 13.5 us
  waiting for transfers between devices: 24.6 us -> 15.6 us
  starting transfers between devices: 35.4 us -> 32.5 us
  Pallas kernels: 48.2 us -> 45.5 us
  local copies, waits for them, and re-layouts: 6.59 us -> 4.9 us
    all_to_all x0 -> x1, blocking collectives: none -> 13.5 us  [on_device_tiled(): arrived = lax.all_to_all(back, both_axes, 0, 0, tiled=True)]
    all_to_all x3 -> x2, waiting for transfers between devices: 15.6 us -> 6.68 us  [on_device_tiled(): arrived = lax.all_to_all(back, both_axes, 0, 0, tiled=True)]
    all_to_all x3 -> x2, starting transfers between devices: 9.93 us -> 6.26 us  [on_device_tiled(): arrived = lax.all_to_all(back, both_axes, 0, 0, tiled=True)]
    pallas_call x4, Pallas kernels: 16 us -> 12.8 us  [finish(): pl.pallas_call(functools.partial(final_kernel, own, len(before)), out_sha...]
    slice x5 -> x0, local copies, waits for them, and re-layouts: 2.06 us -> none  [the longest x1 2.05 us: near_of(): x[:, momenta, :, columns - 2 * TILE:]]
    concatenate x2 -> x0, other arithmetic: 1.89 us -> none  [the longest x1 1.04 us: on_device_tiled(): jnp.concatenate([x[..., columns - TILE:] for x in (hist_retarded, hist_le...]
    ppermute x1, waiting for transfers between devices: 1.22 us -> 0.01 us  [shifted(): return lax.ppermute(x, axis, pairs)]
    unnamed x27 -> x29, local copies, waits for them, and re-layouts: 4.18 us -> 3.28 us
  transfers between devices with their start and end apart: 14 -> 13, of which waited for: 7 -> 6; matrix products, arithmetic and copies ran while one was open for 5% -> 4% of each run, Pallas kernels for 32% -> 31%
where the time goes in v3:
time: 116 us
  Pallas kernels  45.5 us (39%)
  starting transfers between devices  32.5 us (28%)
  waiting for transfers between devices  15.6 us (13%)
  blocking collectives  13.5 us (12%)
  local copies, waits for them, and re-layouts  4.9 us (4%)
  other arithmetic  3.2 us (3%)
    pallas_call x4, Pallas kernels, beside(): pl.pallas_call(final_ladder_kernel, out_shape=(pltpu.HBM(ladder_shape, jn...  23.2 us
    all_to_all x3, starting transfers between devices, on_device_tiled(): arrived = lax.all_to_all(send, both_axes, 0, 0, tiled=True)  15.4 us
    all_to_all x1, blocking collectives, on_device_tiled(): arrived = lax.all_to_all(back, both_axes, 0, 0, tiled=True)  13.5 us
    pallas_call x4, Pallas kernels, finish(): pl.pallas_call(functools.partial(final_kernel, own, len(before)), out_sha...  12.8 us
    all_to_all x3, waiting for transfers between devices, on_device_tiled(): arrived = lax.all_to_all(send, both_axes, 0, 0, tiled=True)  8.35 us
    all_to_all x2, waiting for transfers between devices, on_device_tiled(): arrived = lax.all_to_all(back, both_axes, 0, 0, tiled=True)  6.68 us
    all_to_all x2, starting transfers between devices, on_device_tiled(): arrived = lax.all_to_all(back, both_axes, 0, 0, tiled=True)  6.26 us
    pallas_call x6, Pallas kernels, call(): pl.pallas_call(kernel, out_shape=shapes, in_specs=[VMEM] * len(operands),...  6 us
  transfers between devices with their start and end apart: 13, of which 6 were waited for; matrix products, arithmetic and copies ran while one was open for 4% of the time, Pallas kernels for 31%

profile of v3, /device:TPU:1, one launch (start us, length us, event | category | flops | bytes accessed | tf_op | source)
XLA Modules:
  0.0 115.7 jit_solution(11721417018245441954)
XLA Ops:
  0.0 1.2 %copy.12.propagator_ref = f32[2,32,16,16]{3,2,1,0:T(8,128)S(1)} copy(f32[2,32,16,16]{1,3,2,0:T(8,128)} %param.10) | data formatting | bytes 131072 | tf_op args[2]
  1.2 0.0 copy-start.11
  1.2 0.0 copy-start.13
  1.3 0.0 copy-start.12
  1.3 3.5 %shard_map.82 = (f32[512,128]{1,0:T(8,128)}, f32[512,128]{1,0:T(8,128)S(1)}, f32[4,8,16,256]{3,2,1,0:T(8,128)S(1)}, f32[4,8,16,256]{3,2,1,0:T(8,128)S(1)}, f32[4...) custom-call(f32[2,32,16,16]{3,2,1,0:T(8,128)S(1)} %copy.12.propagator_ref, ...), custom_call_target="tpu_custom_call" | custom-call | tf_op jit(solution)/shard_map/pallas_call | solution.py:488
  4.7 0.0 copy-start
  4.8 0.0 copy-start.1
  4.8 1.5 %collective-permute-start = (f32[512,128]{1,0:T(8,128)}, f32[512,128]{1,0:T(8,128)}, u32[]{:S(2)}, u32[]{:S(2)}) collective-permute-start(f32[512,128]{1,0:T(8,128)} %get-tuple-element.64), channel_id=1, source_target_pairs={{3,2},{7,6},{11,10},{15,14},{19,18},{23,22},{27,26},{31,30}} | collective-permute-start | bytes 786440 | tf_op jit(solution)/shard_map/ppermute | solution.py:502
  6.3 1.5 %collective-permute-start.1 = (f32[4,8,16,256]{3,2,1,0:T(8,128)S(1)}, f32[4,8,16,256]{3,2,1,0:T(8,128)}, u32[]{:S(2)}, u32[]{:S(2)}) collective-permute-start(f32[4,8,16,256]{3,2,1,0:T(8,128)S(1)} %get-tuple-element.68), channel_id=1, source_target_pairs={{3,0},{7,4},{11,8},{15,12},{19,16},{23,20},{27,24},{31,28}} | collective-permute-start | bytes 1572872 | tf_op jit(solution)/shard_map/ppermute | solution.py:504
  7.7 1.3 %collective-permute-start.2 = (f32[4,8,16,256]{3,2,1,0:T(8,128)S(1)}, f32[4,8,16,256]{3,2,1,0:T(8,128)}, u32[]{:S(2)}, u32[]{:S(2)}) collective-permute-start(f32[4,8,16,256]{3,2,1,0:T(8,128)S(1)} %get-tuple-element.69), channel_id=1, source_target_pairs={{3,1},{7,5},{11,9},{15,13},{19,17},{23,21},{27,25},{31,29}} | collective-permute-start | bytes 1572872 | tf_op jit(solution)/shard_map/ppermute | solution.py:504
  9.0 0.0 collective-permute-done
  9.0 1.7 %broadcast_select_fusion = f32[512,128]{1,0:T(8,128)} fusion(f32[512,128]{1,0:T(8,128)S(1)} %get-tuple-element.63, f32[512,128]{1,0:T(8,128)} %collective-permute-done, pred[]{:T(512)S(6)} %eq.15), kind=kLoop, calls=%fused_computation.1 | loop fusion | flops 65536 | bytes 786433 | tf_op jit(solution)/shard_map/jit(_where)/select_n | solution.py:505
  10.7 0.1 mul.51
  10.8 8.9 %all-to-all-start = ((f32[32,16,128]{2,1,0:T(8,128)}), f32[32,16,128]{2,1,0:T(8,128)S(1)}, u32[]{:S(2)}, u32[]{:S(2)}) async-start(f32[32,16,128]{2,1,0:T(8,128)} %bitcast.23), calls=%async_computation | async-start | bytes 524288 | tf_op jit(solution)/shard_map/all_to_all | solution.py:546
  19.7 3.5 %collective-permute-start.3 = (f32[4,32,16,128]{3,2,1,0:T(8,128)}, f32[4,32,16,128]{3,2,1,0:T(8,128)}, u32[]{:S(2)}, u32[]{:S(2)}) collective-permute-start(f32[4,32,16,128]{3,2,1,0:T(8,128)} %get-tuple-element.76), channel_id=1, source_target_pairs={{0,1},{1,2},{2,3},{4,5},{5,6},{6,7},{8,9},{9,10},{10,11},{12,13},{... | collective-permute-start | bytes 3145736 | tf_op jit(solution)/shard_map/ppermute | solution.py:25
  23.3 0.1 broadcast_multiply_fusion.1
  23.4 0.1 mul.57
  23.5 1.5 %collective-permute-start.4 = (f32[4,8,16,256]{3,2,1,0:T(8,128)S(1)}, f32[4,8,16,256]{3,2,1,0:T(8,128)}, u32[]{:S(2)}, u32[]{:S(2)}) collective-permute-start(f32[4,8,16,256]{3,2,1,0:T(8,128)S(1)} %get-tuple-element.77), channel_id=1, source_target_pairs={{3,2},{7,6},{11,10},{15,14},{19,18},{23,22},{27,26},{31,30}} | collective-permute-start | bytes 1572872 | tf_op jit(solution)/shard_map/ppermute | solution.py:509
  24.9 0.1 broadcast_multiply_fusion
  25.0 0.7 mul.62
  25.7 0.1 mul.55
  25.8 0.7 constant_dynamic-slice_fusion.1
  26.4 0.1 pad_maximum_fusion.strength_ref
  26.5 0.0 collective-permute-done.1
  26.5 0.0 collective-permute-done.2
  26.5 3.5 %all-to-all-done = f32[32,16,128]{2,1,0:T(8,128)S(1)} async-done(((f32[32,16,128]{2,1,0:T(8,128)}), f32[32,16,128]{2,1,0:T(8,128)S(1)}, u32[]{:S(2)}, u32[]{:S(2)}) %all-to-all-start) | async-done | bytes 262176 | tf_op jit(solution)/shard_map/all_to_all | solution.py:546
  30.0 1.8 %shard_map.83 = f32[32,16,128]{2,1,0:T(8,128)} custom-call(f32[8,4,16,128]{3,2,1,0:T(8,128)S(1)} %bitcast.14, bf16[512,256]{1,0:T(8,128)(2,1)S(1)} %copy-done.1, bf16[512,256]{1,0:T(8,128)(2,1)S(1)} %copy-done, f32[1,128]{1,0:T(1,128)S(1)} %pad_maximum_fusion.strength_ref, f32[1,128]{1,0:T(1,128)S(1)} %concatenate.7.mean_ref), custom_call_target="tpu_custom_call" | custom-call | tf_op jit(solution)/shard_map/pallas_call | solution.py:477
  31.8 2.8 %all-to-all-start.1 = ((f32[32,16,128]{2,1,0:T(8,128)}), f32[32,16,128]{2,1,0:T(8,128)S(1)}, u32[]{:S(2)}, u32[]{:S(2)}) async-start(f32[32,16,128]{2,1,0:T(8,128)} %shard_map.83), calls=%async_computation.1 | async-start | bytes 524288 | tf_op jit(solution)/shard_map/all_to_all | solution.py:568
  34.6 0.0 collective-permute-done.4
  34.6 1.3 %select_select_fusion.near_ref = f32[4,8,16,256]{3,2,1,0:T(8,128)S(1)} fusion(f32[4,8,16,256]{3,2,1,0:T(8,128)} %collective-permute-done.4, f32[4,8,16,256]{3,2,1,0:T(8,128)} %collective-permute-done.2, f32[4,8,16,256]{3,2,1,0:T(8,128)} %collective-permute-done.1, f32[4,8,16,256]{3,2,1,0:T(8,128)S(1)} %get-tuple-element.81, pred[]{:T(512)S(6)} %eq.19, ...), kind=kLoop, calls=%fused_computation | loop fusion | flops 393216 | bytes 2621443 | tf_op jit(solution)/shard_map/jit(_where)/select_n | solution.py:563
  35.9 1.0 shard_map.84
  36.9 0.0 collective-permute-done.3.rim_ref
  36.9 5.8 %shard_map.85 = (bf16[8,384,256]{2,1,0:T(8,128)(2,1)}, bf16[8,384,256]{2,1,0:T(8,128)(2,1)}) custom-call(s32[1]{0:T(128)} %bitcast.3.tm_ref, f32[2,32,16,512]{3,2,1,0:T(8,128)} %retarded_ref.5, f32[2,32,16,512]{3,2,1,0:T(8,128)} %lesser_ref.5, f32[4,32,16,128]{3,2,1,0:T(8,128)} %collective-permute-done.3.rim_ref), custom_call_target="tpu_custom_call" | custom-call | tf_op jit(solution)/shard_map/pallas_call | solution.py:527
  42.7 2.2 %all-to-all-done.1 = f32[32,16,128]{2,1,0:T(8,128)S(1)} async-done(((f32[32,16,128]{2,1,0:T(8,128)}), f32[32,16,128]{2,1,0:T(8,128)S(1)}, u32[]{:S(2)}, u32[]{:S(2)}) %all-to-all-start.1) | async-done | bytes 262176 | tf_op jit(solution)/shard_map/all_to_all | solution.py:568
  45.0 0.5 shard_map.86
  45.5 0.0 copy-start.10
  45.5 0.6 copy-done.10
  46.2 3.7 %all-to-all-start.2 = ((f32[32,8,128]{2,1,0:T(8,128)}), f32[32,8,128]{2,1,0:T(8,128)S(1)}, u32[]{:S(2)}, u32[]{:S(2)}) async-start(f32[32,8,128]{2,1,0:T(8,128)} %bitcast.20), calls=%async_computation.2 | async-start | bytes 262144 | tf_op jit(solution)/shard_map/all_to_all | solution.py:546
  49.9 5.8 %shard_map.87 = (bf16[8,384,256]{2,1,0:T(8,128)(2,1)}, bf16[8,384,256]{2,1,0:T(8,128)(2,1)}) custom-call(s32[1]{0:T(128)} %bitcast.6.tm_ref, f32[2,32,16,512]{3,2,1,0:T(8,128)} %retarded_ref.5, f32[2,32,16,512]{3,2,1,0:T(8,128)} %lesser_ref.5, f32[4,32,16,128]{3,2,1,0:T(8,128)} %collective-permute-done.3.rim_ref), custom_call_target="tpu_custom_call" | custom-call | tf_op jit(solution)/shard_map/pallas_call | solution.py:527
  55.7 2.4 %all-to-all-done.2 = f32[32,8,128]{2,1,0:T(8,128)S(1)} async-done(((f32[32,8,128]{2,1,0:T(8,128)}), f32[32,8,128]{2,1,0:T(8,128)S(1)}, u32[]{:S(2)}, u32[]{:S(2)}) %all-to-all-start.2) | async-done | bytes 131104 | tf_op jit(solution)/shard_map/all_to_all | solution.py:546
  58.1 1.1 shard_map.88
  59.2 0.0 copy-start.8
  59.2 0.7 copy-done.8
  59.9 3.5 %all-to-all-start.3 = ((f32[32,16,128]{2,1,0:T(8,128)}), f32[32,16,128]{2,1,0:T(8,128)S(1)}, u32[]{:S(2)}, u32[]{:S(2)}) async-start(f32[32,16,128]{2,1,0:T(8,128)} %copy-done.8), calls=%async_computation.3 | async-start | bytes 524288 | tf_op jit(solution)/shard_map/all_to_all | solution.py:568
  63.4 5.8 %shard_map.89 = (bf16[8,384,256]{2,1,0:T(8,128)(2,1)}, bf16[8,384,256]{2,1,0:T(8,128)(2,1)}) custom-call(s32[1]{0:T(128)} %bitcast.8.tm_ref, f32[2,32,16,512]{3,2,1,0:T(8,128)} %retarded_ref.5, f32[2,32,16,512]{3,2,1,0:T(8,128)} %lesser_ref.5, f32[4,32,16,128]{3,2,1,0:T(8,128)} %collective-permute-done.3.rim_ref), custom_call_target="tpu_custom_call" | custom-call | tf_op jit(solution)/shard_map/pallas_call | solution.py:527
  69.2 4.4 %all-to-all-done.3 = f32[32,16,128]{2,1,0:T(8,128)S(1)} async-done(((f32[32,16,128]{2,1,0:T(8,128)}), f32[32,16,128]{2,1,0:T(8,128)S(1)}, u32[]{:S(2)}, u32[]{:S(2)}) %all-to-all-start.3) | async-done | bytes 262176 | tf_op jit(solution)/shard_map/all_to_all | solution.py:568
  73.6 0.5 shard_map.90
  74.2 0.0 copy-start.9
  74.2 0.6 copy-done.9
  74.8 2.8 %all-to-all-start.4 = ((f32[32,8,128]{2,1,0:T(8,128)}), f32[32,8,128]{2,1,0:T(8,128)S(1)}, u32[]{:S(2)}, u32[]{:S(2)}) async-start(f32[32,8,128]{2,1,0:T(8,128)} %bitcast.19), calls=%async_computation.4 | async-start | bytes 262144 | tf_op jit(solution)/shard_map/all_to_all | solution.py:546
  77.6 5.8 %shard_map.91 = (bf16[8,384,256]{2,1,0:T(8,128)(2,1)}, bf16[8,384,256]{2,1,0:T(8,128)(2,1)}) custom-call(s32[1]{0:T(128)} %bitcast.tm_ref, f32[2,32,16,512]{3,2,1,0:T(8,128)} %retarded_ref.5, f32[2,32,16,512]{3,2,1,0:T(8,128)} %lesser_ref.5, f32[4,32,16,128]{3,2,1,0:T(8,128)} %collective-permute-done.3.rim_ref), custom_call_target="tpu_custom_call" | custom-call | tf_op jit(solution)/shard_map/pallas_call | solution.py:527
  83.4 2.5 %all-to-all-done.4 = f32[32,8,128]{2,1,0:T(8,128)S(1)} async-done(((f32[32,8,128]{2,1,0:T(8,128)}), f32[32,8,128]{2,1,0:T(8,128)S(1)}, u32[]{:S(2)}, u32[]{:S(2)}) %all-to-all-start.4) | async-done | bytes 131104 | tf_op jit(solution)/shard_map/all_to_all | solution.py:546
  86.0 1.1 shard_map.92
  87.0 13.5 %all_to_all.30 = f32[32,16,128]{2,1,0:T(8,128)S(1)} all-to-all(f32[32,16,128]{2,1,0:T(8,128)S(1)} %shard_map.92), channel_id=1, replica_groups=mesh['mom'=8,'tm'=4] {'mom','tm'}, dimensions={0} | all-to-all | bytes 524288 | tf_op jit(solution)/shard_map/all_to_all | solution.py:568
  100.6 0.6 collective-permute-start.6
  101.2 0.1 collective-permute-start.5
  101.3 4.3 %shard_map.93.others_0_ = f32[2,32,16,512]{3,2,1,0:T(8,128)} custom-call(s32[1]{0:T(128)} %bitcast.3.tm_ref, f32[512,128]{1,0:T(8,128)S(1)} %bitcast.17, f32[2,32,16,16]{3,2,1,0:T(8,128)S(1)} %copy.12.propagator_ref, bf16[8,384,256]{2,1,0:T(8,128)(2,1)} %get-tuple-element.113.high_ref, bf16[8,384,256]{2,1,0:T(8,128)(2,1)} %get-tuple-element.114.low_ref), custom_call_target="tpu_custom_call" | custom-call | tf_op jit(solution)/shard_map/pallas_call | solution.py:583
  105.5 0.0 collective-permute-done.6.arrived_ref
  105.6 2.9 %shard_map.94.others_0_ = f32[2,32,16,512]{3,2,1,0:T(8,128)} custom-call(s32[1]{0:T(128)} %bitcast.6.tm_ref, f32[512,128]{1,0:T(8,128)S(1)} %collective-permute-done.6.arrived_ref, f32[2,32,16,16]{3,2,1,0:T(8,128)S(1)} %copy.12.propagator_ref, bf16[8,384,256]{2,1,0:T(8,128)(2,1)S(1)} %copy-done.2, ...), custom_call_target="tpu_custom_call", output_to_operand_aliasing={{}: (5, {})} | custom-call | tf_op jit(solution)/shard_map/pallas_call | solution.py:583
  108.5 0.6 collective-permute-done.5.arrived_ref
  109.0 0.8 collective-permute-start.7
  109.9 2.9 %shard_map.95.others_0_ = f32[2,32,16,512]{3,2,1,0:T(8,128)} custom-call(s32[1]{0:T(128)} %bitcast.8.tm_ref, f32[512,128]{1,0:T(8,128)S(1)} %collective-permute-done.5.arrived_ref, f32[2,32,16,16]{3,2,1,0:T(8,128)S(1)} %copy.12.propagator_ref, bf16[8,384,256]{2,1,0:T(8,128)(2,1)S(1)} %copy-done.4, ...), custom_call_target="tpu_custom_call", output_to_operand_aliasing={{}: (5, {})} | custom-call | tf_op jit(solution)/shard_map/pallas_call | solution.py:583
  112.8 0.0 collective-permute-done.7.arrived_ref
  112.8 2.9 %shard_map.96 = f32[2,32,16,512]{3,2,1,0:T(8,128)} custom-call(s32[1]{0:T(128)} %bitcast.tm_ref, f32[512,128]{1,0:T(8,128)S(1)} %collective-permute-done.7.arrived_ref, f32[2,32,16,16]{3,2,1,0:T(8,128)S(1)} %copy.12.propagator_ref, bf16[8,384,256]{2,1,0:T(8,128)(2,1)S(1)} %copy-done.6, ...), custom_call_target="tpu_custom_call", output_to_operand_aliasing={{}: (5, {})} | custom-call | tf_op jit(solution)/shard_map/pallas_call | solution.py:583
  (21 shorter events, 0.1 us)
Async XLA Ops:
  1.2 9.5 %copy-start.11 = (f32[256]{0:T(256)S(1)}, f32[256]{0:T(256)}, u32[]{:S(2)}) copy-start(f32[256]{0:T(256)} %param.11) | copy-start | bytes 3076
  1.2 22.0 %copy-start.13 = (f32[8]{0:T(128)S(1)}, f32[8]{0:T(128)}, u32[]{:S(2)}) copy-start(f32[8]{0:T(128)} %param.13) | copy-start | bytes 100
  1.3 22.1 %copy-start.12 = (f32[256]{0:T(256)S(1)}, f32[256]{0:T(256)}, u32[]{:S(2)}) copy-start(f32[256]{0:T(256)} %param.12) | copy-start | bytes 3076
  4.7 25.3 %copy-start = (bf16[512,256]{1,0:T(8,128)(2,1)S(1)}, bf16[512,256]{1,0:T(8,128)(2,1)}, u32[]{:S(2)}) copy-start(bf16[512,256]{1,0:T(8,128)(2,1)} %constant.33.clone.low_ref) | copy-start | bytes 786436
  4.8 25.2 %copy-start.1 = (bf16[512,256]{1,0:T(8,128)(2,1)S(1)}, bf16[512,256]{1,0:T(8,128)(2,1)}, u32[]{:S(2)}) copy-start(bf16[512,256]{1,0:T(8,128)(2,1)} %constant.32.clone.high_ref) | copy-start | bytes 786436
  4.8 4.3 %collective-permute-start = (f32[512,128]{1,0:T(8,128)}, f32[512,128]{1,0:T(8,128)}, u32[]{:S(2)}, u32[]{:S(2)}) collective-permute-start(f32[512,128]{1,0:T(8,128)} %get-tuple-element.64), channel_id=1, source_target_pairs={{3,2},{7,6},{11,10},{15,14},{19,18},{23,22},{27,26},{31,30}} | collective-permute-start | bytes 786440 | tf_op jit(solution)/shard_map/ppermute | solution.py:502
  6.3 20.3 %collective-permute-start.1 = (f32[4,8,16,256]{3,2,1,0:T(8,128)S(1)}, f32[4,8,16,256]{3,2,1,0:T(8,128)}, u32[]{:S(2)}, u32[]{:S(2)}) collective-permute-start(f32[4,8,16,256]{3,2,1,0:T(8,128)S(1)} %get-tuple-element.68), channel_id=1, source_target_pairs={{3,0},{7,4},{11,8},{15,12},{19,16},{23,20},{27,24},{31,28}} | collective-permute-start | bytes 1572872 | tf_op jit(solution)/shard_map/ppermute | solution.py:504
  7.7 18.8 %collective-permute-start.2 = (f32[4,8,16,256]{3,2,1,0:T(8,128)S(1)}, f32[4,8,16,256]{3,2,1,0:T(8,128)}, u32[]{:S(2)}, u32[]{:S(2)}) collective-permute-start(f32[4,8,16,256]{3,2,1,0:T(8,128)S(1)} %get-tuple-element.69), channel_id=1, source_target_pairs={{3,1},{7,5},{11,9},{15,13},{19,17},{23,21},{27,25},{31,29}} | collective-permute-start | bytes 1572872 | tf_op jit(solution)/shard_map/ppermute | solution.py:504
  10.8 19.2 %all-to-all-start = ((f32[32,16,128]{2,1,0:T(8,128)}), f32[32,16,128]{2,1,0:T(8,128)S(1)}, u32[]{:S(2)}, u32[]{:S(2)}) async-start(f32[32,16,128]{2,1,0:T(8,128)} %bitcast.23), calls=%async_computation | async-start | bytes 524288 | tf_op jit(solution)/shard_map/all_to_all | solution.py:546
  19.7 17.2 %collective-permute-start.3 = (f32[4,32,16,128]{3,2,1,0:T(8,128)}, f32[4,32,16,128]{3,2,1,0:T(8,128)}, u32[]{:S(2)}, u32[]{:S(2)}) collective-permute-start(f32[4,32,16,128]{3,2,1,0:T(8,128)} %get-tuple-element.76), channel_id=1, source_target_pairs={{0,1},{1,2},{2,3},{4,5},{5,6},{6,7},{8,9},{9,10},{10,11},{12,13},{... | collective-permute-start | bytes 3145736 | tf_op jit(solution)/shard_map/ppermute | solution.py:25
  23.5 11.1 %collective-permute-start.4 = (f32[4,8,16,256]{3,2,1,0:T(8,128)S(1)}, f32[4,8,16,256]{3,2,1,0:T(8,128)}, u32[]{:S(2)}, u32[]{:S(2)}) collective-permute-start(f32[4,8,16,256]{3,2,1,0:T(8,128)S(1)} %get-tuple-element.77), channel_id=1, source_target_pairs={{3,2},{7,6},{11,10},{15,14},{19,18},{23,22},{27,26},{31,30}} | collective-permute-start | bytes 1572872 | tf_op jit(solution)/shard_map/ppermute | solution.py:509
  31.8 13.2 %all-to-all-start.1 = ((f32[32,16,128]{2,1,0:T(8,128)}), f32[32,16,128]{2,1,0:T(8,128)S(1)}, u32[]{:S(2)}, u32[]{:S(2)}) async-start(f32[32,16,128]{2,1,0:T(8,128)} %shard_map.83), calls=%async_computation.1 | async-start | bytes 524288 | tf_op jit(solution)/shard_map/all_to_all | solution.py:568
  45.5 0.7 copy-start.10
  46.2 11.9 %all-to-all-start.2 = ((f32[32,8,128]{2,1,0:T(8,128)}), f32[32,8,128]{2,1,0:T(8,128)S(1)}, u32[]{:S(2)}, u32[]{:S(2)}) async-start(f32[32,8,128]{2,1,0:T(8,128)} %bitcast.20), calls=%async_computation.2 | async-start | bytes 262144 | tf_op jit(solution)/shard_map/all_to_all | solution.py:546
  59.2 0.7 copy-start.8
  59.9 13.7 %all-to-all-start.3 = ((f32[32,16,128]{2,1,0:T(8,128)}), f32[32,16,128]{2,1,0:T(8,128)S(1)}, u32[]{:S(2)}, u32[]{:S(2)}) async-start(f32[32,16,128]{2,1,0:T(8,128)} %copy-done.8), calls=%async_computation.3 | async-start | bytes 524288 | tf_op jit(solution)/shard_map/all_to_all | solution.py:568
  74.2 0.7 copy-start.9
  74.8 11.1 %all-to-all-start.4 = ((f32[32,8,128]{2,1,0:T(8,128)}), f32[32,8,128]{2,1,0:T(8,128)S(1)}, u32[]{:S(2)}, u32[]{:S(2)}) async-start(f32[32,8,128]{2,1,0:T(8,128)} %bitcast.19), calls=%async_computation.4 | async-start | bytes 262144 | tf_op jit(solution)/shard_map/all_to_all | solution.py:546
  100.6 5.0 %copy-start.2 = (bf16[8,384,256]{2,1,0:T(8,128)(2,1)S(1)}, bf16[8,384,256]{2,1,0:T(8,128)(2,1)}, u32[]{:S(2)}) copy-start(bf16[8,384,256]{2,1,0:T(8,128)(2,1)} %get-tuple-element.111.high_ref) | copy-start | bytes 4718596
  100.6 5.0 %copy-start.3 = (bf16[8,384,256]{2,1,0:T(8,128)(2,1)S(1)}, bf16[8,384,256]{2,1,0:T(8,128)(2,1)}, u32[]{:S(2)}) copy-start(bf16[8,384,256]{2,1,0:T(8,128)(2,1)} %get-tuple-element.112.low_ref) | copy-start | bytes 4718596
  100.6 5.0 %collective-permute-start.6 = (f32[512,128]{1,0:T(8,128)S(1)}, f32[512,128]{1,0:T(8,128)S(1)}, u32[]{:S(2)}, u32[]{:S(2)}) collective-permute-start(f32[512,128]{1,0:T(8,128)S(1)} %bitcast.15), channel_id=1, source_target_pairs={{0,1},{1,0},{2,3},{3,2},{4,5},{5,4},{6,7},{7,6},{8,9},{9,8},{10,11... | collective-permute-start | bytes 786440 | tf_op jit(solution)/shard_map/ppermute | solution.py:606
  101.2 7.9 %collective-permute-start.5 = (f32[512,128]{1,0:T(8,128)S(1)}, f32[512,128]{1,0:T(8,128)S(1)}, u32[]{:S(2)}, u32[]{:S(2)}) collective-permute-start(f32[512,128]{1,0:T(8,128)S(1)} %bitcast.16), channel_id=1, source_target_pairs={{0,2},{1,3},{2,0},{3,1},{4,6},{5,7},{6,4},{7,5},{8,10},{9,11},{10,... | collective-permute-start | bytes 786440 | tf_op jit(solution)/shard_map/ppermute | solution.py:606
  105.5 4.4 %copy-start.4 = (bf16[8,384,256]{2,1,0:T(8,128)(2,1)S(1)}, bf16[8,384,256]{2,1,0:T(8,128)(2,1)}, u32[]{:S(2)}) copy-start(bf16[8,384,256]{2,1,0:T(8,128)(2,1)} %get-tuple-element.118.high_ref) | copy-start | bytes 4718596
  105.5 4.4 %copy-start.5 = (bf16[8,384,256]{2,1,0:T(8,128)(2,1)S(1)}, bf16[8,384,256]{2,1,0:T(8,128)(2,1)}, u32[]{:S(2)}) copy-start(bf16[8,384,256]{2,1,0:T(8,128)(2,1)} %get-tuple-element.119.low_ref) | copy-start | bytes 4718596
  108.4 4.3 %copy-start.6 = (bf16[8,384,256]{2,1,0:T(8,128)(2,1)S(1)}, bf16[8,384,256]{2,1,0:T(8,128)(2,1)}, u32[]{:S(2)}) copy-start(bf16[8,384,256]{2,1,0:T(8,128)(2,1)} %get-tuple-element.116.high_ref) | copy-start | bytes 4718596
  108.5 4.3 %copy-start.7 = (bf16[8,384,256]{2,1,0:T(8,128)(2,1)S(1)}, bf16[8,384,256]{2,1,0:T(8,128)(2,1)}, u32[]{:S(2)}) copy-start(bf16[8,384,256]{2,1,0:T(8,128)(2,1)} %get-tuple-element.117.low_ref) | copy-start | bytes 4718596
  109.0 3.7 %collective-permute-start.7 = (f32[512,128]{1,0:T(8,128)S(1)}, f32[512,128]{1,0:T(8,128)S(1)}, u32[]{:S(2)}, u32[]{:S(2)}) collective-permute-start(f32[512,128]{1,0:T(8,128)S(1)} %collective-permute-done.5.arrived_ref), channel_id=1, source_target_pairs={{0,1},{1,0},{2,3},{3,2},{4,5},{5,4},{6,7},{7,6},{8,9},{9,8},{10,11... | collective-permute-start | bytes 786440 | tf_op jit(solution)/shard_map/ppermute | solution.py:606

commit v4 on v2

--- a/solution.py
+++ b/solution.py
@@ -218,9 +218,28 @@
         copy.wait()
 
 
-def first_window_kernel(
-    own, propagator_ref, retarded_ref, lesser_ref, low_ref, high_ref, near0_ref, near1_ref, window_ref, arrive, pass_on
-):
+def region_copies(retarded_ref, lesser_ref, near_refs, momenta, own, semaphores):
+    copies = []
+    for kind, ref in enumerate((retarded_ref, lesser_ref)):
+        both = pl.ds(2 * kind, 2)
+        last = ref.shape[3]
+        for number, (tm, near_ref) in enumerate(zip(momenta, near_refs)):
+            source = ref.at[:, tm * own : (tm + 1) * own, :, last - 2 * TILE :]
+            copies.append(pltpu.make_async_copy(source, near_ref.at[both], semaphores.at[kind, number]))
+    return copies
+
+
+def regions_kernel(own, momenta, retarded_ref, lesser_ref, *others):
+    *near_refs, rim_ref, passing = others
+    copies = region_copies(retarded_ref, lesser_ref, near_refs, momenta, own, passing)
+    for kind, ref in enumerate((retarded_ref, lesser_ref)):
+        source = ref.at[:, :, :, ref.shape[3] - TILE :]
+        copies.append(pltpu.make_async_copy(source, rim_ref.at[pl.ds(2 * kind, 2)], passing.at[kind, len(near_refs)]))
+    wait_all(start_all(copies))
+
+
+def first_window_kernel(own, propagator_ref, retarded_ref, lesser_ref, low_ref, high_ref, *others):
+    *near_refs, window_ref, arrive, pass_on = others
     momenta, columns = lesser_ref.shape[1], lesser_ref.shape[3]
     half = momenta // 2
     fetches = start_all(
@@ -233,17 +252,7 @@
             for number, first in enumerate(range(0, momenta, own))
         ]
     )
-    copies = start_all(
-        [
-            pltpu.make_async_copy(
-                ref.at[:, tm * own : (tm + 1) * own, :, columns - 2 * TILE :],
-                near_ref.at[2 * kind : 2 * kind + 2],
-                pass_on.at[tm, kind],
-            )
-            for tm, near_ref in enumerate((near0_ref, near1_ref))
-            for kind, ref in enumerate((retarded_ref, lesser_ref))
-        ]
-    )
+    copies = start_all(region_copies(retarded_ref, lesser_ref, near_refs, (0, 1), own, pass_on))
     for number, fetch in enumerate(fetches):
         fetch.wait()
         for k in range(number * own, (number + 1) * own):
@@ -347,9 +356,13 @@
     return tiles
 
 
-def final_ladder_kernel(tm_ref, retarded_ref, lesser_ref, rim_ref, high_out, low_out, region_ref, high_ref, low_ref, arrive, leave):
-    own = high_ref.shape[0]
-    momenta = pl.ds(tm_ref[0] * own, own)
+def final_ladder_kernel(tm_ref, retarded_ref, lesser_ref, rim_ref, *others):
+    *outs, region_ref, ladder_ref, arrive, leave = others
+    count, rows_each = ladder_ref.shape[0], ladder_ref.shape[1] // 2
+    high_ref = ladder_ref.at[:, :rows_each]
+    low_ref = ladder_ref.at[:, rows_each:]
+    own = count // 2
+    momenta = pl.ds(tm_ref[0] // 2 * count, count)
     fetches = []
     for kind, ref in enumerate((retarded_ref, lesser_ref)):
         both = pl.ds(2 * kind, 2)
@@ -365,35 +378,37 @@
         )
     wait_all(fetches)
 
-    def leaving(k):
-        return [
-            pltpu.make_async_copy(ref.at[k], out.at[k], leave.at[k, which])
-            for which, (ref, out) in enumerate(((high_ref, high_out), (low_ref, low_out)))
-        ]
-
-    def one(k, carry):
+    def leaving(block, n):
+        k = block * own + n
+        return [pltpu.make_async_copy(ladder_ref.at[k], outs[block].at[n], leave.at[k])]
+
+    def one(block, n, carry):
+        k = block * own + n
+        source = (tm_ref[0] % 2 ^ block) * own + n
         for part in range(2):
-            region = jnp.concatenate([region_ref[2 * kind + part, k] for kind in range(2)], axis=0)
+            region = jnp.concatenate([region_ref[2 * kind + part, source] for kind in range(2)], axis=0)
             lanes = pl.ds(part * TILE, TILE)
-            for turn in range(3):
-                from_lane = turn * 4 * ORB
-                tiles = trade([region[:, from_lane + t * TILE : from_lane + (t + 1) * TILE] for t in range(4)])
-                for step in range(4 * turn - 1, 4 * turn + 3):
-                    if step >= 0:
-                        high, low = halves(tiles[step - 4 * turn + 1])
-                        for kind in range(2):
-                            rows = pl.ds(step // 4 * TILE + kind * HALF + step % 4 * ORB, ORB)
-                            high_ref[k, rows, lanes] = high[kind * ORB : (kind + 1) * ORB]
-                            low_ref[k, rows, lanes] = low[kind * ORB : (kind + 1) * ORB]
+            tiles = [region[:, t * TILE : (t + 1) * TILE] for t in range(5)]
+            first, third = trade(tiles[:4]), trade(tiles[1:])
+            lower = lower_lanes(tiles[0].shape)
+            second = [pltpu.roll(jnp.where(lower, z, x), HALF, 1) for x, z in zip(first, third)]
+            for step, tile in enumerate((first + second + third)[1:]):
+                high, low = halves(tile)
+                for kind in range(2):
+                    rows = pl.ds(step // 4 * TILE + kind * HALF + step % 4 * ORB, ORB)
+                    high_ref[k, rows, lanes] = high[kind * ORB : (kind + 1) * ORB]
+                    low_ref[k, rows, lanes] = low[kind * ORB : (kind + 1) * ORB]
             for kind in range(2):
                 rows = pl.ds(2 * TILE + kind * HALF + 3 * ORB, ORB)
                 high_ref[k, rows, lanes] = jnp.zeros((ORB, TILE), jnp.bfloat16)
                 low_ref[k, rows, lanes] = jnp.zeros((ORB, TILE), jnp.bfloat16)
-        start_all(leaving(k))
+        start_all(leaving(block, n))
         return carry
 
-    lax.fori_loop(0, own, one, 0)
-    lax.fori_loop(0, own, lambda k, c: (wait_all(leaving(k)), c)[1], 0)
+    for block in range(2):
+        lax.fori_loop(0, own, functools.partial(one, block), 0)
+    for block in range(2):
+        lax.fori_loop(0, own, lambda n, c: (wait_all(leaving(block, n)), c)[1], 0)
 
 
 def stepped(pair):
@@ -416,27 +431,20 @@
     return jnp.concatenate(rows, axis=0)
 
 
-def final_kernel(own, before, tm_ref, arrived_ref, propagator_ref, high_ref, low_ref, *others):
-    out_ref, high_here, low_here, out_here, arrive, leave = others[before:]
+def final_kernel(own, before, tm_ref, arrived_ref, propagator_ref, ladder_ref, *others):
+    out_ref, ladder_here, out_here, arrive, leave = others[before:]
     base = tm_ref[0] * own
-
     group = own // 2
+    rows_each = ladder_here.shape[1] // 2
 
     def arriving(number):
         momenta = pl.ds(number * group, group)
-        return [
-            pltpu.make_async_copy(ref.at[momenta], here.at[momenta], arrive.at[number, which])
-            for which, (ref, here) in enumerate(((high_ref, high_here), (low_ref, low_here)))
-        ]
+        return [pltpu.make_async_copy(ladder_ref.at[momenta], ladder_here.at[momenta], arrive.at[number])]
 
     def leaving(number):
-        return [
-            pltpu.make_async_copy(
-                out_here.at[:, pl.ds(number * group, group)],
-                out_ref.at[:, pl.ds(base + number * group, group)],
-                leave.at[number],
-            )
-        ]
+        momenta = pl.ds(number * group, group)
+        source, target = out_here.at[:, momenta], out_ref.at[:, pl.ds(base + number * group, group)]
+        return [pltpu.make_async_copy(source, target, leave.at[number])]
 
     def one(number, carry):
         wait_all(arriving(number))
@@ -444,7 +452,8 @@
             k = number * group + n
             pieces = coefficients(arrived_ref, propagator_ref.at[:, base + k], k, own)
             left_high, left_low = halves(jnp.concatenate([stepped(pair) for pair in pieces], axis=0))
-            parts = contract(left_high, left_low, high_here[k], low_here[k], TILE)
+            right = ladder_here.at[k]
+            parts = contract(left_high, left_low, right[:rows_each], right[rows_each:], TILE)
             for part, value in enumerate(parts):
                 tiles = trade([value[s * ORB : (s + 1) * ORB] for s in range(4)])
                 for t, tile in enumerate(tiles):
@@ -452,10 +461,11 @@
         start_all(leaving(number))
         return carry
 
-    for number in range(own // group):
+    groups = own // group
+    for number in range(groups):
         start_all(arriving(number))
-    lax.fori_loop(0, own // group, one, 0)
-    for number in range(own // group):
+    lax.fori_loop(0, groups, one, 0)
+    for number in range(groups):
         wait_all(leaving(number))
 
 
@@ -494,7 +504,7 @@
         out_specs=(VMEM,) * 4,
         scratch_shapes=[
             pltpu.VMEM((2, momenta_here, ORB, TILE), jnp.float32),
-            pltpu.SemaphoreType.DMA((momenta_here // own,)),
+            pltpu.SemaphoreType.DMA((peers,)),
             pltpu.SemaphoreType.DMA((2, 2)),
         ],
         compiler_params=limit(8),
@@ -507,15 +517,16 @@
     send, hist_lesser, hist_retarded, coupling, mf_weight, lag_weight = lax.optimization_barrier(
         (send, hist_lesser, hist_retarded, coupling, mf_weight, lag_weight)
     )
-
-    def near_of(tm):
-        momenta = slice(tm * own, (tm + 1) * own)
-        return jnp.concatenate([x[:, momenta, :, columns - 2 * TILE :] for x in (hist_retarded, hist_lesser)], axis=0)
-
-    near.append(lax.ppermute(near_of(2), "tm", [(3, 2)]))
-    rim = jnp.concatenate([x[..., columns - TILE :] for x in (hist_retarded, hist_lesser)], axis=0)
+    two, mine, rim = pl.pallas_call(
+        functools.partial(regions_kernel, own, (2, 3)),
+        out_shape=(near_shape, near_shape, f32((4, momenta_here, ORB, TILE))),
+        in_specs=[IN_HBM, IN_HBM],
+        out_specs=(VMEM,) * 3,
+        scratch_shapes=[pltpu.SemaphoreType.DMA((2, 3))],
+        compiler_params=limit(4),
+    )(*(pltpu.with_memory_space_constraint(x, pltpu.HBM) for x in (hist_retarded, hist_lesser)))
+    near.append(lax.ppermute(two, "tm", [(3, 2)]))
     rim = shifted(rim, "tm", 1)
-
     me = lax.axis_index("mom") * peers + lax.axis_index("tm")
     last_mark = (jnp.arange(W) == W - 1).astype(jnp.float32)
     strong = (coupling * coupling).reshape(ORB, 1, ORB) * lag_weight[:, None]
@@ -527,35 +538,33 @@
     table_high, table_low = fourier_tables()
 
     ladders = []
-    ladder_shape = (own, 3 * TILE, 2 * TILE)
-
-    def beside(arrived, sent):
-        _, retarded, lesser, edge = lax.optimization_barrier((sent, hist_retarded, hist_lesser, rim))
+    ladder_shape = (own, 2 * 3 * TILE, 2 * TILE)
+
+    def send_beside(sent):
+        sent, retarded, lesser, edge = lax.optimization_barrier((sent, hist_retarded, hist_lesser, rim))
+        arrived = lax.all_to_all(sent, both_axes, 0, 0, tiled=True)
         momenta = (here ^ len(ladders)).reshape(1).astype(jnp.int32)
         ladder = pl.pallas_call(
             final_ladder_kernel,
             out_shape=(pltpu.HBM(ladder_shape, jnp.bfloat16),) * 2,
             in_specs=[SMEM, IN_HBM, IN_HBM, IN_HBM],
-            out_specs=(IN_HBM, IN_HBM),
+            out_specs=(IN_HBM,) * 2,
             scratch_shapes=[
-                pltpu.VMEM((4, own, ORB, TILE + columns), jnp.float32),
-                pltpu.VMEM(ladder_shape, jnp.bfloat16),
-                pltpu.VMEM(ladder_shape, jnp.bfloat16),
+                pltpu.VMEM((4, 2 * own, ORB, TILE + columns), jnp.float32),
+                pltpu.VMEM((2 * own, *ladder_shape[1:]), jnp.bfloat16),
                 pltpu.SemaphoreType.DMA((2, 2)),
-                pltpu.SemaphoreType.DMA((own, 2)),
+                pltpu.SemaphoreType.DMA((2 * own,)),
             ],
-            compiler_params=limit(6),
+            compiler_params=limit(12),
         )(momenta, *(pltpu.with_memory_space_constraint(x, pltpu.HBM) for x in (retarded, lesser, edge)))
         arrived, *ladder = lax.optimization_barrier((arrived, *ladder))
-        ladders.append(ladder)
+        ladders.extend(ladder)
         return arrived
 
     for sweep in range(PASSES):
         arrived = lax.all_to_all(send, both_axes, 0, 0, tiled=True)
         if sweep == 0:
             arrived, *near[:2] = lax.optimization_barrier((arrived, *near[:2]))
-        else:
-            arrived = beside(arrived, send)
         back = call(
             fourier_kernel,
             f32((devices, 2 * own, TILE)),
@@ -567,16 +576,13 @@
         )
         if sweep == 0:
             near[2], _ = lax.optimization_barrier((near[2], back))
-            mine = near_of(peers - 1)
             for tm, received in enumerate(near):
                 mine = jnp.where(here == tm, received, mine)
             rungs = bf16((own, 2 * TILE, 2 * TILE))
             rungs = call(functools.partial(window_ladder_kernel, own), (rungs, rungs), mine)
             rim, *rungs = lax.optimization_barrier((rim, *rungs))
             propagator_own = own_block(propagator, own, 1)
-        arrived = lax.all_to_all(back, both_axes, 0, 0, tiled=True)
-        if sweep:
-            arrived = beside(arrived, back)
+        arrived = send_beside(back) if sweep else lax.all_to_all(back, both_axes, 0, 0, tiled=True)
         arrived = arrived.reshape(2 * count, TILE)
         if sweep + 1 < PASSES:
             send = call(
@@ -592,22 +598,21 @@
         return pl.pallas_call(
             functools.partial(final_kernel, own, len(before)),
             out_shape=pltpu.HBM(hist_lesser.shape, jnp.float32),
-            in_specs=[SMEM, VMEM, VMEM] + [IN_HBM] * (2 + len(before)),
+            in_specs=[SMEM, VMEM, VMEM] + [IN_HBM] * (1 + len(before)),
             out_specs=IN_HBM,
             scratch_shapes=[
                 pltpu.VMEM(ladder_shape, jnp.bfloat16),
-                pltpu.VMEM(ladder_shape, jnp.bfloat16),
                 pltpu.VMEM((2, own, ORB, columns), jnp.float32),
-                pltpu.SemaphoreType.DMA((own, 2)),
+                pltpu.SemaphoreType.DMA((own,)),
                 pltpu.SemaphoreType.DMA((own,)),
             ],
-            input_output_aliases={5: 0} if before else {},
+            input_output_aliases={4: 0} if before else {},
             compiler_params=limit(6),
         )(
             (here ^ step).reshape(1).astype(jnp.int32),
             coefficients_of,
             propagator,
-            *[pltpu.with_memory_space_constraint(x, pltpu.HBM) for x in ladders[step]],
+            pltpu.with_memory_space_constraint(ladders[step], pltpu.HBM) if step < 3 else ladders[step],
             *before,
         )
 

time: 120 us -> 112 us (0.933)
  blocking collectives: 0 us -> 21.6 us
  waiting for transfers between devices: 24.6 us -> 16.1 us
  starting transfers between devices: 35.4 us -> 27.9 us
  Pallas kernels: 48.2 us -> 41.2 us
  local copies, waits for them, and re-layouts: 6.59 us -> 2.31 us
  other arithmetic: 4.14 us -> 2.23 us
    all_to_all x0 -> x2, blocking collectives: none -> 21.6 us  [on_device_tiled(): arrived = lax.all_to_all(send, both_axes, 0, 0, tiled=True)]
    all_to_all x3 -> x1, waiting for transfers between devices: 7.76 us -> 1.88 us  [on_device_tiled(): arrived = lax.all_to_all(send, both_axes, 0, 0, tiled=True)]
    pallas_call x4 -> x3, Pallas kernels: 23.2 us -> 17.3 us  [the longest x2 14.5 us: send_beside(): pl.pallas_call(final_ladder_kernel, out_shape=(pltpu.HBM(ladder_shape, jn...]
    all_to_all x3 -> x1, starting transfers between devices: 15.4 us -> 9.88 us  [on_device_tiled(): arrived = lax.all_to_all(send, both_axes, 0, 0, tiled=True)]
    all_to_all x3, waiting for transfers between devices: 15.6 us -> 12.5 us  [the longest x2 6.26 us: send_beside(): arrived = lax.all_to_all(sent, both_axes, 0, 0, tiled=True)]
    unnamed x27 -> x17, local copies, waits for them, and re-layouts: 4.18 us -> 1.96 us
    slice x5 -> x0, local copies, waits for them, and re-layouts: 2.06 us -> none  [the longest x1 2.05 us: near_of(): x[:, momenta, :, columns - 2 * TILE:]]
    concatenate x2 -> x0, other arithmetic: 1.89 us -> none  [the longest x1 1.04 us: on_device_tiled(): jnp.concatenate([x[..., columns - TILE:] for x in (hist_retarded, hist_le...]
  transfers between devices with their start and end apart: 14 -> 12, of which waited for: 7 -> 5; matrix products, arithmetic and copies ran while one was open for 5% -> 2% of each run, Pallas kernels for 32% -> 29%
where the time goes in v4:
time: 112 us
  Pallas kernels  41.2 us (37%)
  starting transfers between devices  27.9 us (25%)
  blocking collectives  21.6 us (19%)
  waiting for transfers between devices  16.1 us (14%)
  local copies, waits for them, and re-layouts  2.31 us (2%)
  other arithmetic  2.23 us (2%)
    all_to_all x2, blocking collectives, on_device_tiled(): arrived = lax.all_to_all(send, both_axes, 0, 0, tiled=True)  21.6 us
    pallas_call x4, Pallas kernels, finish(): pl.pallas_call(functools.partial(final_kernel, own, len(before)), out_sha...  14.8 us
    pallas_call x2, Pallas kernels, send_beside(): pl.pallas_call(final_ladder_kernel, out_shape=(pltpu.HBM(ladder_shape, jn...  14.5 us
    all_to_all x1, starting transfers between devices, on_device_tiled(): arrived = lax.all_to_all(send, both_axes, 0, 0, tiled=True)  9.88 us
    pallas_call x6, Pallas kernels, call(): pl.pallas_call(kernel, out_shape=shapes, in_specs=[VMEM] * len(operands),...  6.7 us
    all_to_all x2, waiting for transfers between devices, send_beside(): arrived = lax.all_to_all(sent, both_axes, 0, 0, tiled=True)  6.26 us
    all_to_all x1, waiting for transfers between devices, on_device_tiled(): lax.all_to_all(back, both_axes, 0, 0, tiled=True)  6.2 us
    all_to_all x2, starting transfers between devices, send_beside(): arrived = lax.all_to_all(sent, both_axes, 0, 0, tiled=True)  4.96 us
  transfers between devices with their start and end apart: 12, of which 5 were waited for; matrix products, arithmetic and copies ran while one was open for 2% of the time, Pallas kernels for 29%

profile of v4, /device:TPU:1, one launch (start us, length us, event | category | flops | bytes accessed | tf_op | source)
XLA Modules:
  0.0 111.6 jit_solution(17649202352675849923)
XLA Ops:
  0.0 1.2 %copy.12.propagator_ref = f32[2,32,16,16]{3,2,1,0:T(8,128)S(1)} copy(f32[2,32,16,16]{1,3,2,0:T(8,128)} %param.10) | data formatting | bytes 131072 | tf_op args[2]
  1.2 0.0 copy-start.5
  1.2 2.4 %shard_map.82 = (f32[512,128]{1,0:T(8,128)S(1)}, f32[512,128]{1,0:T(8,128)S(1)}, f32[4,8,16,256]{3,2,1,0:T(8,128)S(1)}, f32[4,8,16,256]{3,2,1,0:T(8,128)S(1)}) custom-call(f32[2,32,16,16]{3,2,1,0:T(8,128)S(1)} %copy.12.propagator_ref, f32[2,32,16,512]{3,2,1,0:T(8,128)} %retarded_ref.4, f32[2,32,16,512]{3,2,1,0:T(8,128)} %lesser_ref.4), custom_call_target="tpu_custom_call" | custom-call | tf_op jit(solution)/shard_map/pallas_call | solution.py:500
  3.6 0.7 collective-permute-start
  4.3 0.7 collective-permute-start.1
  5.0 1.3 %collective-permute-start.2 = (f32[4,8,16,256]{3,2,1,0:T(8,128)S(1)}, f32[4,8,16,256]{3,2,1,0:T(8,128)}, u32[]{:S(2)}, u32[]{:S(2)}) collective-permute-start(f32[4,8,16,256]{3,2,1,0:T(8,128)S(1)} %get-tuple-element.51), channel_id=1, source_target_pairs={{3,1},{7,5},{11,9},{15,13},{19,17},{23,21},{27,25},{31,29}} | collective-permute-start | bytes 1572872 | tf_op jit(solution)/shard_map/ppermute | solution.py:515
  6.3 0.0 collective-permute-done
  6.3 0.7 broadcast_select_fusion
  7.0 0.0 copy-done.5
  7.0 0.1 mul.51
  7.1 9.9 %all-to-all-start = ((f32[32,16,128]{2,1,0:T(8,128)}), f32[32,16,128]{2,1,0:T(8,128)S(1)}, u32[]{:S(2)}, u32[]{:S(2)}) async-start(f32[32,16,128]{2,1,0:T(8,128)} %bitcast.1), calls=%async_computation | async-start | bytes 524288 | tf_op jit(solution)/shard_map/all_to_all | solution.py:565
  17.0 0.0 copy-start.7
  17.0 0.0 copy-start.6
  17.0 0.0 copy-start.1
  17.1 0.0 copy-start.2
  17.1 2.8 %shard_map.84 = (f32[4,8,16,256]{3,2,1,0:T(8,128)}, f32[4,8,16,256]{3,2,1,0:T(8,128)S(1)}, f32[4,32,16,128]{3,2,1,0:T(8,128)}) custom-call(f32[2,32,16,512]{3,2,1,0:T(8,128)} %retarded_ref.4, f32[2,32,16,512]{3,2,1,0:T(8,128)} %lesser_ref.4), custom_call_target="tpu_custom_call" | custom-call | tf_op jit(solution)/shard_map/pallas_call | solution.py:520
  19.9 3.5 %collective-permute-start.3 = (f32[4,32,16,128]{3,2,1,0:T(8,128)}, f32[4,32,16,128]{3,2,1,0:T(8,128)}, u32[]{:S(2)}, u32[]{:S(2)}) collective-permute-start(f32[4,32,16,128]{3,2,1,0:T(8,128)} %get-tuple-element.58), channel_id=1, source_target_pairs={{0,1},{1,2},{2,3},{4,5},{5,6},{6,7},{8,9},{9,10},{10,11},{12,13},{... | collective-permute-start | bytes 3145736 | tf_op jit(solution)/shard_map/ppermute | solution.py:25
  23.4 0.0 copy-done.7
  23.4 0.1 broadcast_multiply_fusion.1
  23.5 0.0 copy-done.6
  23.5 0.1 mul.57
  23.6 1.5 %collective-permute-start.4 = (f32[4,8,16,256]{3,2,1,0:T(8,128)}, f32[4,8,16,256]{3,2,1,0:T(8,128)}, u32[]{:S(2)}, u32[]{:S(2)}) collective-permute-start(f32[4,8,16,256]{3,2,1,0:T(8,128)} %get-tuple-element.59), channel_id=1, source_target_pairs={{3,2},{7,6},{11,10},{15,14},{19,18},{23,22},{27,26},{31,30}} | collective-permute-start | bytes 1572872 | tf_op jit(solution)/shard_map/ppermute | solution.py:528
  25.0 0.1 broadcast_multiply_fusion
  25.1 0.1 mul.55
  25.2 0.1 mul.62
  25.3 0.1 pad_maximum_fusion.strength_ref
  25.4 0.0 collective-permute-done.1
  25.4 0.0 collective-permute-done.2
  25.4 1.9 %all-to-all-done = f32[32,16,128]{2,1,0:T(8,128)S(1)} async-done(((f32[32,16,128]{2,1,0:T(8,128)}), f32[32,16,128]{2,1,0:T(8,128)S(1)}, u32[]{:S(2)}, u32[]{:S(2)}) %all-to-all-start) | async-done | bytes 262176 | tf_op jit(solution)/shard_map/all_to_all | solution.py:565
  27.3 0.0 copy-done.1
  27.3 0.0 copy-done.2
  27.3 1.8 %shard_map.83 = f32[32,16,128]{2,1,0:T(8,128)} custom-call(f32[8,4,16,128]{3,2,1,0:T(8,128)S(1)} %bitcast.13, bf16[512,256]{1,0:T(8,128)(2,1)S(1)} %copy-done.1, bf16[512,256]{1,0:T(8,128)(2,1)S(1)} %copy-done.2, f32[1,128]{1,0:T(1,128)S(1)} %pad_maximum_fusion.strength_ref, f32[1,128]{1,0:T(1,128)S(1)} %concatenate.7.mean_ref), custom_call_target="tpu_custom_call" | custom-call | tf_op jit(solution)/shard_map/pallas_call | solution.py:489
  29.0 0.0 copy-done.4
  29.0 3.9 %all-to-all-start.1 = ((f32[32,16,128]{2,1,0:T(8,128)}), f32[32,16,128]{2,1,0:T(8,128)S(1)}, u32[]{:S(2)}, u32[]{:S(2)}) async-start(f32[32,16,128]{2,1,0:T(8,128)} %shard_map.83), calls=%async_computation.1 | async-start | bytes 524288 | tf_op jit(solution)/shard_map/all_to_all | solution.py:585
  32.9 0.0 collective-permute-done.4
  33.0 1.3 %select_select_fusion.near_ref = f32[4,8,16,256]{3,2,1,0:T(8,128)S(1)} fusion(f32[4,8,16,256]{3,2,1,0:T(8,128)} %collective-permute-done.4, f32[4,8,16,256]{3,2,1,0:T(8,128)} %collective-permute-done.2, f32[4,8,16,256]{3,2,1,0:T(8,128)} %copy-done.4, f32[4,8,16,256]{3,2,1,0:T(8,128)S(1)} %get-tuple-element.63, pred[]{:T(512)S(6)} %eq.19, pred[]{:T(512)S(6)} %eq.18, ...), kind=kLoop, calls=%fused_computation | loop fusion | flops 393216 | bytes 2621443 | tf_op jit(solution)/shard_map/jit(_where)/select_n | solution.py:580
  34.2 1.0 shard_map.85
  35.2 1.7 %collective-permute-done.3.rim_ref = f32[4,32,16,128]{3,2,1,0:T(8,128)} collective-permute-done((f32[4,32,16,128]{3,2,1,0:T(8,128)}, f32[4,32,16,128]{3,2,1,0:T(8,128)}, u32[]{:S(2)}, u32[]{:S(2)}) %collective-permute-start.3) | collective-permute-done | bytes 1048608 | tf_op jit(solution)/shard_map/ppermute | solution.py:25
  37.0 6.2 %all-to-all-done.1 = f32[32,16,128]{2,1,0:T(8,128)S(1)} async-done(((f32[32,16,128]{2,1,0:T(8,128)}), f32[32,16,128]{2,1,0:T(8,128)S(1)}, u32[]{:S(2)}, u32[]{:S(2)}) %all-to-all-start.1) | async-done | bytes 262176 | tf_op jit(solution)/shard_map/all_to_all | solution.py:585
  43.2 0.5 shard_map.86
  43.7 10.7 %all_to_all.30 = f32[32,8,128]{2,1,0:T(8,128)S(1)} all-to-all(f32[32,8,128]{2,1,0:T(8,128)S(1)} %bitcast.20), channel_id=1, replica_groups=mesh['mom'=8,'tm'=4] {'mom','tm'}, dimensions={0} | all-to-all | bytes 262144 | tf_op jit(solution)/shard_map/all_to_all | solution.py:565
  54.5 1.1 shard_map.87
  55.5 0.0 copy-start.3
  55.6 0.7 copy-done.3
  56.2 2.5 %all-to-all-start.3 = ((f32[32,16,128]{2,1,0:T(8,128)}), f32[32,16,128]{2,1,0:T(8,128)S(1)}, u32[]{:S(2)}, u32[]{:S(2)}) async-start(f32[32,16,128]{2,1,0:T(8,128)} %copy-done.3), calls=%async_computation.3 | async-start | bytes 524288 | tf_op jit(solution)/shard_map/all_to_all | solution.py:545
  58.7 7.3 %shard_map.88 = (bf16[8,768,256]{2,1,0:T(8,128)(2,1)}, bf16[8,768,256]{2,1,0:T(8,128)(2,1)}) custom-call(s32[1]{0:T(128)} %bitcast.6.tm_ref, f32[2,32,16,512]{3,2,1,0:T(8,128)} %retarded_ref.4, f32[2,32,16,512]{3,2,1,0:T(8,128)} %lesser_ref.4, f32[4,32,16,128]{3,2,1,0:T(8,128)} %collective-permute-done.3.rim_ref), custom_call_target="tpu_custom_call" | custom-call | tf_op jit(solution)/shard_map/pallas_call | solution.py:547
  66.0 3.1 %all-to-all-done.3 = f32[32,16,128]{2,1,0:T(8,128)S(1)} async-done(((f32[32,16,128]{2,1,0:T(8,128)}), f32[32,16,128]{2,1,0:T(8,128)S(1)}, u32[]{:S(2)}, u32[]{:S(2)}) %all-to-all-start.3) | async-done | bytes 262176 | tf_op jit(solution)/shard_map/all_to_all | solution.py:545
  69.1 0.5 shard_map.89
  69.7 10.9 %all_to_all.31 = f32[32,8,128]{2,1,0:T(8,128)S(1)} all-to-all(f32[32,8,128]{2,1,0:T(8,128)S(1)} %bitcast.19), channel_id=1, replica_groups=mesh['mom'=8,'tm'=4] {'mom','tm'}, dimensions={0} | all-to-all | bytes 262144 | tf_op jit(solution)/shard_map/all_to_all | solution.py:565
  80.6 1.8 %shard_map.90 = f32[32,16,128]{2,1,0:T(8,128)} custom-call(f32[8,4,8,128]{3,2,1,0:T(8,128)S(1)} %bitcast.21, bf16[512,256]{1,0:T(8,128)(2,1)S(1)} %copy-done.1, bf16[512,256]{1,0:T(8,128)(2,1)S(1)} %copy-done.2, f32[1,128]{1,0:T(1,128)S(1)} %pad_maximum_fusion.strength_ref, f32[1,128]{1,0:T(1,128)S(1)} %concatenate.7.mean_ref), custom_call_target="tpu_custom_call" | custom-call | tf_op jit(solution)/shard_map/pallas_call | solution.py:489
  82.3 2.5 %all-to-all-start.5 = ((f32[32,16,128]{2,1,0:T(8,128)}), f32[32,16,128]{2,1,0:T(8,128)S(1)}, u32[]{:S(2)}, u32[]{:S(2)}) async-start(f32[32,16,128]{2,1,0:T(8,128)} %shard_map.90), calls=%async_computation.5 | async-start | bytes 524288 | tf_op jit(solution)/shard_map/all_to_all | solution.py:545
  84.8 7.2 %shard_map.91 = (bf16[8,768,256]{2,1,0:T(8,128)(2,1)}, bf16[8,768,256]{2,1,0:T(8,128)(2,1)}) custom-call(s32[1]{0:T(128)} %bitcast.10.tm_ref, f32[2,32,16,512]{3,2,1,0:T(8,128)} %retarded_ref.4, f32[2,32,16,512]{3,2,1,0:T(8,128)} %lesser_ref.4, f32[4,32,16,128]{3,2,1,0:T(8,128)} %collective-permute-done.3.rim_ref), custom_call_target="tpu_custom_call" | custom-call | tf_op jit(solution)/shard_map/pallas_call | solution.py:547
  92.1 3.1 %all-to-all-done.5 = f32[32,16,128]{2,1,0:T(8,128)S(1)} async-done(((f32[32,16,128]{2,1,0:T(8,128)}), f32[32,16,128]{2,1,0:T(8,128)S(1)}, u32[]{:S(2)}, u32[]{:S(2)}) %all-to-all-start.5) | async-done | bytes 262176 | tf_op jit(solution)/shard_map/all_to_all | solution.py:545
  95.2 0.6 collective-permute-start.6
  95.8 0.0 collective-permute-start.5
  95.8 4.0 %shard_map.92.others_0_ = f32[2,32,16,512]{3,2,1,0:T(8,128)} custom-call(s32[1]{0:T(128)} %bitcast.6.tm_ref, f32[512,128]{1,0:T(8,128)S(1)} %bitcast.17, f32[2,32,16,16]{3,2,1,0:T(8,128)S(1)} %copy.12.propagator_ref, bf16[8,768,256]{2,1,0:T(8,128)(2,1)} %get-tuple-element.84.ladder_ref), custom_call_target="tpu_custom_call" | custom-call | tf_op jit(solution)/shard_map/pallas_call | solution.py:598
  99.8 0.0 collective-permute-done.6.arrived_ref
  99.8 4.0 %shard_map.93.others_0_ = f32[2,32,16,512]{3,2,1,0:T(8,128)} custom-call(s32[1]{0:T(128)} %bitcast.12.tm_ref, f32[512,128]{1,0:T(8,128)S(1)} %collective-permute-done.6.arrived_ref, f32[2,32,16,16]{3,2,1,0:T(8,128)S(1)} %copy.12.propagator_ref, bf16[8,768,256]{2,1,0:T(8,128)(2,1)} %get-tuple-element.83.ladder_ref, ...), custom_call_target="tpu_custom_call", output_to_operand_aliasing={{}: (4, {})} | custom-call | tf_op jit(solution)/shard_map/pallas_call | solution.py:598
  103.8 0.0 collective-permute-done.5.arrived_ref
  103.8 0.9 collective-permute-start.7
  104.7 4.1 %shard_map.94.others_0_ = f32[2,32,16,512]{3,2,1,0:T(8,128)} custom-call(s32[1]{0:T(128)} %bitcast.10.tm_ref, f32[512,128]{1,0:T(8,128)S(1)} %collective-permute-done.5.arrived_ref, f32[2,32,16,16]{3,2,1,0:T(8,128)S(1)} %copy.12.propagator_ref, bf16[8,768,256]{2,1,0:T(8,128)(2,1)} %get-tuple-element.87.ladder_ref, ...), custom_call_target="tpu_custom_call", output_to_operand_aliasing={{}: (4, {})} | custom-call | tf_op jit(solution)/shard_map/pallas_call | solution.py:598
  108.8 0.0 collective-permute-done.7.arrived_ref
  108.8 0.0 copy-done
  108.8 2.8 %shard_map.95 = f32[2,32,16,512]{3,2,1,0:T(8,128)} custom-call(s32[1]{0:T(128)} %bitcast.tm_ref, f32[512,128]{1,0:T(8,128)S(1)} %collective-permute-done.7.arrived_ref, f32[2,32,16,16]{3,2,1,0:T(8,128)S(1)} %copy.12.propagator_ref, bf16[8,768,256]{2,1,0:T(8,128)(2,1)S(1)} %copy-done, ...), custom_call_target="tpu_custom_call", output_to_operand_aliasing={{}: (4, {})} | custom-call | tf_op jit(solution)/shard_map/pallas_call | solution.py:598
  (7 shorter events, 0.0 us)
Async XLA Ops:
  1.2 5.8 %copy-start.5 = (f32[256]{0:T(256)S(1)}, f32[256]{0:T(256)}, u32[]{:S(2)}) copy-start(f32[256]{0:T(256)} %param.11) | copy-start | bytes 3076
  3.6 2.7 %collective-permute-start = (f32[512,128]{1,0:T(8,128)S(1)}, f32[512,128]{1,0:T(8,128)S(1)}, u32[]{:S(2)}, u32[]{:S(2)}) collective-permute-start(f32[512,128]{1,0:T(8,128)S(1)} %get-tuple-element.48), channel_id=1, source_target_pairs={{3,2},{7,6},{11,10},{15,14},{19,18},{23,22},{27,26},{31,30}} | collective-permute-start | bytes 786440 | tf_op jit(solution)/shard_map/ppermute | solution.py:514
  4.3 21.1 %collective-permute-start.1 = (f32[4,8,16,256]{3,2,1,0:T(8,128)S(1)}, f32[4,8,16,256]{3,2,1,0:T(8,128)S(1)}, u32[]{:S(2)}, u32[]{:S(2)}) collective-permute-start(f32[4,8,16,256]{3,2,1,0:T(8,128)S(1)} %get-tuple-element.50), channel_id=1, source_target_pairs={{3,0},{7,4},{11,8},{15,12},{19,16},{23,20},{27,24},{31,28}} | collective-permute-start | bytes 1572872 | tf_op jit(solution)/shard_map/ppermute | solution.py:515
  5.0 20.4 %collective-permute-start.2 = (f32[4,8,16,256]{3,2,1,0:T(8,128)S(1)}, f32[4,8,16,256]{3,2,1,0:T(8,128)}, u32[]{:S(2)}, u32[]{:S(2)}) collective-permute-start(f32[4,8,16,256]{3,2,1,0:T(8,128)S(1)} %get-tuple-element.51), channel_id=1, source_target_pairs={{3,1},{7,5},{11,9},{15,13},{19,17},{23,21},{27,25},{31,29}} | collective-permute-start | bytes 1572872 | tf_op jit(solution)/shard_map/ppermute | solution.py:515
  7.1 20.1 %all-to-all-start = ((f32[32,16,128]{2,1,0:T(8,128)}), f32[32,16,128]{2,1,0:T(8,128)S(1)}, u32[]{:S(2)}, u32[]{:S(2)}) async-start(f32[32,16,128]{2,1,0:T(8,128)} %bitcast.1), calls=%async_computation | async-start | bytes 524288 | tf_op jit(solution)/shard_map/all_to_all | solution.py:565
  17.0 6.4 %copy-start.7 = (f32[8]{0:T(128)S(1)}, f32[8]{0:T(128)}, u32[]{:S(2)}) copy-start(f32[8]{0:T(128)} %param.13) | copy-start | bytes 100
  17.0 6.5 %copy-start.6 = (f32[256]{0:T(256)S(1)}, f32[256]{0:T(256)}, u32[]{:S(2)}) copy-start(f32[256]{0:T(256)} %param.12) | copy-start | bytes 3076
  17.0 10.2 %copy-start.1 = (bf16[512,256]{1,0:T(8,128)(2,1)S(1)}, bf16[512,256]{1,0:T(8,128)(2,1)}, u32[]{:S(2)}) copy-start(bf16[512,256]{1,0:T(8,128)(2,1)} %constant.32.clone.high_ref) | copy-start | bytes 786436
  17.1 10.2 %copy-start.2 = (bf16[512,256]{1,0:T(8,128)(2,1)S(1)}, bf16[512,256]{1,0:T(8,128)(2,1)}, u32[]{:S(2)}) copy-start(bf16[512,256]{1,0:T(8,128)(2,1)} %constant.33.clone.low_ref) | copy-start | bytes 786436
  19.9 17.1 %collective-permute-start.3 = (f32[4,32,16,128]{3,2,1,0:T(8,128)}, f32[4,32,16,128]{3,2,1,0:T(8,128)}, u32[]{:S(2)}, u32[]{:S(2)}) collective-permute-start(f32[4,32,16,128]{3,2,1,0:T(8,128)} %get-tuple-element.58), channel_id=1, source_target_pairs={{0,1},{1,2},{2,3},{4,5},{5,6},{6,7},{8,9},{9,10},{10,11},{12,13},{... | collective-permute-start | bytes 3145736 | tf_op jit(solution)/shard_map/ppermute | solution.py:25
  23.6 9.4 %collective-permute-start.4 = (f32[4,8,16,256]{3,2,1,0:T(8,128)}, f32[4,8,16,256]{3,2,1,0:T(8,128)}, u32[]{:S(2)}, u32[]{:S(2)}) collective-permute-start(f32[4,8,16,256]{3,2,1,0:T(8,128)} %get-tuple-element.59), channel_id=1, source_target_pairs={{3,2},{7,6},{11,10},{15,14},{19,18},{23,22},{27,26},{31,30}} | collective-permute-start | bytes 1572872 | tf_op jit(solution)/shard_map/ppermute | solution.py:528
  25.4 3.7 %copy-start.4 = (f32[4,8,16,256]{3,2,1,0:T(8,128)}, f32[4,8,16,256]{3,2,1,0:T(8,128)S(1)}, u32[]{:S(2)}) copy-start(f32[4,8,16,256]{3,2,1,0:T(8,128)S(1)} %collective-permute-done.1) | copy-start | bytes 1572868
  29.0 14.1 %all-to-all-start.1 = ((f32[32,16,128]{2,1,0:T(8,128)}), f32[32,16,128]{2,1,0:T(8,128)S(1)}, u32[]{:S(2)}, u32[]{:S(2)}) async-start(f32[32,16,128]{2,1,0:T(8,128)} %shard_map.83), calls=%async_computation.1 | async-start | bytes 524288 | tf_op jit(solution)/shard_map/all_to_all | solution.py:585
  55.5 0.7 copy-start.3
  56.2 12.9 %all-to-all-start.3 = ((f32[32,16,128]{2,1,0:T(8,128)}), f32[32,16,128]{2,1,0:T(8,128)S(1)}, u32[]{:S(2)}, u32[]{:S(2)}) async-start(f32[32,16,128]{2,1,0:T(8,128)} %copy-done.3), calls=%async_computation.3 | async-start | bytes 524288 | tf_op jit(solution)/shard_map/all_to_all | solution.py:545
  82.3 12.9 %all-to-all-start.5 = ((f32[32,16,128]{2,1,0:T(8,128)}), f32[32,16,128]{2,1,0:T(8,128)S(1)}, u32[]{:S(2)}, u32[]{:S(2)}) async-start(f32[32,16,128]{2,1,0:T(8,128)} %shard_map.90), calls=%async_computation.5 | async-start | bytes 524288 | tf_op jit(solution)/shard_map/all_to_all | solution.py:545
  95.2 4.6 %collective-permute-start.6 = (f32[512,128]{1,0:T(8,128)S(1)}, f32[512,128]{1,0:T(8,128)S(1)}, u32[]{:S(2)}, u32[]{:S(2)}) collective-permute-start(f32[512,128]{1,0:T(8,128)S(1)} %bitcast.15), channel_id=1, source_target_pairs={{0,1},{1,0},{2,3},{3,2},{4,5},{5,4},{6,7},{7,6},{8,9},{9,8},{10,11... | collective-permute-start | bytes 786440 | tf_op jit(solution)/shard_map/ppermute | solution.py:620
  95.8 8.0 %collective-permute-start.5 = (f32[512,128]{1,0:T(8,128)S(1)}, f32[512,128]{1,0:T(8,128)S(1)}, u32[]{:S(2)}, u32[]{:S(2)}) collective-permute-start(f32[512,128]{1,0:T(8,128)S(1)} %bitcast.16), channel_id=1, source_target_pairs={{0,2},{1,3},{2,0},{3,1},{4,6},{5,7},{6,4},{7,5},{8,10},{9,11},{10,... | collective-permute-start | bytes 786440 | tf_op jit(solution)/shard_map/ppermute | solution.py:620
  103.8 5.0 %collective-permute-start.7 = (f32[512,128]{1,0:T(8,128)S(1)}, f32[512,128]{1,0:T(8,128)S(1)}, u32[]{:S(2)}, u32[]{:S(2)}) collective-permute-start(f32[512,128]{1,0:T(8,128)S(1)} %collective-permute-done.5.arrived_ref), channel_id=1, source_target_pairs={{0,1},{1,0},{2,3},{3,2},{4,5},{5,4},{6,7},{7,6},{8,9},{9,8},{10,11... | collective-permute-start | bytes 786440 | tf_op jit(solution)/shard_map/ppermute | solution.py:620
  104.7 4.1 %copy-start = (bf16[8,768,256]{2,1,0:T(8,128)(2,1)S(1)}, bf16[8,768,256]{2,1,0:T(8,128)(2,1)}, u32[]{:S(2)}) copy-start(bf16[8,768,256]{2,1,0:T(8,128)(2,1)} %get-tuple-element.86.ladder_ref) | copy-start | bytes 9437188

commit v5 on v4

--- a/solution.py
+++ b/solution.py
@@ -218,30 +218,46 @@
         copy.wait()
 
 
-def region_copies(retarded_ref, lesser_ref, near_refs, momenta, own, semaphores):
+def near_copies(histories, near_ref, tm, own, semaphores):
     copies = []
-    for kind, ref in enumerate((retarded_ref, lesser_ref)):
-        both = pl.ds(2 * kind, 2)
+    for kind, ref in enumerate(histories):
         last = ref.shape[3]
-        for number, (tm, near_ref) in enumerate(zip(momenta, near_refs)):
-            source = ref.at[:, tm * own : (tm + 1) * own, :, last - 2 * TILE :]
-            copies.append(pltpu.make_async_copy(source, near_ref.at[both], semaphores.at[kind, number]))
+        source = ref.at[:, tm * own : (tm + 1) * own, :, last - 2 * TILE :]
+        copies.append(pltpu.make_async_copy(source, near_ref.at[pl.ds(2 * kind, 2)], semaphores.at[kind]))
     return copies
 
 
-def regions_kernel(own, momenta, retarded_ref, lesser_ref, *others):
-    *near_refs, rim_ref, passing = others
-    copies = region_copies(retarded_ref, lesser_ref, near_refs, momenta, own, passing)
-    for kind, ref in enumerate((retarded_ref, lesser_ref)):
-        source = ref.at[:, :, :, ref.shape[3] - TILE :]
-        copies.append(pltpu.make_async_copy(source, rim_ref.at[pl.ds(2 * kind, 2)], passing.at[kind, len(near_refs)]))
-    wait_all(start_all(copies))
-
-
-def first_window_kernel(own, propagator_ref, retarded_ref, lesser_ref, low_ref, high_ref, *others):
-    *near_refs, window_ref, arrive, pass_on = others
+def rim_copies(ref, near_ref, own, semaphores):
+    copies = []
+    for number in range(8):
+        part, half, quarter = number // 4, number // 2 % 2, number % 2
+        source = ref.at[part, pl.ds((2 * half + quarter) * own, own), :, pl.ds(ref.shape[3] - TILE, TILE)]
+        target = near_ref.at[2 * part + half, :, :, pl.ds(quarter * TILE, TILE)]
+        copies.append(pltpu.make_async_copy(source, target, semaphores.at[number]))
+    return copies
+
+
+def settings_kernel(index_ref, coupling_ref, mf_ref, lag_ref, strength_ref, mean_ref):
+    lane = lax.broadcasted_iota(jnp.int32, strength_ref.shape, 1)
+    first = index_ref[0] // 2 * ORB
+    lag = index_ref[0] % 2 * (W // 2) + lane // ORB % (W // 2)
+    zero = jnp.zeros(strength_ref.shape, jnp.float32)
+    coupling, mf, weight = zero, zero, zero
+    for b in range(ORB):
+        coupling = jnp.where(lane % ORB == b, coupling_ref[first + b], coupling)
+        mf = jnp.where(lane % ORB == b, mf_ref[first + b], mf)
+    for m in range(W):
+        weight = jnp.where(lag == m, lag_ref[m], weight)
+    strength_ref[...] = coupling * coupling * weight
+    mean_ref[...] = jnp.where((lag == W - 1) & (lane < HALF), mf * weight, zero)
+
+
+def first_window_kernel(own, tm_ref, propagator_ref, retarded_ref, lesser_ref, low_ref, high_ref, *others):
+    *out_refs, window_ref, arrive, pass_on = others
+    histories = (retarded_ref, lesser_ref)
     momenta, columns = lesser_ref.shape[1], lesser_ref.shape[3]
     half = momenta // 2
+    last = len(out_refs)
     fetches = start_all(
         [
             pltpu.make_async_copy(
@@ -252,7 +268,21 @@
             for number, first in enumerate(range(0, momenta, own))
         ]
     )
-    copies = start_all(region_copies(retarded_ref, lesser_ref, near_refs, (0, 1), own, pass_on))
+
+    def near():
+        return [c for tm, ref in enumerate(out_refs) for c in near_copies(histories, ref, tm, own, pass_on.at[tm])]
+
+    def rims(second):
+        pairs = ((0, retarded_ref), (second, lesser_ref))
+        return [c for number, ref in pairs for c in rim_copies(ref, out_refs[number], own, pass_on.at[number])]
+
+    cases = ((tm_ref[0] == last, near), (tm_ref[0] == 0, lambda: rims(2)), ((tm_ref[0] != 0) & (tm_ref[0] != last), lambda: rims(1)))
+    for case, copies in cases:
+
+        @pl.when(case)
+        def _():
+            start_all(copies())
+
     for number, fetch in enumerate(fetches):
         fetch.wait()
         for k in range(number * own, (number + 1) * own):
@@ -260,7 +290,11 @@
             right = jnp.concatenate([window_ref[0, k], window_ref[1, k]], axis=1)
             imag, real = contract(*halves(left), *halves(right), TILE)
             store_window(low_ref if k < half else high_ref, k % half, half, -real, imag)
-    wait_all(copies)
+    for case, copies in cases:
+
+        @pl.when(case)
+        def _():
+            wait_all(copies())
 
 
 def fourier_kernel(arrived_ref, high_ref, low_ref, strength_ref, mean_ref, out_ref):
@@ -327,7 +361,18 @@
     return imag, -real
 
 
-def window_ladder_kernel(own, near_ref, high_ref, low_ref):
+def window_ladder_kernel(own, tm_ref, retarded_ref, lesser_ref, *others):
+    *near_refs, high_ref, low_ref, near_ref, arrive = others
+    for tm in range(len(near_refs) + 1):
+
+        @pl.when(tm_ref[0] == tm)
+        def _():
+            if tm < len(near_refs):
+                copies = [pltpu.make_async_copy(near_refs[tm], near_ref, arrive.at[0])]
+            else:
+                copies = near_copies((retarded_ref, lesser_ref), near_ref, tm, own, arrive)
+            wait_all(start_all(copies))
+
     for k in range(own):
         regions = [[near_ref[2 * kind + part, k] for part in range(2)] for kind in range(2)]
         high_ref[k], low_ref[k] = halves(ladder(regions, TILE))
@@ -356,26 +401,47 @@
     return tiles
 
 
-def final_ladder_kernel(tm_ref, retarded_ref, lesser_ref, rim_ref, *others):
-    *outs, region_ref, ladder_ref, arrive, leave = others
+def final_ladder_kernel(tm_ref, retarded_ref, lesser_ref, *others):
+    *others, region_ref, ladder_ref, arrive, arrive_rim, leave = others
+    outs, rim_refs = others[-2:], others[:-2]
     count, rows_each = ladder_ref.shape[0], ladder_ref.shape[1] // 2
     high_ref = ladder_ref.at[:, :rows_each]
     low_ref = ladder_ref.at[:, rows_each:]
-    own = count // 2
-    momenta = pl.ds(tm_ref[0] // 2 * count, count)
-    fetches = []
-    for kind, ref in enumerate((retarded_ref, lesser_ref)):
-        both = pl.ds(2 * kind, 2)
-        fetches += start_all(
-            [
-                pltpu.make_async_copy(
-                    ref.at[:, momenta], region_ref.at[both, :, :, pl.ds(TILE, ref.shape[3])], arrive.at[kind, 0]
-                ),
-                pltpu.make_async_copy(
-                    rim_ref.at[both, momenta], region_ref.at[both, :, :, pl.ds(0, TILE)], arrive.at[kind, 1]
-                ),
-            ]
-        )
+    own = count // len(outs)
+    half = tm_ref[1] // len(outs)
+    fetches = start_all(
+        [
+            pltpu.make_async_copy(
+                ref.at[:, pl.ds(half * count, count)],
+                region_ref.at[pl.ds(2 * kind, 2), :, :, pl.ds(TILE, ref.shape[3])],
+                arrive.at[kind],
+            )
+            for kind, ref in enumerate((retarded_ref, lesser_ref))
+        ]
+    )
+
+    def rims(second):
+        copies = []
+        for kind, ref in enumerate((rim_refs[0], rim_refs[second])):
+            for part in range(2):
+                for quarter in range(2):
+                    source = ref.at[2 * part + half, :, :, pl.ds(quarter * TILE, TILE)]
+                    target = region_ref.at[2 * kind + part, pl.ds(quarter * own, own), :, pl.ds(0, TILE)]
+                    copies.append(pltpu.make_async_copy(source, target, arrive_rim.at[2 * kind + part, quarter]))
+        return copies
+
+    @pl.when(tm_ref[0] == 0)
+    def _():
+        region_ref[:, :, :, :TILE] = jnp.zeros((4, count, ORB, TILE), jnp.float32)
+
+    @pl.when(tm_ref[0] == 1)
+    def _():
+        wait_all(start_all(rims(2)))
+
+    @pl.when(tm_ref[0] > 1)
+    def _():
+        wait_all(start_all(rims(1)))
+
     wait_all(fetches)
 
     def leaving(block, n):
@@ -497,74 +563,70 @@
     half = momenta_here // 2
     sent = f32((devices * half, TILE))
     near_shape = f32((4, own, ORB, 2 * TILE))
+    here = lax.axis_index("tm")
+    last = here == peers - 1
+    here_array = here.reshape(1).astype(jnp.int32)
     low, high, *near = pl.pallas_call(
         functools.partial(first_window_kernel, own),
-        out_shape=(sent, sent, near_shape, near_shape),
-        in_specs=[VMEM, IN_HBM, IN_HBM],
-        out_specs=(VMEM,) * 4,
+        out_shape=(sent, sent, near_shape, near_shape, near_shape),
+        in_specs=[SMEM, VMEM, IN_HBM, IN_HBM],
+        out_specs=(VMEM,) * 5,
         scratch_shapes=[
             pltpu.VMEM((2, momenta_here, ORB, TILE), jnp.float32),
             pltpu.SemaphoreType.DMA((peers,)),
-            pltpu.SemaphoreType.DMA((2, 2)),
+            pltpu.SemaphoreType.DMA((peers - 1, 8)),
         ],
         compiler_params=limit(8),
-    )(propagator, *(pltpu.with_memory_space_constraint(x, pltpu.HBM) for x in (hist_retarded, hist_lesser)))
-    here = lax.axis_index("tm")
-    last = here == peers - 1
-    low = lax.ppermute(low, "tm", [(3, 2)])
-    near = [lax.ppermute(block, "tm", [(3, tm)]) for tm, block in enumerate(near)]
+    )(here_array, propagator, *(pltpu.with_memory_space_constraint(x, pltpu.HBM) for x in (hist_retarded, hist_lesser)))
+    neighbours = [(0, 1), (1, 0), (2, 3), (3, 2)]
+    low = lax.ppermute(low, "tm", neighbours)
+    near[0] = lax.ppermute(near[0], "tm", [(3, 0), (0, 1), (1, 2), (2, 3)])
+    near[1] = lax.ppermute(near[1], "tm", [(3, 1), (1, 2), (2, 3), (0, 0)])
     send = jnp.where(last, high, low).reshape(devices, half, TILE)
-    send, hist_lesser, hist_retarded, coupling, mf_weight, lag_weight = lax.optimization_barrier(
-        (send, hist_lesser, hist_retarded, coupling, mf_weight, lag_weight)
-    )
-    two, mine, rim = pl.pallas_call(
-        functools.partial(regions_kernel, own, (2, 3)),
-        out_shape=(near_shape, near_shape, f32((4, momenta_here, ORB, TILE))),
-        in_specs=[IN_HBM, IN_HBM],
-        out_specs=(VMEM,) * 3,
-        scratch_shapes=[pltpu.SemaphoreType.DMA((2, 3))],
+    send, near[2], hist_lesser, hist_retarded, coupling, mf_weight, lag_weight = lax.optimization_barrier(
+        (send, near[2], hist_lesser, hist_retarded, coupling, mf_weight, lag_weight)
+    )
+    near[2] = lax.ppermute(near[2], "tm", neighbours)
+    histories = [pltpu.with_memory_space_constraint(x, pltpu.HBM) for x in (hist_retarded, hist_lesser)]
+    me = lax.axis_index("mom") * peers + here
+    strength, mean = pl.pallas_call(
+        settings_kernel,
+        out_shape=(f32((1, TILE)), f32((1, TILE))),
+        in_specs=[SMEM] * 4,
+        out_specs=(VMEM,) * 2,
         compiler_params=limit(4),
-    )(*(pltpu.with_memory_space_constraint(x, pltpu.HBM) for x in (hist_retarded, hist_lesser)))
-    near.append(lax.ppermute(two, "tm", [(3, 2)]))
-    rim = shifted(rim, "tm", 1)
-    me = lax.axis_index("mom") * peers + lax.axis_index("tm")
-    last_mark = (jnp.arange(W) == W - 1).astype(jnp.float32)
-    strong = (coupling * coupling).reshape(ORB, 1, ORB) * lag_weight[:, None]
-    mean = mf_weight.reshape(ORB, 1, ORB) * (lag_weight * last_mark)[:, None]
-    strong = lax.dynamic_slice_in_dim(strong.reshape(devices, HALF), me, 1, 0)
-    mean = lax.dynamic_slice_in_dim(mean.reshape(devices, HALF), me, 1, 0)
-    strength = jnp.concatenate([strong, strong], axis=1)
-    mean = jnp.concatenate([mean, jnp.zeros_like(mean)], axis=1)
+    )(me.reshape(1).astype(jnp.int32), coupling, mf_weight, lag_weight)
     table_high, table_low = fourier_tables()
 
     ladders = []
     ladder_shape = (own, 2 * 3 * TILE, 2 * TILE)
 
     def send_beside(sent):
-        sent, retarded, lesser, edge = lax.optimization_barrier((sent, hist_retarded, hist_lesser, rim))
+        sent, retarded, lesser, *edges = lax.optimization_barrier((sent, hist_retarded, hist_lesser, *near))
         arrived = lax.all_to_all(sent, both_axes, 0, 0, tiled=True)
-        momenta = (here ^ len(ladders)).reshape(1).astype(jnp.int32)
         ladder = pl.pallas_call(
             final_ladder_kernel,
             out_shape=(pltpu.HBM(ladder_shape, jnp.bfloat16),) * 2,
-            in_specs=[SMEM, IN_HBM, IN_HBM, IN_HBM],
+            in_specs=[SMEM] + [IN_HBM] * 5,
             out_specs=(IN_HBM,) * 2,
             scratch_shapes=[
                 pltpu.VMEM((4, 2 * own, ORB, TILE + columns), jnp.float32),
                 pltpu.VMEM((2 * own, *ladder_shape[1:]), jnp.bfloat16),
-                pltpu.SemaphoreType.DMA((2, 2)),
+                pltpu.SemaphoreType.DMA((2,)),
+                pltpu.SemaphoreType.DMA((4, 2)),
                 pltpu.SemaphoreType.DMA((2 * own,)),
             ],
             compiler_params=limit(12),
-        )(momenta, *(pltpu.with_memory_space_constraint(x, pltpu.HBM) for x in (retarded, lesser, edge)))
+        )(
+            jnp.stack([here, here ^ len(ladders)]).astype(jnp.int32),
+            *(pltpu.with_memory_space_constraint(x, pltpu.HBM) for x in (retarded, lesser, *edges)),
+        )
         arrived, *ladder = lax.optimization_barrier((arrived, *ladder))
         ladders.extend(ladder)
         return arrived
 
     for sweep in range(PASSES):
         arrived = lax.all_to_all(send, both_axes, 0, 0, tiled=True)
-        if sweep == 0:
-            arrived, *near[:2] = lax.optimization_barrier((arrived, *near[:2]))
         back = call(
             fourier_kernel,
             f32((devices, 2 * own, TILE)),
@@ -576,11 +638,15 @@
         )
         if sweep == 0:
             near[2], _ = lax.optimization_barrier((near[2], back))
-            for tm, received in enumerate(near):
-                mine = jnp.where(here == tm, received, mine)
             rungs = bf16((own, 2 * TILE, 2 * TILE))
-            rungs = call(functools.partial(window_ladder_kernel, own), (rungs, rungs), mine)
-            rim, *rungs = lax.optimization_barrier((rim, *rungs))
+            rungs = pl.pallas_call(
+                functools.partial(window_ladder_kernel, own),
+                out_shape=(rungs, rungs),
+                in_specs=[SMEM] + [IN_HBM] * 5,
+                out_specs=(VMEM, VMEM),
+                scratch_shapes=[pltpu.VMEM(near_shape.shape, jnp.float32), pltpu.SemaphoreType.DMA((2,))],
+                compiler_params=limit(8),
+            )(here_array, *histories, *[pltpu.with_memory_space_constraint(x, pltpu.HBM) for x in near])
             propagator_own = own_block(propagator, own, 1)
         arrived = send_beside(back) if sweep else lax.all_to_all(back, both_axes, 0, 0, tiled=True)
         arrived = arrived.reshape(2 * count, TILE)

time: 112 us -> 108 us (0.964)
  starting transfers between devices: 27.9 us -> 20.6 us
  waiting for transfers between devices: 16.1 us -> 20.4 us
  other arithmetic: 2.23 us -> 0.81 us
    all_to_all x1, waiting for transfers between devices: 1.88 us -> 5.51 us  [on_device_tiled(): arrived = lax.all_to_all(send, both_axes, 0, 0, tiled=True)]
    ppermute x5 -> x4, starting transfers between devices: 7.67 us -> 4.24 us  [the longest x1 2.26 us: on_device_tiled(): near[1] = lax.ppermute(near[1], 'tm', [(3, 1), (1, 2), (2, 3), (0, 0)])]
    all_to_all x1, starting transfers between devices: 9.88 us -> 7.11 us  [on_device_tiled(): arrived = lax.all_to_all(send, both_axes, 0, 0, tiled=True)]
    ppermute x5 -> x4, waiting for transfers between devices: 1.73 us -> 3.27 us  [the longest x1 1.8 us: on_device_tiled(): near[1] = lax.ppermute(near[1], 'tm', [(3, 1), (1, 2), (2, 3), (0, 0)])]
    select_n x1 -> x0, other arithmetic: 1.27 us -> none  [on_device_tiled(): mine = jnp.where(here == tm, received, mine)]
    all_to_all x2, waiting for transfers between devices: 6.26 us -> 5.1 us  [send_beside(): arrived = lax.all_to_all(sent, both_axes, 0, 0, tiled=True)]
    pallas_call x6 -> x5, Pallas kernels: 6.7 us -> 5.69 us  [call(): pl.pallas_call(kernel, out_shape=shapes, in_specs=[VMEM] * len(operands),...]
    pallas_call x1 -> x2, Pallas kernels: 2.79 us -> 2.67 us  [the longest x1 2.07 us: on_device_tiled(): pl.pallas_call(functools.partial(window_ladder_kernel, own), out_shape=(r...]
  transfers between devices with their start and end apart: 12 -> 11, of which waited for: 5 -> 6; matrix products, arithmetic and copies ran while one was open for 2% -> 0% of each run, Pallas kernels for 29% -> 30%
where the time goes in v5:
time: 108 us
  Pallas kernels  41.4 us (38%)
  blocking collectives  22.1 us (20%)
  starting transfers between devices  20.6 us (19%)
  waiting for transfers between devices  20.4 us (19%)
  local copies, waits for them, and re-layouts  1.97 us (2%)
    all_to_all x2, blocking collectives, on_device_tiled(): arrived = lax.all_to_all(send, both_axes, 0, 0, tiled=True)  22.1 us
    pallas_call x2, Pallas kernels, send_beside(): pl.pallas_call(final_ladder_kernel, out_shape=(pltpu.HBM(ladder_shape, jn...  15.6 us
    pallas_call x4, Pallas kernels, finish(): pl.pallas_call(functools.partial(final_kernel, own, len(before)), out_sha...  14.8 us
    all_to_all x1, starting transfers between devices, on_device_tiled(): arrived = lax.all_to_all(send, both_axes, 0, 0, tiled=True)  7.11 us
    all_to_all x1, waiting for transfers between devices, on_device_tiled(): lax.all_to_all(back, both_axes, 0, 0, tiled=True)  6.47 us
    pallas_call x5, Pallas kernels, call(): pl.pallas_call(kernel, out_shape=shapes, in_specs=[VMEM] * len(operands),...  5.69 us
    all_to_all x1, waiting for transfers between devices, on_device_tiled(): arrived = lax.all_to_all(send, both_axes, 0, 0, tiled=True)  5.51 us
    all_to_all x2, waiting for transfers between devices, send_beside(): arrived = lax.all_to_all(sent, both_axes, 0, 0, tiled=True)  5.1 us
  transfers between devices with their start and end apart: 11, of which 6 were waited for; matrix products, arithmetic and copies ran while one was open for 0% of the time, Pallas kernels for 30%

profile of v5, /device:TPU:1, one launch (start us, length us, event | category | flops | bytes accessed | tf_op | source)
XLA Modules:
  0.0 107.5 jit_solution(6690831478092246884)
XLA Ops:
  0.0 1.2 %copy.12.propagator_ref = f32[2,32,16,16]{3,2,1,0:T(8,128)S(1)} copy(f32[2,32,16,16]{1,3,2,0:T(8,128)} %param.10) | data formatting | bytes 131072 | tf_op args[2]
  1.2 0.0 copy-start.4
  1.2 0.0 copy-start.5
  1.3 0.0 copy-start.6
  1.3 0.0 copy-start.1
  1.3 0.0 copy-start.2
  1.3 2.6 %shard_map.82 = (f32[512,128]{1,0:T(8,128)S(1)}, f32[512,128]{1,0:T(8,128)S(1)}, f32[4,8,16,256]{3,2,1,0:T(8,128)S(1)}, f32[4,8,16,256]{3,2,1,0:T(8,128)S(1)}, f32[4,8,16,256]{3,2,1,0:T(8,128)S(1)}) custom-call(s32[1]{0:T(128)} %bitcast.1.tm_ref, f32[2,32,16,16]{3,2,1,0:T(8,128)S(1)} %copy.12.propagator_ref, f32[2,32,16,512]{3,2,1,0:T(8,128)} %retarded_ref.4, ...), custom_call_target="tpu_custom_call" | custom-call | tf_op jit(solution)/shard_map/pallas_call | solution.py:569
  3.9 0.1 collective-permute-start
  4.1 1.5 %collective-permute-done = f32[512,128]{1,0:T(8,128)S(1)} collective-permute-done((f32[512,128]{1,0:T(8,128)S(1)}, f32[512,128]{1,0:T(8,128)S(1)}, u32[]{:S(2)}, u32[]{:S(2)}) %collective-permute-start) | collective-permute-done | bytes 262176 | tf_op jit(solution)/shard_map/ppermute | solution.py:582
  5.5 0.7 broadcast_select_fusion
  6.3 7.1 %all-to-all-start = ((f32[32,16,128]{2,1,0:T(8,128)}), f32[32,16,128]{2,1,0:T(8,128)S(1)}, u32[]{:S(2)}, u32[]{:S(2)}) async-start(f32[32,16,128]{2,1,0:T(8,128)} %bitcast.2), calls=%async_computation | async-start | bytes 524288 | tf_op jit(solution)/shard_map/all_to_all | solution.py:629
  13.4 0.3 collective-permute-start.3
  13.7 1.5 %collective-permute-start.1 = (f32[4,8,16,256]{3,2,1,0:T(8,128)S(1)}, f32[4,8,16,256]{3,2,1,0:T(8,128)}, u32[]{:S(2)}, u32[]{:S(2)}) collective-permute-start(f32[4,8,16,256]{3,2,1,0:T(8,128)S(1)} %get-tuple-element.57), channel_id=1, source_target_pairs={{3,0},{0,1},{1,2},{2,3},{7,4},{4,5},{5,6},{6,7},{11,8},{8,9},{9,10... | collective-permute-start | bytes 1572872 | tf_op jit(solution)/shard_map/ppermute | solution.py:583
  15.2 2.3 %collective-permute-start.2 = (f32[4,8,16,256]{3,2,1,0:T(8,128)S(1)}, f32[4,8,16,256]{3,2,1,0:T(8,128)}, u32[]{:S(2)}, u32[]{:S(2)}) collective-permute-start(f32[4,8,16,256]{3,2,1,0:T(8,128)S(1)} %get-tuple-element.58), channel_id=1, source_target_pairs={{3,1},{1,2},{2,3},{0,0},{7,5},{5,6},{6,7},{4,4},{11,9},{9,10},{10,... | collective-permute-start | bytes 1572872 | tf_op jit(solution)/shard_map/ppermute | solution.py:584
  17.5 0.0 copy-done.4
  17.5 0.0 copy-done.5
  17.5 0.0 copy-done.6
  17.5 0.6 shard_map.83
  18.1 5.5 %all-to-all-done = f32[32,16,128]{2,1,0:T(8,128)S(1)} async-done(((f32[32,16,128]{2,1,0:T(8,128)}), f32[32,16,128]{2,1,0:T(8,128)S(1)}, u32[]{:S(2)}, u32[]{:S(2)}) %all-to-all-start) | async-done | bytes 262176 | tf_op jit(solution)/shard_map/all_to_all | solution.py:629
  23.6 0.0 copy-done.1
  23.6 0.0 copy-done.2
  23.6 1.8 %shard_map.84 = f32[32,16,128]{2,1,0:T(8,128)} custom-call(f32[8,4,16,128]{3,2,1,0:T(8,128)S(1)} %bitcast.14, bf16[512,256]{1,0:T(8,128)(2,1)S(1)} %copy-done.1, bf16[512,256]{1,0:T(8,128)(2,1)S(1)} %copy-done.2, f32[1,128]{1,0:T(1,128)S(1)} %get-tuple-element.53.strength_ref, f32[1,128]{1,0:T(1,128)S(1)} %get-tuple-element.54.mean_ref), custom_call_target="tpu_custom_call" | custom-call | tf_op jit(solution)/shard_map/pallas_call | solution.py:555
  25.4 2.8 %all-to-all-start.1 = ((f32[32,16,128]{2,1,0:T(8,128)}), f32[32,16,128]{2,1,0:T(8,128)S(1)}, u32[]{:S(2)}, u32[]{:S(2)}) async-start(f32[32,16,128]{2,1,0:T(8,128)} %shard_map.84), calls=%async_computation.1 | async-start | bytes 524288 | tf_op jit(solution)/shard_map/all_to_all | solution.py:651
  28.2 0.0 collective-permute-done.3.others_2_
  28.2 0.0 collective-permute-done.1.others_0_
  28.2 1.8 %collective-permute-done.2.others_1_ = f32[4,8,16,256]{3,2,1,0:T(8,128)} collective-permute-done((f32[4,8,16,256]{3,2,1,0:T(8,128)S(1)}, f32[4,8,16,256]{3,2,1,0:T(8,128)}, u32[]{:S(2)}, u32[]{:S(2)}) %collective-permute-start.2) | collective-permute-done | bytes 524320 | tf_op jit(solution)/shard_map/ppermute | solution.py:584
  30.0 2.1 %shard_map.85 = (bf16[8,256,256]{2,1,0:T(8,128)(2,1)S(1)}, bf16[8,256,256]{2,1,0:T(8,128)(2,1)S(1)}) custom-call(s32[1]{0:T(128)} %bitcast.1.tm_ref, f32[2,32,16,512]{3,2,1,0:T(8,128)} %retarded_ref.4, f32[2,32,16,512]{3,2,1,0:T(8,128)} %lesser_ref.4, f32[4,8,16,256]{3,2,1,0:T(8,128)} %collective-permute-done.1.others_0_, ...), custom_call_target="tpu_custom_call" | custom-call | tf_op jit(solution)/shard_map/pallas_call | solution.py:642
  32.1 6.5 %all-to-all-done.1 = f32[32,16,128]{2,1,0:T(8,128)S(1)} async-done(((f32[32,16,128]{2,1,0:T(8,128)}), f32[32,16,128]{2,1,0:T(8,128)S(1)}, u32[]{:S(2)}, u32[]{:S(2)}) %all-to-all-start.1) | async-done | bytes 262176 | tf_op jit(solution)/shard_map/all_to_all | solution.py:651
  38.6 0.5 shard_map.86
  39.1 10.6 %all_to_all.30 = f32[32,8,128]{2,1,0:T(8,128)S(1)} all-to-all(f32[32,8,128]{2,1,0:T(8,128)S(1)} %bitcast.21), channel_id=1, replica_groups=mesh['mom'=8,'tm'=4] {'mom','tm'}, dimensions={0} | all-to-all | bytes 262144 | tf_op jit(solution)/shard_map/all_to_all | solution.py:629
  49.8 1.1 shard_map.87
  50.9 0.0 copy-start.3
  50.9 0.7 copy-done.3
  51.6 2.5 %all-to-all-start.3 = ((f32[32,16,128]{2,1,0:T(8,128)}), f32[32,16,128]{2,1,0:T(8,128)S(1)}, u32[]{:S(2)}, u32[]{:S(2)}) async-start(f32[32,16,128]{2,1,0:T(8,128)} %copy-done.3), calls=%async_computation.3 | async-start | bytes 524288 | tf_op jit(solution)/shard_map/all_to_all | solution.py:606
  54.1 0.1 pad_add_fusion
  54.1 7.8 %shard_map.88 = (bf16[8,768,256]{2,1,0:T(8,128)(2,1)}, bf16[8,768,256]{2,1,0:T(8,128)(2,1)}) custom-call(s32[2]{0:T(128)S(1)} %get-tuple-element.87.tm_ref, f32[2,32,16,512]{3,2,1,0:T(8,128)} %retarded_ref.4, f32[2,32,16,512]{3,2,1,0:T(8,128)} %lesser_ref.4, f32[4,8,16,256]{3,2,1,0:T(8,128)} %collective-permute-done.1.others_0_, ...), custom_call_target="tpu_custom_call" | custom-call | tf_op jit(solution)/shard_map/pallas_call | solution.py:607
  62.0 2.5 %all-to-all-done.3 = f32[32,16,128]{2,1,0:T(8,128)S(1)} async-done(((f32[32,16,128]{2,1,0:T(8,128)}), f32[32,16,128]{2,1,0:T(8,128)S(1)}, u32[]{:S(2)}, u32[]{:S(2)}) %all-to-all-start.3) | async-done | bytes 262176 | tf_op jit(solution)/shard_map/all_to_all | solution.py:606
  64.5 0.5 shard_map.89
  65.0 11.5 %all_to_all.31 = f32[32,8,128]{2,1,0:T(8,128)S(1)} all-to-all(f32[32,8,128]{2,1,0:T(8,128)S(1)} %bitcast.20), channel_id=1, replica_groups=mesh['mom'=8,'tm'=4] {'mom','tm'}, dimensions={0} | all-to-all | bytes 262144 | tf_op jit(solution)/shard_map/all_to_all | solution.py:629
  76.5 1.8 %shard_map.90 = f32[32,16,128]{2,1,0:T(8,128)} custom-call(f32[8,4,8,128]{3,2,1,0:T(8,128)S(1)} %bitcast.22, bf16[512,256]{1,0:T(8,128)(2,1)S(1)} %copy-done.1, bf16[512,256]{1,0:T(8,128)(2,1)S(1)} %copy-done.2, f32[1,128]{1,0:T(1,128)S(1)} %get-tuple-element.53.strength_ref, f32[1,128]{1,0:T(1,128)S(1)} %get-tuple-element.54.mean_ref), custom_call_target="tpu_custom_call" | custom-call | tf_op jit(solution)/shard_map/pallas_call | solution.py:555
  78.3 2.5 %all-to-all-start.5 = ((f32[32,16,128]{2,1,0:T(8,128)}), f32[32,16,128]{2,1,0:T(8,128)S(1)}, u32[]{:S(2)}, u32[]{:S(2)}) async-start(f32[32,16,128]{2,1,0:T(8,128)} %shard_map.90), calls=%async_computation.5 | async-start | bytes 524288 | tf_op jit(solution)/shard_map/all_to_all | solution.py:606
  80.7 7.8 %shard_map.91 = (bf16[8,768,256]{2,1,0:T(8,128)(2,1)}, bf16[8,768,256]{2,1,0:T(8,128)(2,1)}) custom-call(s32[2]{0:T(128)S(1)} %get-tuple-element.88.tm_ref, f32[2,32,16,512]{3,2,1,0:T(8,128)} %retarded_ref.4, f32[2,32,16,512]{3,2,1,0:T(8,128)} %lesser_ref.4, f32[4,8,16,256]{3,2,1,0:T(8,128)} %collective-permute-done.1.others_0_, ...), custom_call_target="tpu_custom_call" | custom-call | tf_op jit(solution)/shard_map/pallas_call | solution.py:607
  88.5 2.6 %all-to-all-done.5 = f32[32,16,128]{2,1,0:T(8,128)S(1)} async-done(((f32[32,16,128]{2,1,0:T(8,128)}), f32[32,16,128]{2,1,0:T(8,128)S(1)}, u32[]{:S(2)}, u32[]{:S(2)}) %all-to-all-start.5) | async-done | bytes 262176 | tf_op jit(solution)/shard_map/all_to_all | solution.py:606
  91.1 0.6 collective-permute-start.5
  91.7 0.0 collective-permute-start.4
  91.8 4.0 %shard_map.92.others_0_ = f32[2,32,16,512]{3,2,1,0:T(8,128)} custom-call(s32[1]{0:T(128)} %bitcast.1.tm_ref, f32[512,128]{1,0:T(8,128)S(1)} %bitcast.18, f32[2,32,16,16]{3,2,1,0:T(8,128)S(1)} %copy.12.propagator_ref, bf16[8,768,256]{2,1,0:T(8,128)(2,1)} %get-tuple-element.82.ladder_ref), custom_call_target="tpu_custom_call" | custom-call | tf_op jit(solution)/shard_map/pallas_call | solution.py:664
  95.8 0.0 collective-permute-done.5.arrived_ref
  95.8 4.0 %shard_map.93.others_0_ = f32[2,32,16,512]{3,2,1,0:T(8,128)} custom-call(s32[1]{0:T(128)} %bitcast.13.tm_ref, f32[512,128]{1,0:T(8,128)S(1)} %collective-permute-done.5.arrived_ref, f32[2,32,16,16]{3,2,1,0:T(8,128)S(1)} %copy.12.propagator_ref, bf16[8,768,256]{2,1,0:T(8,128)(2,1)} %get-tuple-element.81.ladder_ref, ...), custom_call_target="tpu_custom_call", output_to_operand_aliasing={{}: (4, {})} | custom-call | tf_op jit(solution)/shard_map/pallas_call | solution.py:664
  99.7 0.0 collective-permute-done.4.arrived_ref
  99.8 0.9 collective-permute-start.6
  100.6 0.0 copy-start
  100.6 4.1 %shard_map.94.others_0_ = f32[2,32,16,512]{3,2,1,0:T(8,128)} custom-call(s32[1]{0:T(128)} %bitcast.11.tm_ref, f32[512,128]{1,0:T(8,128)S(1)} %collective-permute-done.4.arrived_ref, f32[2,32,16,16]{3,2,1,0:T(8,128)S(1)} %copy.12.propagator_ref, bf16[8,768,256]{2,1,0:T(8,128)(2,1)} %get-tuple-element.85.ladder_ref, ...), custom_call_target="tpu_custom_call", output_to_operand_aliasing={{}: (4, {})} | custom-call | tf_op jit(solution)/shard_map/pallas_call | solution.py:664
  104.7 0.0 collective-permute-done.6.arrived_ref
  104.7 0.0 copy-done
  104.8 2.8 %shard_map.95 = f32[2,32,16,512]{3,2,1,0:T(8,128)} custom-call(s32[1]{0:T(128)} %bitcast.tm_ref, f32[512,128]{1,0:T(8,128)S(1)} %collective-permute-done.6.arrived_ref, f32[2,32,16,16]{3,2,1,0:T(8,128)S(1)} %copy.12.propagator_ref, bf16[8,768,256]{2,1,0:T(8,128)(2,1)S(1)} %copy-done, ...), custom_call_target="tpu_custom_call", output_to_operand_aliasing={{}: (4, {})} | custom-call | tf_op jit(solution)/shard_map/pallas_call | solution.py:664
  (1 shorter events, 0.0 us)
Async XLA Ops:
  1.2 16.3 %copy-start.4 = (f32[256]{0:T(256)S(1)}, f32[256]{0:T(256)}, u32[]{:S(2)}) copy-start(f32[256]{0:T(256)} %coupling_ref) | copy-start | bytes 3076
  1.2 16.3 %copy-start.5 = (f32[256]{0:T(256)S(1)}, f32[256]{0:T(256)}, u32[]{:S(2)}) copy-start(f32[256]{0:T(256)} %mf_ref) | copy-start | bytes 3076
  1.3 16.3 %copy-start.6 = (f32[8]{0:T(128)S(1)}, f32[8]{0:T(128)}, u32[]{:S(2)}) copy-start(f32[8]{0:T(128)} %lag_ref) | copy-start | bytes 100
  1.3 22.4 %copy-start.1 = (bf16[512,256]{1,0:T(8,128)(2,1)S(1)}, bf16[512,256]{1,0:T(8,128)(2,1)}, u32[]{:S(2)}) copy-start(bf16[512,256]{1,0:T(8,128)(2,1)} %constant.27.clone.high_ref) | copy-start | bytes 786436
  1.3 22.4 %copy-start.2 = (bf16[512,256]{1,0:T(8,128)(2,1)S(1)}, bf16[512,256]{1,0:T(8,128)(2,1)}, u32[]{:S(2)}) copy-start(bf16[512,256]{1,0:T(8,128)(2,1)} %constant.28.clone.low_ref) | copy-start | bytes 786436
  3.9 1.6 %collective-permute-start = (f32[512,128]{1,0:T(8,128)S(1)}, f32[512,128]{1,0:T(8,128)S(1)}, u32[]{:S(2)}, u32[]{:S(2)}) collective-permute-start(f32[512,128]{1,0:T(8,128)S(1)} %get-tuple-element.47), channel_id=1, source_target_pairs={{0,1},{1,0},{2,3},{3,2},{4,5},{5,4},{6,7},{7,6},{8,9},{9,8},{10,11... | collective-permute-start | bytes 786440 | tf_op jit(solution)/shard_map/ppermute | solution.py:582
  6.3 17.4 %all-to-all-start = ((f32[32,16,128]{2,1,0:T(8,128)}), f32[32,16,128]{2,1,0:T(8,128)S(1)}, u32[]{:S(2)}, u32[]{:S(2)}) async-start(f32[32,16,128]{2,1,0:T(8,128)} %bitcast.2), calls=%async_computation | async-start | bytes 524288 | tf_op jit(solution)/shard_map/all_to_all | solution.py:629
  13.4 14.9 %collective-permute-start.3 = (f32[4,8,16,256]{3,2,1,0:T(8,128)S(1)}, f32[4,8,16,256]{3,2,1,0:T(8,128)}, u32[]{:S(2)}, u32[]{:S(2)}) collective-permute-start(f32[4,8,16,256]{3,2,1,0:T(8,128)S(1)} %get-tuple-element.59), channel_id=1, source_target_pairs={{0,1},{1,0},{2,3},{3,2},{4,5},{5,4},{6,7},{7,6},{8,9},{9,8},{10,11... | collective-permute-start | bytes 1572872 | tf_op jit(solution)/shard_map/ppermute | solution.py:589
  13.7 14.5 %collective-permute-start.1 = (f32[4,8,16,256]{3,2,1,0:T(8,128)S(1)}, f32[4,8,16,256]{3,2,1,0:T(8,128)}, u32[]{:S(2)}, u32[]{:S(2)}) collective-permute-start(f32[4,8,16,256]{3,2,1,0:T(8,128)S(1)} %get-tuple-element.57), channel_id=1, source_target_pairs={{3,0},{0,1},{1,2},{2,3},{7,4},{4,5},{5,6},{6,7},{11,8},{8,9},{9,10... | collective-permute-start | bytes 1572872 | tf_op jit(solution)/shard_map/ppermute | solution.py:583
  15.2 14.8 %collective-permute-start.2 = (f32[4,8,16,256]{3,2,1,0:T(8,128)S(1)}, f32[4,8,16,256]{3,2,1,0:T(8,128)}, u32[]{:S(2)}, u32[]{:S(2)}) collective-permute-start(f32[4,8,16,256]{3,2,1,0:T(8,128)S(1)} %get-tuple-element.58), channel_id=1, source_target_pairs={{3,1},{1,2},{2,3},{0,0},{7,5},{5,6},{6,7},{4,4},{11,9},{9,10},{10,... | collective-permute-start | bytes 1572872 | tf_op jit(solution)/shard_map/ppermute | solution.py:584
  25.4 13.2 %all-to-all-start.1 = ((f32[32,16,128]{2,1,0:T(8,128)}), f32[32,16,128]{2,1,0:T(8,128)S(1)}, u32[]{:S(2)}, u32[]{:S(2)}) async-start(f32[32,16,128]{2,1,0:T(8,128)} %shard_map.84), calls=%async_computation.1 | async-start | bytes 524288 | tf_op jit(solution)/shard_map/all_to_all | solution.py:651
  50.9 0.7 copy-start.3
  51.6 12.9 %all-to-all-start.3 = ((f32[32,16,128]{2,1,0:T(8,128)}), f32[32,16,128]{2,1,0:T(8,128)S(1)}, u32[]{:S(2)}, u32[]{:S(2)}) async-start(f32[32,16,128]{2,1,0:T(8,128)} %copy-done.3), calls=%async_computation.3 | async-start | bytes 524288 | tf_op jit(solution)/shard_map/all_to_all | solution.py:606
  78.3 12.9 %all-to-all-start.5 = ((f32[32,16,128]{2,1,0:T(8,128)}), f32[32,16,128]{2,1,0:T(8,128)S(1)}, u32[]{:S(2)}, u32[]{:S(2)}) async-start(f32[32,16,128]{2,1,0:T(8,128)} %shard_map.90), calls=%async_computation.5 | async-start | bytes 524288 | tf_op jit(solution)/shard_map/all_to_all | solution.py:606
  91.1 4.6 %collective-permute-start.5 = (f32[512,128]{1,0:T(8,128)S(1)}, f32[512,128]{1,0:T(8,128)S(1)}, u32[]{:S(2)}, u32[]{:S(2)}) collective-permute-start(f32[512,128]{1,0:T(8,128)S(1)} %bitcast.16), channel_id=1, source_target_pairs={{0,1},{1,0},{2,3},{3,2},{4,5},{5,4},{6,7},{7,6},{8,9},{9,8},{10,11... | collective-permute-start | bytes 786440 | tf_op jit(solution)/shard_map/ppermute | solution.py:686
  91.7 8.0 %collective-permute-start.4 = (f32[512,128]{1,0:T(8,128)S(1)}, f32[512,128]{1,0:T(8,128)S(1)}, u32[]{:S(2)}, u32[]{:S(2)}) collective-permute-start(f32[512,128]{1,0:T(8,128)S(1)} %bitcast.17), channel_id=1, source_target_pairs={{0,2},{1,3},{2,0},{3,1},{4,6},{5,7},{6,4},{7,5},{8,10},{9,11},{10,... | collective-permute-start | bytes 786440 | tf_op jit(solution)/shard_map/ppermute | solution.py:686
  99.8 5.0 %collective-permute-start.6 = (f32[512,128]{1,0:T(8,128)S(1)}, f32[512,128]{1,0:T(8,128)S(1)}, u32[]{:S(2)}, u32[]{:S(2)}) collective-permute-start(f32[512,128]{1,0:T(8,128)S(1)} %collective-permute-done.4.arrived_ref), channel_id=1, source_target_pairs={{0,1},{1,0},{2,3},{3,2},{4,5},{5,4},{6,7},{7,6},{8,9},{9,8},{10,11... | collective-permute-start | bytes 786440 | tf_op jit(solution)/shard_map/ppermute | solution.py:686
  100.6 4.1 %copy-start = (bf16[8,768,256]{2,1,0:T(8,128)(2,1)S(1)}, bf16[8,768,256]{2,1,0:T(8,128)(2,1)}, u32[]{:S(2)}) copy-start(bf16[8,768,256]{2,1,0:T(8,128)(2,1)} %get-tuple-element.84.ladder_ref) | copy-start | bytes 9437188

commit v6 on v5

--- a/solution.py
+++ b/solution.py
@@ -252,20 +252,18 @@
     mean_ref[...] = jnp.where((lag == W - 1) & (lane < HALF), mf * weight, zero)
 
 
-def first_window_kernel(own, tm_ref, propagator_ref, retarded_ref, lesser_ref, low_ref, high_ref, *others):
-    *out_refs, window_ref, arrive, pass_on = others
+def regions_kernel(own, tm_ref, retarded_ref, lesser_ref, low_ref, high_ref, *others):
+    *out_refs, arrive, pass_on = others
     histories = (retarded_ref, lesser_ref)
     momenta, columns = lesser_ref.shape[1], lesser_ref.shape[3]
     half = momenta // 2
     last = len(out_refs)
-    fetches = start_all(
+    windows = start_all(
         [
             pltpu.make_async_copy(
-                lesser_ref.at[:, first : first + own, :, columns - TILE :],
-                window_ref.at[:, first : first + own],
-                arrive.at[number],
+                lesser_ref.at[:, number * half : (number + 1) * half, :, columns - TILE :], ref, arrive.at[number]
             )
-            for number, first in enumerate(range(0, momenta, own))
+            for number, ref in enumerate((low_ref, high_ref))
         ]
     )
 
@@ -276,25 +274,29 @@
         pairs = ((0, retarded_ref), (second, lesser_ref))
         return [c for number, ref in pairs for c in rim_copies(ref, out_refs[number], own, pass_on.at[number])]
 
-    cases = ((tm_ref[0] == last, near), (tm_ref[0] == 0, lambda: rims(2)), ((tm_ref[0] != 0) & (tm_ref[0] != last), lambda: rims(1)))
-    for case, copies in cases:
+    edge = (tm_ref[0] == 0) | (tm_ref[0] == last)
+    for case, copies in (
+        (tm_ref[0] == last, near),
+        (tm_ref[0] == 0, lambda: rims(2)),
+        (jnp.logical_not(edge), lambda: rims(1)),
+    ):
 
         @pl.when(case)
         def _():
-            start_all(copies())
-
-    for number, fetch in enumerate(fetches):
-        fetch.wait()
-        for k in range(number * own, (number + 1) * own):
-            left = jnp.concatenate([propagator_ref[0, k], propagator_ref[1, k]], axis=0)
-            right = jnp.concatenate([window_ref[0, k], window_ref[1, k]], axis=1)
-            imag, real = contract(*halves(left), *halves(right), TILE)
-            store_window(low_ref if k < half else high_ref, k % half, half, -real, imag)
-    for case, copies in cases:
-
-        @pl.when(case)
-        def _():
-            wait_all(copies())
+            wait_all(start_all(copies()))
+
+    wait_all(windows)
+
+
+def first_window_kernel(tm_ref, last, propagator_ref, low_ref, high_ref, send_ref):
+    half = low_ref.shape[1]
+    upper = tm_ref[0] == last
+    first = jnp.where(upper, half, 0)
+    for k in range(half):
+        left = jnp.concatenate([propagator_ref[part, first + k] for part in range(2)], axis=0)
+        window = [jnp.where(upper, high_ref[part, k], low_ref[part, k]) for part in range(2)]
+        imag, real = contract(*halves(left), *halves(jnp.concatenate(window, axis=1)), TILE)
+        store_window(send_ref, k, half, -real, imag)
 
 
 def fourier_kernel(arrived_ref, high_ref, low_ref, strength_ref, mean_ref, out_ref):
@@ -403,16 +405,17 @@
 
 def final_ladder_kernel(tm_ref, retarded_ref, lesser_ref, *others):
     *others, region_ref, ladder_ref, arrive, arrive_rim, leave = others
-    outs, rim_refs = others[-2:], others[:-2]
+    rim_refs, outs = others[:3], others[3:]
     count, rows_each = ladder_ref.shape[0], ladder_ref.shape[1] // 2
     high_ref = ladder_ref.at[:, :rows_each]
     low_ref = ladder_ref.at[:, rows_each:]
     own = count // len(outs)
-    half = tm_ref[1] // len(outs)
+    blocks = len(outs)
+    momenta = pl.ds(tm_ref[1] // blocks * count, count)
     fetches = start_all(
         [
             pltpu.make_async_copy(
-                ref.at[:, pl.ds(half * count, count)],
+                ref.at[:, momenta],
                 region_ref.at[pl.ds(2 * kind, 2), :, :, pl.ds(TILE, ref.shape[3])],
                 arrive.at[kind],
             )
@@ -420,27 +423,26 @@
         ]
     )
 
-    def rims(second):
+    def rims(second, quarters):
         copies = []
         for kind, ref in enumerate((rim_refs[0], rim_refs[second])):
             for part in range(2):
-                for quarter in range(2):
-                    source = ref.at[2 * part + half, :, :, pl.ds(quarter * TILE, TILE)]
-                    target = region_ref.at[2 * kind + part, pl.ds(quarter * own, own), :, pl.ds(0, TILE)]
-                    copies.append(pltpu.make_async_copy(source, target, arrive_rim.at[2 * kind + part, quarter]))
+                for number, quarter in enumerate(quarters):
+                    source = ref.at[2 * part + tm_ref[1] // 2, :, :, pl.ds(quarter * TILE, TILE)]
+                    target = region_ref.at[2 * kind + part, pl.ds(number * own, own), :, pl.ds(0, TILE)]
+                    copies.append(pltpu.make_async_copy(source, target, arrive_rim.at[2 * kind + part, number]))
         return copies
 
     @pl.when(tm_ref[0] == 0)
     def _():
         region_ref[:, :, :, :TILE] = jnp.zeros((4, count, ORB, TILE), jnp.float32)
 
-    @pl.when(tm_ref[0] == 1)
-    def _():
-        wait_all(start_all(rims(2)))
-
-    @pl.when(tm_ref[0] > 1)
-    def _():
-        wait_all(start_all(rims(1)))
+    for second, case in ((2, tm_ref[0] == 1), (1, tm_ref[0] > 1)):
+        for quarters in [(0, 1)] if blocks == 2 else [(0,), (1,)]:
+
+            @pl.when(case if blocks == 2 else case & (tm_ref[1] % 2 == quarters[0]))
+            def _():
+                wait_all(start_all(rims(second, quarters)))
 
     wait_all(fetches)
 
@@ -450,7 +452,7 @@
 
     def one(block, n, carry):
         k = block * own + n
-        source = (tm_ref[0] % 2 ^ block) * own + n
+        source = (tm_ref[1] % blocks ^ block) * own + n
         for part in range(2):
             region = jnp.concatenate([region_ref[2 * kind + part, source] for kind in range(2)], axis=0)
             lanes = pl.ds(part * TILE, TILE)
@@ -471,9 +473,9 @@
         start_all(leaving(block, n))
         return carry
 
-    for block in range(2):
+    for block in range(blocks):
         lax.fori_loop(0, own, functools.partial(one, block), 0)
-    for block in range(2):
+    for block in range(blocks):
         lax.fori_loop(0, own, lambda n, c: (wait_all(leaving(block, n)), c)[1], 0)
 
 
@@ -497,10 +499,17 @@
     return jnp.concatenate(rows, axis=0)
 
 
-def final_kernel(own, before, tm_ref, arrived_ref, propagator_ref, ladder_ref, *others):
-    out_ref, ladder_here, out_here, arrive, leave = others[before:]
+def final_kernel(own, fetched, following, before, tm_ref, arrived_ref, propagator_ref, ladder_ref, *others):
+    others = list(others)
+    source_ref = others.pop(0) if following else None
+    others = others[before:]
+    out_ref = others.pop(0)
+    next_ref = others.pop(0) if following else None
+    out_here, arrive, leave, *ladder_here = others
+    ladder_here = ladder_ref if fetched else ladder_here[0]
     base = tm_ref[0] * own
     group = own // 2
+    groups = own // group
     rows_each = ladder_here.shape[1] // 2
 
     def arriving(number):
@@ -513,7 +522,8 @@
         return [pltpu.make_async_copy(source, target, leave.at[number])]
 
     def one(number, carry):
-        wait_all(arriving(number))
+        if not fetched:
+            wait_all(arriving(number))
         for n in range(group):
             k = number * group + n
             pieces = coefficients(arrived_ref, propagator_ref.at[:, base + k], k, own)
@@ -527,10 +537,13 @@
         start_all(leaving(number))
         return carry
 
-    groups = own // group
-    for number in range(groups):
-        start_all(arriving(number))
+    if not fetched:
+        for number in range(groups):
+            start_all(arriving(number))
+    coming = [pltpu.make_async_copy(source_ref, next_ref, arrive.at[groups])] if following else []
+    start_all(coming)
     lax.fori_loop(0, groups, one, 0)
+    wait_all(coming)
     for number in range(groups):
         wait_all(leaving(number))
 
@@ -555,34 +568,36 @@
         return pl.pallas_call(
             kernel,
             out_shape=shapes,
-            in_specs=[VMEM] * len(operands),
+            in_specs=[SMEM if x.dtype == jnp.int32 else VMEM for x in operands],
             out_specs=jax.tree.map(lambda _: VMEM, shapes),
             compiler_params=limit(12),
         )(*operands)
 
     half = momenta_here // 2
-    sent = f32((devices * half, TILE))
+    window_shape = f32((2, half, ORB, TILE))
     near_shape = f32((4, own, ORB, 2 * TILE))
     here = lax.axis_index("tm")
-    last = here == peers - 1
     here_array = here.reshape(1).astype(jnp.int32)
     low, high, *near = pl.pallas_call(
-        functools.partial(first_window_kernel, own),
-        out_shape=(sent, sent, near_shape, near_shape, near_shape),
-        in_specs=[SMEM, VMEM, IN_HBM, IN_HBM],
+        functools.partial(regions_kernel, own),
+        out_shape=(window_shape, window_shape, near_shape, near_shape, near_shape),
+        in_specs=[SMEM, IN_HBM, IN_HBM],
         out_specs=(VMEM,) * 5,
-        scratch_shapes=[
-            pltpu.VMEM((2, momenta_here, ORB, TILE), jnp.float32),
-            pltpu.SemaphoreType.DMA((peers,)),
-            pltpu.SemaphoreType.DMA((peers - 1, 8)),
-        ],
-        compiler_params=limit(8),
-    )(here_array, propagator, *(pltpu.with_memory_space_constraint(x, pltpu.HBM) for x in (hist_retarded, hist_lesser)))
+        scratch_shapes=[pltpu.SemaphoreType.DMA((2,)), pltpu.SemaphoreType.DMA((peers - 1, 8))],
+        compiler_params=limit(4),
+    )(here_array, *(pltpu.with_memory_space_constraint(x, pltpu.HBM) for x in (hist_retarded, hist_lesser)))
     neighbours = [(0, 1), (1, 0), (2, 3), (3, 2)]
     low = lax.ppermute(low, "tm", neighbours)
+    send = call(
+        lambda tm_ref, *refs: first_window_kernel(tm_ref, peers - 1, *refs),
+        f32((devices * half, TILE)),
+        here_array,
+        propagator,
+        low,
+        high,
+    ).reshape(devices, half, TILE)
     near[0] = lax.ppermute(near[0], "tm", [(3, 0), (0, 1), (1, 2), (2, 3)])
     near[1] = lax.ppermute(near[1], "tm", [(3, 1), (1, 2), (2, 3), (0, 0)])
-    send = jnp.where(last, high, low).reshape(devices, half, TILE)
     send, near[2], hist_lesser, hist_retarded, coupling, mf_weight, lag_weight = lax.optimization_barrier(
         (send, near[2], hist_lesser, hist_retarded, coupling, mf_weight, lag_weight)
     )
@@ -598,35 +613,42 @@
     )(me.reshape(1).astype(jnp.int32), coupling, mf_weight, lag_weight)
     table_high, table_low = fourier_tables()
 
-    ladders = []
+    ladders = {}
     ladder_shape = (own, 2 * 3 * TILE, 2 * TILE)
 
-    def send_beside(sent):
-        sent, retarded, lesser, *edges = lax.optimization_barrier((sent, hist_retarded, hist_lesser, *near))
+    def send_beside(sent, step, blocks):
+        edges = [hist_retarded, hist_lesser, *near]
+        if step:
+            sent, *edges = lax.optimization_barrier((sent, *edges))
         arrived = lax.all_to_all(sent, both_axes, 0, 0, tiled=True)
         ladder = pl.pallas_call(
             final_ladder_kernel,
-            out_shape=(pltpu.HBM(ladder_shape, jnp.bfloat16),) * 2,
+            out_shape=[pltpu.HBM(ladder_shape, jnp.bfloat16)] * blocks,
             in_specs=[SMEM] + [IN_HBM] * 5,
-            out_specs=(IN_HBM,) * 2,
+            out_specs=[IN_HBM] * blocks,
             scratch_shapes=[
-                pltpu.VMEM((4, 2 * own, ORB, TILE + columns), jnp.float32),
-                pltpu.VMEM((2 * own, *ladder_shape[1:]), jnp.bfloat16),
+                pltpu.VMEM((4, blocks * own, ORB, TILE + columns), jnp.float32),
+                pltpu.VMEM((blocks * own, *ladder_shape[1:]), jnp.bfloat16),
                 pltpu.SemaphoreType.DMA((2,)),
                 pltpu.SemaphoreType.DMA((4, 2)),
-                pltpu.SemaphoreType.DMA((2 * own,)),
+                pltpu.SemaphoreType.DMA((blocks * own,)),
             ],
-            compiler_params=limit(12),
+            compiler_params=limit(6 * blocks),
         )(
-            jnp.stack([here, here ^ len(ladders)]).astype(jnp.int32),
-            *(pltpu.with_memory_space_constraint(x, pltpu.HBM) for x in (retarded, lesser, *edges)),
+            jnp.stack([here, here ^ step]).astype(jnp.int32),
+            *(pltpu.with_memory_space_constraint(x, pltpu.HBM) for x in edges),
         )
         arrived, *ladder = lax.optimization_barrier((arrived, *ladder))
-        ladders.extend(ladder)
+        ladders.update(zip(range(step, step + blocks), ladder))
         return arrived
 
+    def send_alone(sent):
+        return lax.all_to_all(sent, both_axes, 0, 0, tiled=True)
+
+    send_out = [send_alone, send_alone, lambda sent: send_beside(sent, 1, 1)]
+    send_back = [lambda sent: send_beside(sent, 0, 1), send_alone, lambda sent: send_beside(sent, 2, 2)]
     for sweep in range(PASSES):
-        arrived = lax.all_to_all(send, both_axes, 0, 0, tiled=True)
+        arrived = send_out[sweep](send)
         back = call(
             fourier_kernel,
             f32((devices, 2 * own, TILE)),
@@ -648,7 +670,7 @@
                 compiler_params=limit(8),
             )(here_array, *histories, *[pltpu.with_memory_space_constraint(x, pltpu.HBM) for x in near])
             propagator_own = own_block(propagator, own, 1)
-        arrived = send_beside(back) if sweep else lax.all_to_all(back, both_axes, 0, 0, tiled=True)
+        arrived = send_back[sweep](back)
         arrived = arrived.reshape(2 * count, TILE)
         if sweep + 1 < PASSES:
             send = call(
@@ -659,40 +681,39 @@
                 *rungs,
             ).reshape(devices, own, TILE)
 
-    def finish(new_slice, coefficients_of, step):
-        before = () if new_slice is None else (new_slice,)
-        return pl.pallas_call(
-            functools.partial(final_kernel, own, len(before)),
-            out_shape=pltpu.HBM(hist_lesser.shape, jnp.float32),
-            in_specs=[SMEM, VMEM, VMEM] + [IN_HBM] * (1 + len(before)),
-            out_specs=IN_HBM,
-            scratch_shapes=[
-                pltpu.VMEM(ladder_shape, jnp.bfloat16),
-                pltpu.VMEM((2, own, ORB, columns), jnp.float32),
-                pltpu.SemaphoreType.DMA((own,)),
-                pltpu.SemaphoreType.DMA((own,)),
-            ],
-            input_output_aliases={4: 0} if before else {},
+    def finish(new_slice, ladder, coefficients_of, step):
+        before = [] if new_slice is None else [new_slice]
+        following = [pltpu.with_memory_space_constraint(ladders[step + 1], pltpu.HBM)] if step % 2 == 0 else []
+        fetched = ladder is not None
+        if not fetched:
+            ladder = pltpu.with_memory_space_constraint(ladders[step], pltpu.HBM)
+        scratch = [
+            pltpu.VMEM((2, own, ORB, columns), jnp.float32),
+            pltpu.SemaphoreType.DMA((3,)),
+            pltpu.SemaphoreType.DMA((2,)),
+        ]
+        new_slice, *ladder = pl.pallas_call(
+            functools.partial(final_kernel, own, fetched, len(following), len(before)),
+            out_shape=[pltpu.HBM(hist_lesser.shape, jnp.float32)] + [bf16(ladder_shape)] * len(following),
+            in_specs=[SMEM, VMEM, VMEM, VMEM if fetched else IN_HBM] + [IN_HBM] * len(following + before),
+            out_specs=[IN_HBM] + [VMEM] * len(following),
+            scratch_shapes=scratch if fetched else scratch + [pltpu.VMEM(ladder_shape, jnp.bfloat16)],
+            input_output_aliases={4 + len(following): 0} if before else {},
             compiler_params=limit(6),
-        )(
-            (here ^ step).reshape(1).astype(jnp.int32),
-            coefficients_of,
-            propagator,
-            pltpu.with_memory_space_constraint(ladders[step], pltpu.HBM) if step < 3 else ladders[step],
-            *before,
-        )
+        )((here ^ step).reshape(1).astype(jnp.int32), coefficients_of, propagator, ladder, *following, *before)
+        return new_slice, *ladder
 
     def exchange(x, step):
         return lax.ppermute(x, "tm", [(t, t ^ step) for t in range(peers)])
 
     across = exchange(arrived, 2)
     beside_me = exchange(arrived, 1)
-    new_slice = finish(None, arrived, 0)
-    new_slice = finish(new_slice, beside_me, 1)
+    new_slice, ladder = finish(None, None, arrived, 0)
+    (new_slice,) = finish(new_slice, ladder, beside_me, 1)
     across, new_slice = lax.optimization_barrier((across, new_slice))
     beyond = exchange(across, 1)
-    new_slice = finish(new_slice, across, 2)
-    return finish(new_slice, beyond, 3)
+    new_slice, ladder = finish(new_slice, None, across, 2)
+    return finish(new_slice, ladder, beyond, 3)[0]
 
 
 def on_device(hist_lesser, *others):

time: 108 us -> 105 us (0.972)
  waiting for transfers between devices: 20.4 us -> 16.2 us
  blocking collectives: 22.1 us -> 23.5 us
    all_to_all x2 -> x1, waiting for transfers between devices: 12 us -> 5.51 us  [send_alone(): return lax.all_to_all(sent, both_axes, 0, 0, tiled=True)]
    all_to_all x2 -> x3, starting transfers between devices: 4.96 us -> 8.26 us  [send_beside(): arrived = lax.all_to_all(sent, both_axes, 0, 0, tiled=True)]
    all_to_all x2 -> x1, starting transfers between devices: 9.88 us -> 7.09 us  [send_alone(): return lax.all_to_all(sent, both_axes, 0, 0, tiled=True)]
    all_to_all x2 -> x3, waiting for transfers between devices: 5.1 us -> 7.15 us  [send_beside(): arrived = lax.all_to_all(sent, both_axes, 0, 0, tiled=True)]
    ppermute x3, waiting for transfers between devices: 0.01 us -> 1.54 us  [exchange(): return lax.ppermute(x, 'tm', [(t, t ^ step) for t in range(peers)])]
    all_to_all x2, blocking collectives: 22.1 us -> 23.5 us  [send_alone(): return lax.all_to_all(sent, both_axes, 0, 0, tiled=True)]
    ppermute x1, waiting for transfers between devices: 1.47 us -> 0.26 us  [on_device_tiled(): low = lax.ppermute(low, 'tm', neighbours)]
    pallas_call x12 -> x14, Pallas kernels: 38.7 us -> 39.7 us  [the longest x3 17.7 us: send_beside(): pl.pallas_call(final_ladder_kernel, out_shape=[pltpu.HBM(ladder_shape, jn...]
  transfers between devices with their start and end apart: 11 -> 11, of which waited for: 6 -> 7; matrix products, arithmetic and copies ran while one was open for 0% -> 1% of each run, Pallas kernels for 30% -> 31%
where the time goes in v6:
time: 105 us
  Pallas kernels  42.3 us (40%)
  blocking collectives  23.5 us (22%)
  starting transfers between devices  21 us (20%)
  waiting for transfers between devices  16.2 us (15%)
  local copies, waits for them, and re-layouts  1.26 us (1%)
    all_to_all x2, blocking collectives, send_alone(): return lax.all_to_all(sent, both_axes, 0, 0, tiled=True)  23.5 us
    pallas_call x3, Pallas kernels, send_beside(): pl.pallas_call(final_ladder_kernel, out_shape=[pltpu.HBM(ladder_shape, jn...  17.7 us
    pallas_call x4, Pallas kernels, finish(): pl.pallas_call(functools.partial(final_kernel, own, fetched, len(followin...  12.7 us
    all_to_all x3, starting transfers between devices, send_beside(): arrived = lax.all_to_all(sent, both_axes, 0, 0, tiled=True)  8.26 us
    pallas_call x6, Pallas kernels, call(): pl.pallas_call(kernel, out_shape=shapes, in_specs=[SMEM if x.dtype == jnp...  7.55 us
    all_to_all x3, waiting for transfers between devices, send_beside(): arrived = lax.all_to_all(sent, both_axes, 0, 0, tiled=True)  7.15 us
    all_to_all x1, starting transfers between devices, send_alone(): return lax.all_to_all(sent, both_axes, 0, 0, tiled=True)  7.09 us
    all_to_all x1, waiting for transfers between devices, send_alone(): return lax.all_to_all(sent, both_axes, 0, 0, tiled=True)  5.51 us
  transfers between devices with their start and end apart: 11, of which 7 were waited for; matrix products, arithmetic and copies ran while one was open for 1% of the time, Pallas kernels for 31%

profile of v6, /device:TPU:1, one launch (start us, length us, event | category | flops | bytes accessed | tf_op | source)
XLA Modules:
  0.0 104.7 jit_solution(4426199894246510089)
XLA Ops:
  0.0 0.0 copy-start.2
  0.0 0.0 copy-start.3
  0.0 0.0 copy-start.4
  0.0 0.0 copy-start
  0.0 0.0 copy-start.1
  0.0 1.7 %shard_map.82 = (f32[2,16,16,128]{3,2,1,0:T(8,128)S(1)}, f32[2,16,16,128]{3,2,1,0:T(8,128)S(1)}, f32[4,8,16,256]{3,2,1,0:T(8,128)S(1)}, f32[4,8,16,256]{3,2,1,0:T(8,128)S(1)}, f32[4,8,16,256]{3,2,1,0:T(8,128)S(1)}) custom-call(s32[1]{0:T(128)} %bitcast.1.tm_ref, f32[2,32,16,512]{3,2,1,0:T(8,128)} %retarded_ref.5, f32[2,32,16,512]{3,2,1,0:T(8,128)} %lesser_ref.5), custom_call_target="tpu_custom_call" | custom-call | tf_op jit(solution)/shard_map/pallas_call | solution.py:581
  1.7 0.1 collective-permute-start
  1.8 1.2 %copy.12.refs_0_.propagator_ref = f32[2,32,16,16]{3,2,1,0:T(8,128)S(1)} copy(f32[2,32,16,16]{1,3,2,0:T(8,128)} %param.10) | data formatting | bytes 131072 | tf_op args[2]
  3.1 0.3 collective-permute-done.refs_1_
  3.3 1.2 %shard_map.83 = f32[512,128]{1,0:T(8,128)} custom-call(s32[1]{0:T(128)} %bitcast.1.tm_ref, f32[2,32,16,16]{3,2,1,0:T(8,128)S(1)} %copy.12.refs_0_.propagator_ref, f32[2,16,16,128]{3,2,1,0:T(8,128)S(1)} %collective-permute-done.refs_1_, f32[2,16,16,128]{3,2,1,0:T(8,128)S(1)} %get-tuple-element.50.refs_2_), custom_call_target="tpu_custom_call" | custom-call | tf_op jit(solution)/shard_map/pallas_call | solution.py:568
  4.5 7.1 %all-to-all-start = ((f32[32,16,128]{2,1,0:T(8,128)}), f32[32,16,128]{2,1,0:T(8,128)S(1)}, u32[]{:S(2)}, u32[]{:S(2)}) async-start(f32[32,16,128]{2,1,0:T(8,128)} %bitcast.2), calls=%async_computation | async-start | bytes 524288 | tf_op jit(solution)/shard_map/all_to_all | solution.py:646
  11.6 0.3 collective-permute-start.3
  12.0 1.5 %collective-permute-start.1 = (f32[4,8,16,256]{3,2,1,0:T(8,128)S(1)}, f32[4,8,16,256]{3,2,1,0:T(8,128)}, u32[]{:S(2)}, u32[]{:S(2)}) collective-permute-start(f32[4,8,16,256]{3,2,1,0:T(8,128)S(1)} %get-tuple-element.60), channel_id=1, source_target_pairs={{3,0},{0,1},{1,2},{2,3},{7,4},{4,5},{5,6},{6,7},{11,8},{8,9},{9,10... | collective-permute-start | bytes 1572872 | tf_op jit(solution)/shard_map/ppermute | solution.py:599
  13.5 2.3 %collective-permute-start.2 = (f32[4,8,16,256]{3,2,1,0:T(8,128)S(1)}, f32[4,8,16,256]{3,2,1,0:T(8,128)}, u32[]{:S(2)}, u32[]{:S(2)}) collective-permute-start(f32[4,8,16,256]{3,2,1,0:T(8,128)S(1)} %get-tuple-element.61), channel_id=1, source_target_pairs={{3,1},{1,2},{2,3},{0,0},{7,5},{5,6},{6,7},{4,4},{11,9},{9,10},{10,... | collective-permute-start | bytes 1572872 | tf_op jit(solution)/shard_map/ppermute | solution.py:600
  15.8 0.0 copy-done.2
  15.8 0.0 copy-done.3
  15.8 0.0 copy-done.4
  15.8 0.6 shard_map.84
  16.4 5.5 %all-to-all-done = f32[32,16,128]{2,1,0:T(8,128)S(1)} async-done(((f32[32,16,128]{2,1,0:T(8,128)}), f32[32,16,128]{2,1,0:T(8,128)S(1)}, u32[]{:S(2)}, u32[]{:S(2)}) %all-to-all-start) | async-done | bytes 262176 | tf_op jit(solution)/shard_map/all_to_all | solution.py:646
  21.9 0.0 copy-done
  21.9 0.0 copy-done.1
  21.9 1.8 %shard_map.85 = f32[32,16,128]{2,1,0:T(8,128)} custom-call(f32[8,4,16,128]{3,2,1,0:T(8,128)S(1)} %bitcast.17, bf16[512,256]{1,0:T(8,128)(2,1)S(1)} %copy-done, bf16[512,256]{1,0:T(8,128)(2,1)S(1)} %copy-done.1, f32[1,128]{1,0:T(1,128)S(1)} %get-tuple-element.56.strength_ref, f32[1,128]{1,0:T(1,128)S(1)} %get-tuple-element.57.mean_ref), custom_call_target="tpu_custom_call" | custom-call | tf_op jit(solution)/shard_map/pallas_call | solution.py:568
  23.7 2.8 %all-to-all-start.1 = ((f32[32,16,128]{2,1,0:T(8,128)}), f32[32,16,128]{2,1,0:T(8,128)S(1)}, u32[]{:S(2)}, u32[]{:S(2)}) async-start(f32[32,16,128]{2,1,0:T(8,128)} %shard_map.85), calls=%async_computation.1 | async-start | bytes 524288 | tf_op jit(solution)/shard_map/all_to_all | solution.py:623
  26.5 0.1 pad_add_fusion.tm_ref
  26.5 0.0 collective-permute-done.3.others_2_
  26.6 0.0 collective-permute-done.1.others_0_
  26.6 1.7 %collective-permute-done.2.others_1_ = f32[4,8,16,256]{3,2,1,0:T(8,128)} collective-permute-done((f32[4,8,16,256]{3,2,1,0:T(8,128)S(1)}, f32[4,8,16,256]{3,2,1,0:T(8,128)}, u32[]{:S(2)}, u32[]{:S(2)}) %collective-permute-start.2) | collective-permute-done | bytes 524320 | tf_op jit(solution)/shard_map/ppermute | solution.py:600
  28.3 2.1 %shard_map.87 = (bf16[8,256,256]{2,1,0:T(8,128)(2,1)S(1)}, bf16[8,256,256]{2,1,0:T(8,128)(2,1)S(1)}) custom-call(s32[1]{0:T(128)} %bitcast.1.tm_ref, f32[2,32,16,512]{3,2,1,0:T(8,128)} %retarded_ref.5, f32[2,32,16,512]{3,2,1,0:T(8,128)} %lesser_ref.5, f32[4,8,16,256]{3,2,1,0:T(8,128)} %collective-permute-done.1.others_0_, ...), custom_call_target="tpu_custom_call" | custom-call | tf_op jit(solution)/shard_map/pallas_call | solution.py:664
  30.4 5.0 %shard_map.86.ladder_ref = bf16[8,768,256]{2,1,0:T(8,128)(2,1)} custom-call(s32[2]{0:T(128)S(1)} %pad_add_fusion.tm_ref, f32[2,32,16,512]{3,2,1,0:T(8,128)} %retarded_ref.5, f32[2,32,16,512]{3,2,1,0:T(8,128)} %lesser_ref.5, f32[4,8,16,256]{3,2,1,0:T(8,128)} %collective-permute-done.1.others_0_, f32[4,8,16,256]{3,2,1,0:T(8,128)} %collective-permute-done.2.others_1_, ...), custom_call_target="tpu_custom_call" | custom-call | tf_op jit(solution)/shard_map/pallas_call | solution.py:624
  35.3 1.5 %all-to-all-done.1 = f32[32,16,128]{2,1,0:T(8,128)S(1)} async-done(((f32[32,16,128]{2,1,0:T(8,128)}), f32[32,16,128]{2,1,0:T(8,128)S(1)}, u32[]{:S(2)}, u32[]{:S(2)}) %all-to-all-start.1) | async-done | bytes 262176 | tf_op jit(solution)/shard_map/all_to_all | solution.py:623
  36.9 0.5 shard_map.88
  37.4 11.4 %all_to_all.30 = f32[32,8,128]{2,1,0:T(8,128)S(1)} all-to-all(f32[32,8,128]{2,1,0:T(8,128)S(1)} %bitcast.20), channel_id=1, replica_groups=mesh['mom'=8,'tm'=4] {'mom','tm'}, dimensions={0} | all-to-all | bytes 262144 | tf_op jit(solution)/shard_map/all_to_all | solution.py:646
  48.8 1.1 %shard_map.89 = f32[32,16,128]{2,1,0:T(8,128)S(1)} custom-call(f32[8,4,8,128]{3,2,1,0:T(8,128)S(1)} %bitcast.22, bf16[512,256]{1,0:T(8,128)(2,1)S(1)} %copy-done, bf16[512,256]{1,0:T(8,128)(2,1)S(1)} %copy-done.1, f32[1,128]{1,0:T(1,128)S(1)} %get-tuple-element.56.strength_ref, f32[1,128]{1,0:T(1,128)S(1)} %get-tuple-element.57.mean_ref), custom_call_target="tpu_custom_call" | custom-call | tf_op jit(solution)/shard_map/pallas_call | solution.py:568
  49.9 12.1 %all_to_all.31 = f32[32,16,128]{2,1,0:T(8,128)S(1)} all-to-all(f32[32,16,128]{2,1,0:T(8,128)S(1)} %shard_map.89), channel_id=1, replica_groups=mesh['mom'=8,'tm'=4] {'mom','tm'}, dimensions={0} | all-to-all | bytes 524288 | tf_op jit(solution)/shard_map/all_to_all | solution.py:646
  62.0 1.2 %shard_map.90 = f32[256,128]{1,0:T(8,128)} custom-call(f32[512,128]{1,0:T(8,128)S(1)} %bitcast.19, f32[2,8,16,16]{3,2,1,0:T(8,128)S(1)} %constant_dynamic-slice_fusion.propagator_ref, bf16[8,256,256]{2,1,0:T(8,128)(2,1)S(1)} %get-tuple-element.65.high_ref, bf16[8,256,256]{2,1,0:T(8,128)(2,1)S(1)} %get-tuple-element.66.low_ref), custom_call_target="tpu_custom_call" | custom-call | tf_op jit(solution)/shard_map/pallas_call | solution.py:568
  63.2 2.8 %all-to-all-start.4 = ((f32[32,8,128]{2,1,0:T(8,128)}), f32[32,8,128]{2,1,0:T(8,128)S(1)}, u32[]{:S(2)}, u32[]{:S(2)}) async-start(f32[32,8,128]{2,1,0:T(8,128)} %bitcast.9), calls=%async_computation.4 | async-start | bytes 262144 | tf_op jit(solution)/shard_map/all_to_all | solution.py:623
  66.0 0.1 pad_add_fusion.1.tm_ref
  66.0 5.0 %shard_map.91.others_0_ = bf16[8,768,256]{2,1,0:T(8,128)(2,1)} custom-call(s32[2]{0:T(128)S(1)} %pad_add_fusion.1.tm_ref, f32[2,32,16,512]{3,2,1,0:T(8,128)} %retarded_ref.5, f32[2,32,16,512]{3,2,1,0:T(8,128)} %lesser_ref.5, f32[4,8,16,256]{3,2,1,0:T(8,128)} %collective-permute-done.1.others_0_, f32[4,8,16,256]{3,2,1,0:T(8,128)} %collective-permute-done.2.others_1_, ...), custom_call_target="tpu_custom_call" | custom-call | tf_op jit(solution)/shard_map/pallas_call | solution.py:624
  71.0 3.3 %all-to-all-done.4 = f32[32,8,128]{2,1,0:T(8,128)S(1)} async-done(((f32[32,8,128]{2,1,0:T(8,128)}), f32[32,8,128]{2,1,0:T(8,128)S(1)}, u32[]{:S(2)}, u32[]{:S(2)}) %all-to-all-start.4) | async-done | bytes 131104 | tf_op jit(solution)/shard_map/all_to_all | solution.py:623
  74.3 1.8 %shard_map.92 = f32[32,16,128]{2,1,0:T(8,128)} custom-call(f32[8,4,8,128]{3,2,1,0:T(8,128)S(1)} %bitcast.21, bf16[512,256]{1,0:T(8,128)(2,1)S(1)} %copy-done, bf16[512,256]{1,0:T(8,128)(2,1)S(1)} %copy-done.1, f32[1,128]{1,0:T(1,128)S(1)} %get-tuple-element.56.strength_ref, f32[1,128]{1,0:T(1,128)S(1)} %get-tuple-element.57.mean_ref), custom_call_target="tpu_custom_call" | custom-call | tf_op jit(solution)/shard_map/pallas_call | solution.py:568
  76.1 2.7 %all-to-all-start.5 = ((f32[32,16,128]{2,1,0:T(8,128)}), f32[32,16,128]{2,1,0:T(8,128)S(1)}, u32[]{:S(2)}, u32[]{:S(2)}) async-start(f32[32,16,128]{2,1,0:T(8,128)} %shard_map.92), calls=%async_computation.5 | async-start | bytes 524288 | tf_op jit(solution)/shard_map/all_to_all | solution.py:623
  78.8 0.1 pad_add_fusion.2.tm_ref
  78.8 7.8 %shard_map.93 = (bf16[8,768,256]{2,1,0:T(8,128)(2,1)}, bf16[8,768,256]{2,1,0:T(8,128)(2,1)}) custom-call(s32[2]{0:T(128)S(1)} %pad_add_fusion.2.tm_ref, f32[2,32,16,512]{3,2,1,0:T(8,128)} %retarded_ref.5, f32[2,32,16,512]{3,2,1,0:T(8,128)} %lesser_ref.5, f32[4,8,16,256]{3,2,1,0:T(8,128)} %collective-permute-done.1.others_0_, ...), custom_call_target="tpu_custom_call" | custom-call | tf_op jit(solution)/shard_map/pallas_call | solution.py:624
  86.7 2.4 %all-to-all-done.5 = f32[32,16,128]{2,1,0:T(8,128)S(1)} async-done(((f32[32,16,128]{2,1,0:T(8,128)}), f32[32,16,128]{2,1,0:T(8,128)S(1)}, u32[]{:S(2)}, u32[]{:S(2)}) %all-to-all-start.5) | async-done | bytes 262176 | tf_op jit(solution)/shard_map/all_to_all | solution.py:623
  89.0 0.6 collective-permute-start.5
  89.6 0.0 collective-permute-start.4
  89.7 3.9 %shard_map.94 = (f32[2,32,16,512]{3,2,1,0:T(8,128)}, bf16[8,768,256]{2,1,0:T(8,128)(2,1)S(1)}) custom-call(s32[1]{0:T(128)} %bitcast.1.tm_ref, f32[512,128]{1,0:T(8,128)S(1)} %bitcast.16, f32[2,32,16,16]{3,2,1,0:T(8,128)S(1)} %copy.12.refs_0_.propagator_ref, bf16[8,768,256]{2,1,0:T(8,128)(2,1)} %shard_map.86.ladder_ref, bf16[8,768,256]{2,1,0:T(8,128)(2,1)} %shard_map.91.others_0_), custom_call_target="tpu_custom_call" | custom-call | tf_op jit(solution)/shard_map/pallas_call | solution.py:695
  93.5 0.0 collective-permute-done.5.arrived_ref
  93.6 2.5 %shard_map.95.others_1_ = f32[2,32,16,512]{3,2,1,0:T(8,128)} custom-call(s32[1]{0:T(128)} %bitcast.10.tm_ref, f32[512,128]{1,0:T(8,128)S(1)} %collective-permute-done.5.arrived_ref, f32[2,32,16,16]{3,2,1,0:T(8,128)S(1)} %copy.12.refs_0_.propagator_ref, bf16[8,768,256]{2,1,0:T(8,128)(2,1)S(1)} %get-tuple-element.85.ladder_ref, ...), custom_call_target="tpu_custom_call", output_to_operand_aliasing={{}: (4, {})} | custom-call | tf_op jit(solution)/shard_map/pallas_call | solution.py:695
  96.0 1.5 %collective-permute-done.4.arrived_ref = f32[512,128]{1,0:T(8,128)S(1)} collective-permute-done((f32[512,128]{1,0:T(8,128)S(1)}, f32[512,128]{1,0:T(8,128)S(1)}, u32[]{:S(2)}, u32[]{:S(2)}) %collective-permute-start.4) | collective-permute-done | bytes 262176 | tf_op jit(solution)/shard_map/ppermute | solution.py:707
  97.6 0.8 collective-permute-start.6
  98.4 3.9 %shard_map.96 = (f32[2,32,16,512]{3,2,1,0:T(8,128)}, bf16[8,768,256]{2,1,0:T(8,128)(2,1)S(1)}) custom-call(s32[1]{0:T(128)} %bitcast.12.tm_ref, f32[512,128]{1,0:T(8,128)S(1)} %collective-permute-done.4.arrived_ref, f32[2,32,16,16]{3,2,1,0:T(8,128)S(1)} %copy.12.refs_0_.propagator_ref, ...), custom_call_target="tpu_custom_call", output_to_operand_aliasing={{0}: (5, {})} | custom-call | tf_op jit(solution)/shard_map/pallas_call | solution.py:695
  102.2 0.0 collective-permute-done.6.arrived_ref
  102.2 2.5 %shard_map.97 = f32[2,32,16,512]{3,2,1,0:T(8,128)} custom-call(s32[1]{0:T(128)} %bitcast.tm_ref, f32[512,128]{1,0:T(8,128)S(1)} %collective-permute-done.6.arrived_ref, f32[2,32,16,16]{3,2,1,0:T(8,128)S(1)} %copy.12.refs_0_.propagator_ref, bf16[8,768,256]{2,1,0:T(8,128)(2,1)S(1)} %get-tuple-element.91.ladder_ref, ...), custom_call_target="tpu_custom_call", output_to_operand_aliasing={{}: (4, {})} | custom-call | tf_op jit(solution)/shard_map/pallas_call | solution.py:695
  (1 shorter events, 0.0 us)
Async XLA Ops:
  0.0 15.8 %copy-start.2 = (f32[256]{0:T(256)S(1)}, f32[256]{0:T(256)}, u32[]{:S(2)}) copy-start(f32[256]{0:T(256)} %coupling_ref) | copy-start | bytes 3076
  0.0 15.8 %copy-start.3 = (f32[256]{0:T(256)S(1)}, f32[256]{0:T(256)}, u32[]{:S(2)}) copy-start(f32[256]{0:T(256)} %mf_ref) | copy-start | bytes 3076
  0.0 15.8 %copy-start.4 = (f32[8]{0:T(128)S(1)}, f32[8]{0:T(128)}, u32[]{:S(2)}) copy-start(f32[8]{0:T(128)} %lag_ref) | copy-start | bytes 100
  0.0 21.9 %copy-start = (bf16[512,256]{1,0:T(8,128)(2,1)S(1)}, bf16[512,256]{1,0:T(8,128)(2,1)}, u32[]{:S(2)}) copy-start(bf16[512,256]{1,0:T(8,128)(2,1)} %constant.27.clone.high_ref) | copy-start | bytes 786436
  0.0 21.9 %copy-start.1 = (bf16[512,256]{1,0:T(8,128)(2,1)S(1)}, bf16[512,256]{1,0:T(8,128)(2,1)}, u32[]{:S(2)}) copy-start(bf16[512,256]{1,0:T(8,128)(2,1)} %constant.28.clone.low_ref) | copy-start | bytes 786436
  1.7 1.6 %collective-permute-start = (f32[2,16,16,128]{3,2,1,0:T(8,128)S(1)}, f32[2,16,16,128]{3,2,1,0:T(8,128)S(1)}, u32[]{:S(2)}, u32[]{:S(2)}) collective-permute-start(f32[2,16,16,128]{3,2,1,0:T(8,128)S(1)} %get-tuple-element.49), channel_id=1, source_target_pairs={{0,1},{1,0},{2,3},{3,2},{4,5},{5,4},{6,7},{7,6},{8,9},{9,8},{10,11... | collective-permute-start | bytes 786440 | tf_op jit(solution)/shard_map/ppermute | solution.py:590
  4.5 17.4 %all-to-all-start = ((f32[32,16,128]{2,1,0:T(8,128)}), f32[32,16,128]{2,1,0:T(8,128)S(1)}, u32[]{:S(2)}, u32[]{:S(2)}) async-start(f32[32,16,128]{2,1,0:T(8,128)} %bitcast.2), calls=%async_computation | async-start | bytes 524288 | tf_op jit(solution)/shard_map/all_to_all | solution.py:646
  11.6 14.9 %collective-permute-start.3 = (f32[4,8,16,256]{3,2,1,0:T(8,128)S(1)}, f32[4,8,16,256]{3,2,1,0:T(8,128)}, u32[]{:S(2)}, u32[]{:S(2)}) collective-permute-start(f32[4,8,16,256]{3,2,1,0:T(8,128)S(1)} %get-tuple-element.62), channel_id=1, source_target_pairs={{0,1},{1,0},{2,3},{3,2},{4,5},{5,4},{6,7},{7,6},{8,9},{9,8},{10,11... | collective-permute-start | bytes 1572872 | tf_op jit(solution)/shard_map/ppermute | solution.py:604
  12.0 14.6 %collective-permute-start.1 = (f32[4,8,16,256]{3,2,1,0:T(8,128)S(1)}, f32[4,8,16,256]{3,2,1,0:T(8,128)}, u32[]{:S(2)}, u32[]{:S(2)}) collective-permute-start(f32[4,8,16,256]{3,2,1,0:T(8,128)S(1)} %get-tuple-element.60), channel_id=1, source_target_pairs={{3,0},{0,1},{1,2},{2,3},{7,4},{4,5},{5,6},{6,7},{11,8},{8,9},{9,10... | collective-permute-start | bytes 1572872 | tf_op jit(solution)/shard_map/ppermute | solution.py:599
  13.5 14.8 %collective-permute-start.2 = (f32[4,8,16,256]{3,2,1,0:T(8,128)S(1)}, f32[4,8,16,256]{3,2,1,0:T(8,128)}, u32[]{:S(2)}, u32[]{:S(2)}) collective-permute-start(f32[4,8,16,256]{3,2,1,0:T(8,128)S(1)} %get-tuple-element.61), channel_id=1, source_target_pairs={{3,1},{1,2},{2,3},{0,0},{7,5},{5,6},{6,7},{4,4},{11,9},{9,10},{10,... | collective-permute-start | bytes 1572872 | tf_op jit(solution)/shard_map/ppermute | solution.py:600
  23.7 13.2 %all-to-all-start.1 = ((f32[32,16,128]{2,1,0:T(8,128)}), f32[32,16,128]{2,1,0:T(8,128)S(1)}, u32[]{:S(2)}, u32[]{:S(2)}) async-start(f32[32,16,128]{2,1,0:T(8,128)} %shard_map.85), calls=%async_computation.1 | async-start | bytes 524288 | tf_op jit(solution)/shard_map/all_to_all | solution.py:623
  63.2 11.1 %all-to-all-start.4 = ((f32[32,8,128]{2,1,0:T(8,128)}), f32[32,8,128]{2,1,0:T(8,128)S(1)}, u32[]{:S(2)}, u32[]{:S(2)}) async-start(f32[32,8,128]{2,1,0:T(8,128)} %bitcast.9), calls=%async_computation.4 | async-start | bytes 262144 | tf_op jit(solution)/shard_map/all_to_all | solution.py:623
  76.1 13.0 %all-to-all-start.5 = ((f32[32,16,128]{2,1,0:T(8,128)}), f32[32,16,128]{2,1,0:T(8,128)S(1)}, u32[]{:S(2)}, u32[]{:S(2)}) async-start(f32[32,16,128]{2,1,0:T(8,128)} %shard_map.92), calls=%async_computation.5 | async-start | bytes 524288 | tf_op jit(solution)/shard_map/all_to_all | solution.py:623
  89.0 4.5 %collective-permute-start.5 = (f32[512,128]{1,0:T(8,128)S(1)}, f32[512,128]{1,0:T(8,128)S(1)}, u32[]{:S(2)}, u32[]{:S(2)}) collective-permute-start(f32[512,128]{1,0:T(8,128)S(1)} %bitcast.14), channel_id=1, source_target_pairs={{0,1},{1,0},{2,3},{3,2},{4,5},{5,4},{6,7},{7,6},{8,9},{9,8},{10,11... | collective-permute-start | bytes 786440 | tf_op jit(solution)/shard_map/ppermute | solution.py:707
  89.6 7.9 %collective-permute-start.4 = (f32[512,128]{1,0:T(8,128)S(1)}, f32[512,128]{1,0:T(8,128)S(1)}, u32[]{:S(2)}, u32[]{:S(2)}) collective-permute-start(f32[512,128]{1,0:T(8,128)S(1)} %bitcast.15), channel_id=1, source_target_pairs={{0,2},{1,3},{2,0},{3,1},{4,6},{5,7},{6,4},{7,5},{8,10},{9,11},{10,... | collective-permute-start | bytes 786440 | tf_op jit(solution)/shard_map/ppermute | solution.py:707
  97.6 4.7 %collective-permute-start.6 = (f32[512,128]{1,0:T(8,128)S(1)}, f32[512,128]{1,0:T(8,128)S(1)}, u32[]{:S(2)}, u32[]{:S(2)}) collective-permute-start(f32[512,128]{1,0:T(8,128)S(1)} %collective-permute-done.4.arrived_ref), channel_id=1, source_target_pairs={{0,1},{1,0},{2,3},{3,2},{4,5},{5,4},{6,7},{7,6},{8,9},{9,8},{10,11... | collective-permute-start | bytes 786440 | tf_op jit(solution)/shard_map/ppermute | solution.py:707

commit v7 on v6

--- a/solution.py
+++ b/solution.py
@@ -403,7 +403,7 @@
     return tiles
 
 
-def final_ladder_kernel(tm_ref, retarded_ref, lesser_ref, *others):
+def final_ladder_kernel(tm_ref, retarded_ref, lesser_ref, *others, meanwhile=lambda: None):
     *others, region_ref, ladder_ref, arrive, arrive_rim, leave = others
     rim_refs, outs = others[:3], others[3:]
     count, rows_each = ladder_ref.shape[0], ladder_ref.shape[1] // 2
@@ -437,13 +437,17 @@
     def _():
         region_ref[:, :, :, :TILE] = jnp.zeros((4, count, ORB, TILE), jnp.float32)
 
-    for second, case in ((2, tm_ref[0] == 1), (1, tm_ref[0] > 1)):
-        for quarters in [(0, 1)] if blocks == 2 else [(0,), (1,)]:
-
-            @pl.when(case if blocks == 2 else case & (tm_ref[1] % 2 == quarters[0]))
-            def _():
-                wait_all(start_all(rims(second, quarters)))
-
+    def each_rims(act):
+        for second, case in ((2, tm_ref[0] == 1), (1, tm_ref[0] > 1)):
+            for quarters in [(0, 1)] if blocks == 2 else [(0,), (1,)]:
+
+                @pl.when(case if blocks == 2 else case & (tm_ref[1] % 2 == quarters[0]))
+                def _():
+                    act(rims(second, quarters))
+
+    each_rims(start_all)
+    meanwhile()
+    each_rims(wait_all)
     wait_all(fetches)
 
     def leaving(block, n):
@@ -477,6 +481,13 @@
         lax.fori_loop(0, own, functools.partial(one, block), 0)
     for block in range(blocks):
         lax.fori_loop(0, own, lambda n, c: (wait_all(leaving(block, n)), c)[1], 0)
+
+
+def both_ladders_kernel(own, tm_ref, retarded_ref, lesser_ref, *others):
+    regions, outs, near, others = others[:3], others[3:6], others[6:8], others[8:]
+    histories = (tm_ref, retarded_ref, lesser_ref, *regions)
+    window = functools.partial(window_ladder_kernel, own, *histories, *outs[:2], *near)
+    final_ladder_kernel(*histories, outs[2], *others, meanwhile=window)
 
 
 def stepped(pair):
@@ -616,23 +627,24 @@
     ladders = {}
     ladder_shape = (own, 2 * 3 * TILE, 2 * TILE)
 
+    def ladder_scratch(blocks):
+        return [
+            pltpu.VMEM((4, blocks * own, ORB, TILE + columns), jnp.float32),
+            pltpu.VMEM((blocks * own, *ladder_shape[1:]), jnp.bfloat16),
+            pltpu.SemaphoreType.DMA((2,)),
+            pltpu.SemaphoreType.DMA((4, 2)),
+            pltpu.SemaphoreType.DMA((blocks * own,)),
+        ]
+
     def send_beside(sent, step, blocks):
-        edges = [hist_retarded, hist_lesser, *near]
-        if step:
-            sent, *edges = lax.optimization_barrier((sent, *edges))
+        sent, *edges = lax.optimization_barrier((sent, hist_retarded, hist_lesser, *near))
         arrived = lax.all_to_all(sent, both_axes, 0, 0, tiled=True)
         ladder = pl.pallas_call(
             final_ladder_kernel,
             out_shape=[pltpu.HBM(ladder_shape, jnp.bfloat16)] * blocks,
             in_specs=[SMEM] + [IN_HBM] * 5,
             out_specs=[IN_HBM] * blocks,
-            scratch_shapes=[
-                pltpu.VMEM((4, blocks * own, ORB, TILE + columns), jnp.float32),
-                pltpu.VMEM((blocks * own, *ladder_shape[1:]), jnp.bfloat16),
-                pltpu.SemaphoreType.DMA((2,)),
-                pltpu.SemaphoreType.DMA((4, 2)),
-                pltpu.SemaphoreType.DMA((blocks * own,)),
-            ],
+            scratch_shapes=ladder_scratch(blocks),
             compiler_params=limit(6 * blocks),
         )(
             jnp.stack([here, here ^ step]).astype(jnp.int32),
@@ -646,7 +658,7 @@
         return lax.all_to_all(sent, both_axes, 0, 0, tiled=True)
 
     send_out = [send_alone, send_alone, lambda sent: send_beside(sent, 1, 1)]
-    send_back = [lambda sent: send_beside(sent, 0, 1), send_alone, lambda sent: send_beside(sent, 2, 2)]
+    send_back = [send_alone, send_alone, lambda sent: send_beside(sent, 2, 2)]
     for sweep in range(PASSES):
         arrived = send_out[sweep](send)
         back = call(
@@ -661,14 +673,22 @@
         if sweep == 0:
             near[2], _ = lax.optimization_barrier((near[2], back))
             rungs = bf16((own, 2 * TILE, 2 * TILE))
-            rungs = pl.pallas_call(
-                functools.partial(window_ladder_kernel, own),
-                out_shape=(rungs, rungs),
+            *rungs, ladders[0] = pl.pallas_call(
+                functools.partial(both_ladders_kernel, own),
+                out_shape=(rungs, rungs, pltpu.HBM(ladder_shape, jnp.bfloat16)),
                 in_specs=[SMEM] + [IN_HBM] * 5,
-                out_specs=(VMEM, VMEM),
-                scratch_shapes=[pltpu.VMEM(near_shape.shape, jnp.float32), pltpu.SemaphoreType.DMA((2,))],
-                compiler_params=limit(8),
-            )(here_array, *histories, *[pltpu.with_memory_space_constraint(x, pltpu.HBM) for x in near])
+                out_specs=(VMEM, VMEM, IN_HBM),
+                scratch_shapes=[
+                    pltpu.VMEM(near_shape.shape, jnp.float32),
+                    pltpu.SemaphoreType.DMA((2,)),
+                    *ladder_scratch(1),
+                ],
+                compiler_params=limit(10),
+            )(
+                jnp.stack([here, here]).astype(jnp.int32),
+                *histories,
+                *[pltpu.with_memory_space_constraint(x, pltpu.HBM) for x in near],
+            )
             propagator_own = own_block(propagator, own, 1)
         arrived = send_back[sweep](back)
         arrived = arrived.reshape(2 * count, TILE)

time: 105 us -> 104 us (level)
    pallas_call x3 -> x2, Pallas kernels: 17.7 us -> 12.8 us  [send_beside(): pl.pallas_call(final_ladder_kernel, out_shape=[pltpu.HBM(ladder_shape, jn...]
    pallas_call x1, Pallas kernels: 2.07 us -> 6.24 us  [on_device_tiled(): pl.pallas_call(functools.partial(both_ladders_kernel, own), out_shape=(ru...]
    all_to_all x3 -> x2, starting transfers between devices: 8.26 us -> 5.47 us  [send_beside(): arrived = lax.all_to_all(sent, both_axes, 0, 0, tiled=True)]
    all_to_all x1 -> x2, starting transfers between devices: 7.09 us -> 9.87 us  [send_alone(): return lax.all_to_all(sent, both_axes, 0, 0, tiled=True)]
    all_to_all x1 -> x2, waiting for transfers between devices: 5.51 us -> 7.81 us  [send_alone(): return lax.all_to_all(sent, both_axes, 0, 0, tiled=True)]
    all_to_all x3 -> x2, waiting for transfers between devices: 7.15 us -> 5.74 us  [send_beside(): arrived = lax.all_to_all(sent, both_axes, 0, 0, tiled=True)]
  transfers between devices with their start and end apart: 11 -> 11, of which waited for: 7 -> 7; matrix products, arithmetic and copies ran while one was open for 1% -> 1% of each run, Pallas kernels for 31% -> 30%
where the time goes in v7:
time: 104 us
  Pallas kernels  41.5 us (40%)
  blocking collectives  22.7 us (22%)
  starting transfers between devices  21 us (20%)
  waiting for transfers between devices  17.1 us (16%)
  local copies, waits for them, and re-layouts  1.26 us (1%)
    all_to_all x2, blocking collectives, send_alone(): return lax.all_to_all(sent, both_axes, 0, 0, tiled=True)  22.7 us
    pallas_call x2, Pallas kernels, send_beside(): pl.pallas_call(final_ladder_kernel, out_shape=[pltpu.HBM(ladder_shape, jn...  12.8 us
    pallas_call x4, Pallas kernels, finish(): pl.pallas_call(functools.partial(final_kernel, own, fetched, len(followin...  12.7 us
    all_to_all x2, starting transfers between devices, send_alone(): return lax.all_to_all(sent, both_axes, 0, 0, tiled=True)  9.87 us
    all_to_all x2, waiting for transfers between devices, send_alone(): return lax.all_to_all(sent, both_axes, 0, 0, tiled=True)  7.81 us
    pallas_call x6, Pallas kernels, call(): pl.pallas_call(kernel, out_shape=shapes, in_specs=[SMEM if x.dtype == jnp...  7.54 us
    pallas_call x1, Pallas kernels, on_device_tiled(): pl.pallas_call(functools.partial(both_ladders_kernel, own), out_shape=(ru...  6.24 us
    all_to_all x2, waiting for transfers between devices, send_beside(): arrived = lax.all_to_all(sent, both_axes, 0, 0, tiled=True)  5.74 us
  transfers between devices with their start and end apart: 11, of which 7 were waited for; matrix products, arithmetic and copies ran while one was open for 1% of the time, Pallas kernels for 30%

profile of v7, /device:TPU:1, one launch (start us, length us, event | category | flops | bytes accessed | tf_op | source)
XLA Modules:
  0.0 103.9 jit_solution(12632596885768280793)
XLA Ops:
  0.0 0.0 copy-start.2
  0.0 0.0 copy-start.3
  0.0 0.0 copy-start.4
  0.0 0.0 copy-start
  0.0 0.0 copy-start.1
  0.0 1.7 %shard_map.82 = (f32[2,16,16,128]{3,2,1,0:T(8,128)S(1)}, f32[2,16,16,128]{3,2,1,0:T(8,128)S(1)}, f32[4,8,16,256]{3,2,1,0:T(8,128)S(1)}, f32[4,8,16,256]{3,2,1,0:T(8,128)S(1)}, f32[4,8,16,256]{3,2,1,0:T(8,128)S(1)}) custom-call(s32[1]{0:T(128)} %bitcast.1.tm_ref, f32[2,32,16,512]{3,2,1,0:T(8,128)} %retarded_ref.4, f32[2,32,16,512]{3,2,1,0:T(8,128)} %lesser_ref.4), custom_call_target="tpu_custom_call" | custom-call | tf_op jit(solution)/shard_map/pallas_call | solution.py:592
  1.7 0.1 collective-permute-start
  1.8 1.2 %copy.12.refs_0_.propagator_ref = f32[2,32,16,16]{3,2,1,0:T(8,128)S(1)} copy(f32[2,32,16,16]{1,3,2,0:T(8,128)} %param.10) | data formatting | bytes 131072 | tf_op args[2]
  3.1 0.3 collective-permute-done.refs_1_
  3.3 1.2 %shard_map.83 = f32[512,128]{1,0:T(8,128)} custom-call(s32[1]{0:T(128)} %bitcast.1.tm_ref, f32[2,32,16,16]{3,2,1,0:T(8,128)S(1)} %copy.12.refs_0_.propagator_ref, f32[2,16,16,128]{3,2,1,0:T(8,128)S(1)} %collective-permute-done.refs_1_, f32[2,16,16,128]{3,2,1,0:T(8,128)S(1)} %get-tuple-element.49.refs_2_), custom_call_target="tpu_custom_call" | custom-call | tf_op jit(solution)/shard_map/pallas_call | solution.py:579
  4.5 7.1 %all-to-all-start = ((f32[32,16,128]{2,1,0:T(8,128)}), f32[32,16,128]{2,1,0:T(8,128)S(1)}, u32[]{:S(2)}, u32[]{:S(2)}) async-start(f32[32,16,128]{2,1,0:T(8,128)} %bitcast.2), calls=%async_computation | async-start | bytes 524288 | tf_op jit(solution)/shard_map/all_to_all | solution.py:658
  11.6 0.3 collective-permute-start.3
  12.0 1.5 %collective-permute-start.1 = (f32[4,8,16,256]{3,2,1,0:T(8,128)S(1)}, f32[4,8,16,256]{3,2,1,0:T(8,128)}, u32[]{:S(2)}, u32[]{:S(2)}) collective-permute-start(f32[4,8,16,256]{3,2,1,0:T(8,128)S(1)} %get-tuple-element.59), channel_id=1, source_target_pairs={{3,0},{0,1},{1,2},{2,3},{7,4},{4,5},{5,6},{6,7},{11,8},{8,9},{9,10... | collective-permute-start | bytes 1572872 | tf_op jit(solution)/shard_map/ppermute | solution.py:610
  13.5 2.3 %collective-permute-start.2 = (f32[4,8,16,256]{3,2,1,0:T(8,128)S(1)}, f32[4,8,16,256]{3,2,1,0:T(8,128)}, u32[]{:S(2)}, u32[]{:S(2)}) collective-permute-start(f32[4,8,16,256]{3,2,1,0:T(8,128)S(1)} %get-tuple-element.60), channel_id=1, source_target_pairs={{3,1},{1,2},{2,3},{0,0},{7,5},{5,6},{6,7},{4,4},{11,9},{9,10},{10,... | collective-permute-start | bytes 1572872 | tf_op jit(solution)/shard_map/ppermute | solution.py:611
  15.8 0.0 copy-done.2
  15.8 0.0 copy-done.3
  15.8 0.0 copy-done.4
  15.8 0.6 shard_map.84
  16.4 5.5 %all-to-all-done = f32[32,16,128]{2,1,0:T(8,128)S(1)} async-done(((f32[32,16,128]{2,1,0:T(8,128)}), f32[32,16,128]{2,1,0:T(8,128)S(1)}, u32[]{:S(2)}, u32[]{:S(2)}) %all-to-all-start) | async-done | bytes 262176 | tf_op jit(solution)/shard_map/all_to_all | solution.py:658
  21.9 0.0 copy-done
  21.9 0.0 copy-done.1
  21.9 1.8 %shard_map.85 = f32[32,16,128]{2,1,0:T(8,128)} custom-call(f32[8,4,16,128]{3,2,1,0:T(8,128)S(1)} %bitcast.18, bf16[512,256]{1,0:T(8,128)(2,1)S(1)} %copy-done, bf16[512,256]{1,0:T(8,128)(2,1)S(1)} %copy-done.1, f32[1,128]{1,0:T(1,128)S(1)} %get-tuple-element.55.strength_ref, f32[1,128]{1,0:T(1,128)S(1)} %get-tuple-element.56.mean_ref), custom_call_target="tpu_custom_call" | custom-call | tf_op jit(solution)/shard_map/pallas_call | solution.py:579
  23.7 2.8 %all-to-all-start.1 = ((f32[32,16,128]{2,1,0:T(8,128)}), f32[32,16,128]{2,1,0:T(8,128)S(1)}, u32[]{:S(2)}, u32[]{:S(2)}) async-start(f32[32,16,128]{2,1,0:T(8,128)} %shard_map.85), calls=%async_computation.1 | async-start | bytes 524288 | tf_op jit(solution)/shard_map/all_to_all | solution.py:658
  26.5 0.1 pad_add_fusion
  26.6 0.0 collective-permute-done.3.others_2_
  26.6 0.0 collective-permute-done.1.others_0_
  26.6 1.7 %collective-permute-done.2.others_1_ = f32[4,8,16,256]{3,2,1,0:T(8,128)} collective-permute-done((f32[4,8,16,256]{3,2,1,0:T(8,128)S(1)}, f32[4,8,16,256]{3,2,1,0:T(8,128)}, u32[]{:S(2)}, u32[]{:S(2)}) %collective-permute-start.2) | collective-permute-done | bytes 524320 | tf_op jit(solution)/shard_map/ppermute | solution.py:611
  28.3 6.2 %shard_map.86 = (bf16[8,256,256]{2,1,0:T(8,128)(2,1)S(1)}, bf16[8,256,256]{2,1,0:T(8,128)(2,1)S(1)}, bf16[8,768,256]{2,1,0:T(8,128)(2,1)}) custom-call(s32[2]{0:T(128)S(1)} %get-tuple-element.91.tm_ref, f32[2,32,16,512]{3,2,1,0:T(8,128)} %retarded_ref.4, f32[2,32,16,512]{3,2,1,0:T(8,128)} %lesser_ref.4, f32[4,8,16,256]{3,2,1,0:T(8,128)} %collective-permute-done.1.others_0_, ...), custom_call_target="tpu_custom_call" | custom-call | tf_op jit(solution)/shard_map/pallas_call | solution.py:676
  34.6 2.3 %all-to-all-done.1 = f32[32,16,128]{2,1,0:T(8,128)S(1)} async-done(((f32[32,16,128]{2,1,0:T(8,128)}), f32[32,16,128]{2,1,0:T(8,128)S(1)}, u32[]{:S(2)}, u32[]{:S(2)}) %all-to-all-start.1) | async-done | bytes 262176 | tf_op jit(solution)/shard_map/all_to_all | solution.py:658
  36.9 0.5 shard_map.87
  37.4 10.6 %all_to_all.30 = f32[32,8,128]{2,1,0:T(8,128)S(1)} all-to-all(f32[32,8,128]{2,1,0:T(8,128)S(1)} %bitcast.20), channel_id=1, replica_groups=mesh['mom'=8,'tm'=4] {'mom','tm'}, dimensions={0} | all-to-all | bytes 262144 | tf_op jit(solution)/shard_map/all_to_all | solution.py:658
  48.1 1.1 %shard_map.88 = f32[32,16,128]{2,1,0:T(8,128)S(1)} custom-call(f32[8,4,8,128]{3,2,1,0:T(8,128)S(1)} %bitcast.22, bf16[512,256]{1,0:T(8,128)(2,1)S(1)} %copy-done, bf16[512,256]{1,0:T(8,128)(2,1)S(1)} %copy-done.1, f32[1,128]{1,0:T(1,128)S(1)} %get-tuple-element.55.strength_ref, f32[1,128]{1,0:T(1,128)S(1)} %get-tuple-element.56.mean_ref), custom_call_target="tpu_custom_call" | custom-call | tf_op jit(solution)/shard_map/pallas_call | solution.py:579
  49.1 12.1 %all_to_all.31 = f32[32,16,128]{2,1,0:T(8,128)S(1)} all-to-all(f32[32,16,128]{2,1,0:T(8,128)S(1)} %shard_map.88), channel_id=1, replica_groups=mesh['mom'=8,'tm'=4] {'mom','tm'}, dimensions={0} | all-to-all | bytes 524288 | tf_op jit(solution)/shard_map/all_to_all | solution.py:658
  61.2 1.2 %shard_map.89 = f32[256,128]{1,0:T(8,128)} custom-call(f32[512,128]{1,0:T(8,128)S(1)} %bitcast.19, f32[2,8,16,16]{3,2,1,0:T(8,128)S(1)} %constant_dynamic-slice_fusion.propagator_ref, bf16[8,256,256]{2,1,0:T(8,128)(2,1)S(1)} %get-tuple-element.63.high_ref, bf16[8,256,256]{2,1,0:T(8,128)(2,1)S(1)} %get-tuple-element.64.low_ref), custom_call_target="tpu_custom_call" | custom-call | tf_op jit(solution)/shard_map/pallas_call | solution.py:579
  62.4 2.8 %all-to-all-start.4 = ((f32[32,8,128]{2,1,0:T(8,128)}), f32[32,8,128]{2,1,0:T(8,128)S(1)}, u32[]{:S(2)}, u32[]{:S(2)}) async-start(f32[32,8,128]{2,1,0:T(8,128)} %bitcast.9), calls=%async_computation.4 | async-start | bytes 262144 | tf_op jit(solution)/shard_map/all_to_all | solution.py:641
  65.2 0.1 pad_add_fusion.1.tm_ref
  65.3 5.0 %shard_map.90.others_0_ = bf16[8,768,256]{2,1,0:T(8,128)(2,1)} custom-call(s32[2]{0:T(128)S(1)} %pad_add_fusion.1.tm_ref, f32[2,32,16,512]{3,2,1,0:T(8,128)} %retarded_ref.4, f32[2,32,16,512]{3,2,1,0:T(8,128)} %lesser_ref.4, f32[4,8,16,256]{3,2,1,0:T(8,128)} %collective-permute-done.1.others_0_, f32[4,8,16,256]{3,2,1,0:T(8,128)} %collective-permute-done.2.others_1_, ...), custom_call_target="tpu_custom_call" | custom-call | tf_op jit(solution)/shard_map/pallas_call | solution.py:642
  70.2 3.3 %all-to-all-done.4 = f32[32,8,128]{2,1,0:T(8,128)S(1)} async-done(((f32[32,8,128]{2,1,0:T(8,128)}), f32[32,8,128]{2,1,0:T(8,128)S(1)}, u32[]{:S(2)}, u32[]{:S(2)}) %all-to-all-start.4) | async-done | bytes 131104 | tf_op jit(solution)/shard_map/all_to_all | solution.py:641
  73.5 1.8 %shard_map.91 = f32[32,16,128]{2,1,0:T(8,128)} custom-call(f32[8,4,8,128]{3,2,1,0:T(8,128)S(1)} %bitcast.21, bf16[512,256]{1,0:T(8,128)(2,1)S(1)} %copy-done, bf16[512,256]{1,0:T(8,128)(2,1)S(1)} %copy-done.1, f32[1,128]{1,0:T(1,128)S(1)} %get-tuple-element.55.strength_ref, f32[1,128]{1,0:T(1,128)S(1)} %get-tuple-element.56.mean_ref), custom_call_target="tpu_custom_call" | custom-call | tf_op jit(solution)/shard_map/pallas_call | solution.py:579
  75.3 2.7 %all-to-all-start.5 = ((f32[32,16,128]{2,1,0:T(8,128)}), f32[32,16,128]{2,1,0:T(8,128)S(1)}, u32[]{:S(2)}, u32[]{:S(2)}) async-start(f32[32,16,128]{2,1,0:T(8,128)} %shard_map.91), calls=%async_computation.5 | async-start | bytes 524288 | tf_op jit(solution)/shard_map/all_to_all | solution.py:641
  78.0 7.8 %shard_map.92 = (bf16[8,768,256]{2,1,0:T(8,128)(2,1)}, bf16[8,768,256]{2,1,0:T(8,128)(2,1)}) custom-call(s32[2]{0:T(128)S(1)} %get-tuple-element.92.tm_ref, f32[2,32,16,512]{3,2,1,0:T(8,128)} %retarded_ref.4, f32[2,32,16,512]{3,2,1,0:T(8,128)} %lesser_ref.4, f32[4,8,16,256]{3,2,1,0:T(8,128)} %collective-permute-done.1.others_0_, ...), custom_call_target="tpu_custom_call" | custom-call | tf_op jit(solution)/shard_map/pallas_call | solution.py:642
  85.8 2.5 %all-to-all-done.5 = f32[32,16,128]{2,1,0:T(8,128)S(1)} async-done(((f32[32,16,128]{2,1,0:T(8,128)}), f32[32,16,128]{2,1,0:T(8,128)S(1)}, u32[]{:S(2)}, u32[]{:S(2)}) %all-to-all-start.5) | async-done | bytes 262176 | tf_op jit(solution)/shard_map/all_to_all | solution.py:641
  88.3 0.6 collective-permute-start.5
  88.9 0.0 collective-permute-start.4
  88.9 3.9 %shard_map.93 = (f32[2,32,16,512]{3,2,1,0:T(8,128)}, bf16[8,768,256]{2,1,0:T(8,128)(2,1)S(1)}) custom-call(s32[1]{0:T(128)} %bitcast.1.tm_ref, f32[512,128]{1,0:T(8,128)S(1)} %bitcast.16, f32[2,32,16,16]{3,2,1,0:T(8,128)S(1)} %copy.12.refs_0_.propagator_ref, bf16[8,768,256]{2,1,0:T(8,128)(2,1)} %get-tuple-element.81.ladder_ref, ...), custom_call_target="tpu_custom_call" | custom-call | tf_op jit(solution)/shard_map/pallas_call | solution.py:715
  92.8 0.0 collective-permute-done.5.arrived_ref
  92.8 2.5 %shard_map.94.others_1_ = f32[2,32,16,512]{3,2,1,0:T(8,128)} custom-call(s32[1]{0:T(128)} %bitcast.10.tm_ref, f32[512,128]{1,0:T(8,128)S(1)} %collective-permute-done.5.arrived_ref, f32[2,32,16,16]{3,2,1,0:T(8,128)S(1)} %copy.12.refs_0_.propagator_ref, bf16[8,768,256]{2,1,0:T(8,128)(2,1)S(1)} %get-tuple-element.83.ladder_ref, ...), custom_call_target="tpu_custom_call", output_to_operand_aliasing={{}: (4, {})} | custom-call | tf_op jit(solution)/shard_map/pallas_call | solution.py:715
  95.3 1.5 %collective-permute-done.4.arrived_ref = f32[512,128]{1,0:T(8,128)S(1)} collective-permute-done((f32[512,128]{1,0:T(8,128)S(1)}, f32[512,128]{1,0:T(8,128)S(1)}, u32[]{:S(2)}, u32[]{:S(2)}) %collective-permute-start.4) | collective-permute-done | bytes 262176 | tf_op jit(solution)/shard_map/ppermute | solution.py:727
  96.8 0.8 collective-permute-start.6
  97.6 3.9 %shard_map.95 = (f32[2,32,16,512]{3,2,1,0:T(8,128)}, bf16[8,768,256]{2,1,0:T(8,128)(2,1)S(1)}) custom-call(s32[1]{0:T(128)} %bitcast.12.tm_ref, f32[512,128]{1,0:T(8,128)S(1)} %collective-permute-done.4.arrived_ref, f32[2,32,16,16]{3,2,1,0:T(8,128)S(1)} %copy.12.refs_0_.propagator_ref, ...), custom_call_target="tpu_custom_call", output_to_operand_aliasing={{0}: (5, {})} | custom-call | tf_op jit(solution)/shard_map/pallas_call | solution.py:715
  101.5 0.0 collective-permute-done.6.arrived_ref
  101.5 2.5 %shard_map.96 = f32[2,32,16,512]{3,2,1,0:T(8,128)} custom-call(s32[1]{0:T(128)} %bitcast.tm_ref, f32[512,128]{1,0:T(8,128)S(1)} %collective-permute-done.6.arrived_ref, f32[2,32,16,16]{3,2,1,0:T(8,128)S(1)} %copy.12.refs_0_.propagator_ref, bf16[8,768,256]{2,1,0:T(8,128)(2,1)S(1)} %get-tuple-element.89.ladder_ref, ...), custom_call_target="tpu_custom_call", output_to_operand_aliasing={{}: (4, {})} | custom-call | tf_op jit(solution)/shard_map/pallas_call | solution.py:715
  (1 shorter events, 0.0 us)
Async XLA Ops:
  0.0 15.8 %copy-start.2 = (f32[256]{0:T(256)S(1)}, f32[256]{0:T(256)}, u32[]{:S(2)}) copy-start(f32[256]{0:T(256)} %coupling_ref) | copy-start | bytes 3076
  0.0 15.8 %copy-start.3 = (f32[256]{0:T(256)S(1)}, f32[256]{0:T(256)}, u32[]{:S(2)}) copy-start(f32[256]{0:T(256)} %mf_ref) | copy-start | bytes 3076
  0.0 15.8 %copy-start.4 = (f32[8]{0:T(128)S(1)}, f32[8]{0:T(128)}, u32[]{:S(2)}) copy-start(f32[8]{0:T(128)} %lag_ref) | copy-start | bytes 100
  0.0 21.9 %copy-start = (bf16[512,256]{1,0:T(8,128)(2,1)S(1)}, bf16[512,256]{1,0:T(8,128)(2,1)}, u32[]{:S(2)}) copy-start(bf16[512,256]{1,0:T(8,128)(2,1)} %constant.27.clone.high_ref) | copy-start | bytes 786436
  0.0 21.9 %copy-start.1 = (bf16[512,256]{1,0:T(8,128)(2,1)S(1)}, bf16[512,256]{1,0:T(8,128)(2,1)}, u32[]{:S(2)}) copy-start(bf16[512,256]{1,0:T(8,128)(2,1)} %constant.28.clone.low_ref) | copy-start | bytes 786436
  1.7 1.6 %collective-permute-start = (f32[2,16,16,128]{3,2,1,0:T(8,128)S(1)}, f32[2,16,16,128]{3,2,1,0:T(8,128)S(1)}, u32[]{:S(2)}, u32[]{:S(2)}) collective-permute-start(f32[2,16,16,128]{3,2,1,0:T(8,128)S(1)} %get-tuple-element.48), channel_id=1, source_target_pairs={{0,1},{1,0},{2,3},{3,2},{4,5},{5,4},{6,7},{7,6},{8,9},{9,8},{10,11... | collective-permute-start | bytes 786440 | tf_op jit(solution)/shard_map/ppermute | solution.py:601
  4.5 17.4 %all-to-all-start = ((f32[32,16,128]{2,1,0:T(8,128)}), f32[32,16,128]{2,1,0:T(8,128)S(1)}, u32[]{:S(2)}, u32[]{:S(2)}) async-start(f32[32,16,128]{2,1,0:T(8,128)} %bitcast.2), calls=%async_computation | async-start | bytes 524288 | tf_op jit(solution)/shard_map/all_to_all | solution.py:658
  11.6 14.9 %collective-permute-start.3 = (f32[4,8,16,256]{3,2,1,0:T(8,128)S(1)}, f32[4,8,16,256]{3,2,1,0:T(8,128)}, u32[]{:S(2)}, u32[]{:S(2)}) collective-permute-start(f32[4,8,16,256]{3,2,1,0:T(8,128)S(1)} %get-tuple-element.61), channel_id=1, source_target_pairs={{0,1},{1,0},{2,3},{3,2},{4,5},{5,4},{6,7},{7,6},{8,9},{9,8},{10,11... | collective-permute-start | bytes 1572872 | tf_op jit(solution)/shard_map/ppermute | solution.py:615
  12.0 14.6 %collective-permute-start.1 = (f32[4,8,16,256]{3,2,1,0:T(8,128)S(1)}, f32[4,8,16,256]{3,2,1,0:T(8,128)}, u32[]{:S(2)}, u32[]{:S(2)}) collective-permute-start(f32[4,8,16,256]{3,2,1,0:T(8,128)S(1)} %get-tuple-element.59), channel_id=1, source_target_pairs={{3,0},{0,1},{1,2},{2,3},{7,4},{4,5},{5,6},{6,7},{11,8},{8,9},{9,10... | collective-permute-start | bytes 1572872 | tf_op jit(solution)/shard_map/ppermute | solution.py:610
  13.5 14.8 %collective-permute-start.2 = (f32[4,8,16,256]{3,2,1,0:T(8,128)S(1)}, f32[4,8,16,256]{3,2,1,0:T(8,128)}, u32[]{:S(2)}, u32[]{:S(2)}) collective-permute-start(f32[4,8,16,256]{3,2,1,0:T(8,128)S(1)} %get-tuple-element.60), channel_id=1, source_target_pairs={{3,1},{1,2},{2,3},{0,0},{7,5},{5,6},{6,7},{4,4},{11,9},{9,10},{10,... | collective-permute-start | bytes 1572872 | tf_op jit(solution)/shard_map/ppermute | solution.py:611
  23.7 13.2 %all-to-all-start.1 = ((f32[32,16,128]{2,1,0:T(8,128)}), f32[32,16,128]{2,1,0:T(8,128)S(1)}, u32[]{:S(2)}, u32[]{:S(2)}) async-start(f32[32,16,128]{2,1,0:T(8,128)} %shard_map.85), calls=%async_computation.1 | async-start | bytes 524288 | tf_op jit(solution)/shard_map/all_to_all | solution.py:658
  62.4 11.1 %all-to-all-start.4 = ((f32[32,8,128]{2,1,0:T(8,128)}), f32[32,8,128]{2,1,0:T(8,128)S(1)}, u32[]{:S(2)}, u32[]{:S(2)}) async-start(f32[32,8,128]{2,1,0:T(8,128)} %bitcast.9), calls=%async_computation.4 | async-start | bytes 262144 | tf_op jit(solution)/shard_map/all_to_all | solution.py:641
  75.3 13.0 %all-to-all-start.5 = ((f32[32,16,128]{2,1,0:T(8,128)}), f32[32,16,128]{2,1,0:T(8,128)S(1)}, u32[]{:S(2)}, u32[]{:S(2)}) async-start(f32[32,16,128]{2,1,0:T(8,128)} %shard_map.91), calls=%async_computation.5 | async-start | bytes 524288 | tf_op jit(solution)/shard_map/all_to_all | solution.py:641
  88.3 4.5 %collective-permute-start.5 = (f32[512,128]{1,0:T(8,128)S(1)}, f32[512,128]{1,0:T(8,128)S(1)}, u32[]{:S(2)}, u32[]{:S(2)}) collective-permute-start(f32[512,128]{1,0:T(8,128)S(1)} %bitcast.14), channel_id=1, source_target_pairs={{0,1},{1,0},{2,3},{3,2},{4,5},{5,4},{6,7},{7,6},{8,9},{9,8},{10,11... | collective-permute-start | bytes 786440 | tf_op jit(solution)/shard_map/ppermute | solution.py:727
  88.9 7.9 %collective-permute-start.4 = (f32[512,128]{1,0:T(8,128)S(1)}, f32[512,128]{1,0:T(8,128)S(1)}, u32[]{:S(2)}, u32[]{:S(2)}) collective-permute-start(f32[512,128]{1,0:T(8,128)S(1)} %bitcast.15), channel_id=1, source_target_pairs={{0,2},{1,3},{2,0},{3,1},{4,6},{5,7},{6,4},{7,5},{8,10},{9,11},{10,... | collective-permute-start | bytes 786440 | tf_op jit(solution)/shard_map/ppermute | solution.py:727
  96.8 4.7 %collective-permute-start.6 = (f32[512,128]{1,0:T(8,128)S(1)}, f32[512,128]{1,0:T(8,128)S(1)}, u32[]{:S(2)}, u32[]{:S(2)}) collective-permute-start(f32[512,128]{1,0:T(8,128)S(1)} %collective-permute-done.4.arrived_ref), channel_id=1, source_target_pairs={{0,1},{1,0},{2,3},{3,2},{4,5},{5,4},{6,7},{7,6},{8,9},{9,8},{10,11... | collective-permute-start | bytes 786440 | tf_op jit(solution)/shard_map/ppermute | solution.py:727

commit v8 on v7

--- a/solution.py
+++ b/solution.py
@@ -553,7 +553,8 @@
             start_all(arriving(number))
     coming = [pltpu.make_async_copy(source_ref, next_ref, arrive.at[groups])] if following else []
     start_all(coming)
-    lax.fori_loop(0, groups, one, 0)
+    for number in range(groups):
+        one(number, 0)
     wait_all(coming)
     for number in range(groups):
         wait_all(leaving(number))

time: 104 us -> 104 us (level)
  no operation moved by 1% of the time
where the time goes in v8:
time: 104 us
  Pallas kernels  40.7 us (39%)
  blocking collectives  22.7 us (22%)
  starting transfers between devices  21 us (20%)
  waiting for transfers between devices  17.4 us (17%)
  local copies, waits for them, and re-layouts  1.26 us (1%)
    all_to_all x2, blocking collectives, send_alone(): return lax.all_to_all(sent, both_axes, 0, 0, tiled=True)  22.7 us
    pallas_call x2, Pallas kernels, send_beside(): pl.pallas_call(final_ladder_kernel, out_shape=[pltpu.HBM(ladder_shape, jn...  12.8 us
    pallas_call x4, Pallas kernels, finish(): pl.pallas_call(functools.partial(final_kernel, own, fetched, len(followin...  11.9 us
    all_to_all x2, starting transfers between devices, send_alone(): return lax.all_to_all(sent, both_axes, 0, 0, tiled=True)  9.87 us
    all_to_all x2, waiting for transfers between devices, send_alone(): return lax.all_to_all(sent, both_axes, 0, 0, tiled=True)  7.81 us
    pallas_call x6, Pallas kernels, call(): pl.pallas_call(kernel, out_shape=shapes, in_specs=[SMEM if x.dtype == jnp...  7.55 us
    pallas_call x1, Pallas kernels, on_device_tiled(): pl.pallas_call(functools.partial(both_ladders_kernel, own), out_shape=(ru...  6.24 us
    all_to_all x2, waiting for transfers between devices, send_beside(): arrived = lax.all_to_all(sent, both_axes, 0, 0, tiled=True)  5.71 us
  transfers between devices with their start and end apart: 11, of which 7 were waited for; matrix products, arithmetic and copies ran while one was open for 1% of the time, Pallas kernels for 30%

profile of v8, /device:TPU:1, one launch (start us, length us, event | category | flops | bytes accessed | tf_op | source)
XLA Modules:
  0.0 103.7 jit_solution(10823068177000191899)
XLA Ops:
  0.0 0.0 copy-start.2
  0.0 0.0 copy-start.3
  0.0 0.0 copy-start.4
  0.0 0.0 copy-start
  0.0 0.0 copy-start.1
  0.0 1.7 %shard_map.82 = (f32[2,16,16,128]{3,2,1,0:T(8,128)S(1)}, f32[2,16,16,128]{3,2,1,0:T(8,128)S(1)}, f32[4,8,16,256]{3,2,1,0:T(8,128)S(1)}, f32[4,8,16,256]{3,2,1,0:T(8,128)S(1)}, f32[4,8,16,256]{3,2,1,0:T(8,128)S(1)}) custom-call(s32[1]{0:T(128)} %bitcast.1.tm_ref, f32[2,32,16,512]{3,2,1,0:T(8,128)} %retarded_ref.4, f32[2,32,16,512]{3,2,1,0:T(8,128)} %lesser_ref.4), custom_call_target="tpu_custom_call" | custom-call | tf_op jit(solution)/shard_map/pallas_call | solution.py:593
  1.7 0.1 collective-permute-start
  1.8 1.2 %copy.12.refs_0_.propagator_ref = f32[2,32,16,16]{3,2,1,0:T(8,128)S(1)} copy(f32[2,32,16,16]{1,3,2,0:T(8,128)} %param.10) | data formatting | bytes 131072 | tf_op args[2]
  3.0 0.3 collective-permute-done.refs_1_
  3.3 1.2 %shard_map.83 = f32[512,128]{1,0:T(8,128)} custom-call(s32[1]{0:T(128)} %bitcast.1.tm_ref, f32[2,32,16,16]{3,2,1,0:T(8,128)S(1)} %copy.12.refs_0_.propagator_ref, f32[2,16,16,128]{3,2,1,0:T(8,128)S(1)} %collective-permute-done.refs_1_, f32[2,16,16,128]{3,2,1,0:T(8,128)S(1)} %get-tuple-element.49.refs_2_), custom_call_target="tpu_custom_call" | custom-call | tf_op jit(solution)/shard_map/pallas_call | solution.py:580
  4.5 7.1 %all-to-all-start = ((f32[32,16,128]{2,1,0:T(8,128)}), f32[32,16,128]{2,1,0:T(8,128)S(1)}, u32[]{:S(2)}, u32[]{:S(2)}) async-start(f32[32,16,128]{2,1,0:T(8,128)} %bitcast.2), calls=%async_computation | async-start | bytes 524288 | tf_op jit(solution)/shard_map/all_to_all | solution.py:659
  11.6 0.3 collective-permute-start.3
  11.9 1.5 %collective-permute-start.1 = (f32[4,8,16,256]{3,2,1,0:T(8,128)S(1)}, f32[4,8,16,256]{3,2,1,0:T(8,128)}, u32[]{:S(2)}, u32[]{:S(2)}) collective-permute-start(f32[4,8,16,256]{3,2,1,0:T(8,128)S(1)} %get-tuple-element.59), channel_id=1, source_target_pairs={{3,0},{0,1},{1,2},{2,3},{7,4},{4,5},{5,6},{6,7},{11,8},{8,9},{9,10... | collective-permute-start | bytes 1572872 | tf_op jit(solution)/shard_map/ppermute | solution.py:611
  13.4 2.3 %collective-permute-start.2 = (f32[4,8,16,256]{3,2,1,0:T(8,128)S(1)}, f32[4,8,16,256]{3,2,1,0:T(8,128)}, u32[]{:S(2)}, u32[]{:S(2)}) collective-permute-start(f32[4,8,16,256]{3,2,1,0:T(8,128)S(1)} %get-tuple-element.60), channel_id=1, source_target_pairs={{3,1},{1,2},{2,3},{0,0},{7,5},{5,6},{6,7},{4,4},{11,9},{9,10},{10,... | collective-permute-start | bytes 1572872 | tf_op jit(solution)/shard_map/ppermute | solution.py:612
  15.7 0.0 copy-done.2
  15.7 0.0 copy-done.3
  15.7 0.0 copy-done.4
  15.8 0.6 shard_map.84
  16.4 5.5 %all-to-all-done = f32[32,16,128]{2,1,0:T(8,128)S(1)} async-done(((f32[32,16,128]{2,1,0:T(8,128)}), f32[32,16,128]{2,1,0:T(8,128)S(1)}, u32[]{:S(2)}, u32[]{:S(2)}) %all-to-all-start) | async-done | bytes 262176 | tf_op jit(solution)/shard_map/all_to_all | solution.py:659
  21.9 0.0 copy-done
  21.9 0.0 copy-done.1
  21.9 1.8 %shard_map.85 = f32[32,16,128]{2,1,0:T(8,128)} custom-call(f32[8,4,16,128]{3,2,1,0:T(8,128)S(1)} %bitcast.18, bf16[512,256]{1,0:T(8,128)(2,1)S(1)} %copy-done, bf16[512,256]{1,0:T(8,128)(2,1)S(1)} %copy-done.1, f32[1,128]{1,0:T(1,128)S(1)} %get-tuple-element.55.strength_ref, f32[1,128]{1,0:T(1,128)S(1)} %get-tuple-element.56.mean_ref), custom_call_target="tpu_custom_call" | custom-call | tf_op jit(solution)/shard_map/pallas_call | solution.py:580
  23.6 2.8 %all-to-all-start.1 = ((f32[32,16,128]{2,1,0:T(8,128)}), f32[32,16,128]{2,1,0:T(8,128)S(1)}, u32[]{:S(2)}, u32[]{:S(2)}) async-start(f32[32,16,128]{2,1,0:T(8,128)} %shard_map.85), calls=%async_computation.1 | async-start | bytes 524288 | tf_op jit(solution)/shard_map/all_to_all | solution.py:659
  26.4 0.1 pad_add_fusion
  26.5 0.0 collective-permute-done.3.others_2_
  26.5 0.0 collective-permute-done.1.others_0_
  26.5 1.7 %collective-permute-done.2.others_1_ = f32[4,8,16,256]{3,2,1,0:T(8,128)} collective-permute-done((f32[4,8,16,256]{3,2,1,0:T(8,128)S(1)}, f32[4,8,16,256]{3,2,1,0:T(8,128)}, u32[]{:S(2)}, u32[]{:S(2)}) %collective-permute-start.2) | collective-permute-done | bytes 524320 | tf_op jit(solution)/shard_map/ppermute | solution.py:612
  28.3 6.2 %shard_map.86 = (bf16[8,256,256]{2,1,0:T(8,128)(2,1)S(1)}, bf16[8,256,256]{2,1,0:T(8,128)(2,1)S(1)}, bf16[8,768,256]{2,1,0:T(8,128)(2,1)}) custom-call(s32[2]{0:T(128)S(1)} %get-tuple-element.91.tm_ref, f32[2,32,16,512]{3,2,1,0:T(8,128)} %retarded_ref.4, f32[2,32,16,512]{3,2,1,0:T(8,128)} %lesser_ref.4, f32[4,8,16,256]{3,2,1,0:T(8,128)} %collective-permute-done.1.others_0_, ...), custom_call_target="tpu_custom_call" | custom-call | tf_op jit(solution)/shard_map/pallas_call | solution.py:677
  34.5 2.3 %all-to-all-done.1 = f32[32,16,128]{2,1,0:T(8,128)S(1)} async-done(((f32[32,16,128]{2,1,0:T(8,128)}), f32[32,16,128]{2,1,0:T(8,128)S(1)}, u32[]{:S(2)}, u32[]{:S(2)}) %all-to-all-start.1) | async-done | bytes 262176 | tf_op jit(solution)/shard_map/all_to_all | solution.py:659
  36.8 0.5 shard_map.87
  37.4 10.6 %all_to_all.30 = f32[32,8,128]{2,1,0:T(8,128)S(1)} all-to-all(f32[32,8,128]{2,1,0:T(8,128)S(1)} %bitcast.20), channel_id=1, replica_groups=mesh['mom'=8,'tm'=4] {'mom','tm'}, dimensions={0} | all-to-all | bytes 262144 | tf_op jit(solution)/shard_map/all_to_all | solution.py:659
  48.0 1.1 %shard_map.88 = f32[32,16,128]{2,1,0:T(8,128)S(1)} custom-call(f32[8,4,8,128]{3,2,1,0:T(8,128)S(1)} %bitcast.22, bf16[512,256]{1,0:T(8,128)(2,1)S(1)} %copy-done, bf16[512,256]{1,0:T(8,128)(2,1)S(1)} %copy-done.1, f32[1,128]{1,0:T(1,128)S(1)} %get-tuple-element.55.strength_ref, f32[1,128]{1,0:T(1,128)S(1)} %get-tuple-element.56.mean_ref), custom_call_target="tpu_custom_call" | custom-call | tf_op jit(solution)/shard_map/pallas_call | solution.py:580
  49.1 12.1 %all_to_all.31 = f32[32,16,128]{2,1,0:T(8,128)S(1)} all-to-all(f32[32,16,128]{2,1,0:T(8,128)S(1)} %shard_map.88), channel_id=1, replica_groups=mesh['mom'=8,'tm'=4] {'mom','tm'}, dimensions={0} | all-to-all | bytes 524288 | tf_op jit(solution)/shard_map/all_to_all | solution.py:659
  61.2 1.2 %shard_map.89 = f32[256,128]{1,0:T(8,128)} custom-call(f32[512,128]{1,0:T(8,128)S(1)} %bitcast.19, f32[2,8,16,16]{3,2,1,0:T(8,128)S(1)} %constant_dynamic-slice_fusion.propagator_ref, bf16[8,256,256]{2,1,0:T(8,128)(2,1)S(1)} %get-tuple-element.63.high_ref, bf16[8,256,256]{2,1,0:T(8,128)(2,1)S(1)} %get-tuple-element.64.low_ref), custom_call_target="tpu_custom_call" | custom-call | tf_op jit(solution)/shard_map/pallas_call | solution.py:580
  62.4 2.8 %all-to-all-start.4 = ((f32[32,8,128]{2,1,0:T(8,128)}), f32[32,8,128]{2,1,0:T(8,128)S(1)}, u32[]{:S(2)}, u32[]{:S(2)}) async-start(f32[32,8,128]{2,1,0:T(8,128)} %bitcast.9), calls=%async_computation.4 | async-start | bytes 262144 | tf_op jit(solution)/shard_map/all_to_all | solution.py:642
  65.2 0.1 pad_add_fusion.1.tm_ref
  65.2 5.0 %shard_map.90.others_0_ = bf16[8,768,256]{2,1,0:T(8,128)(2,1)} custom-call(s32[2]{0:T(128)S(1)} %pad_add_fusion.1.tm_ref, f32[2,32,16,512]{3,2,1,0:T(8,128)} %retarded_ref.4, f32[2,32,16,512]{3,2,1,0:T(8,128)} %lesser_ref.4, f32[4,8,16,256]{3,2,1,0:T(8,128)} %collective-permute-done.1.others_0_, f32[4,8,16,256]{3,2,1,0:T(8,128)} %collective-permute-done.2.others_1_, ...), custom_call_target="tpu_custom_call" | custom-call | tf_op jit(solution)/shard_map/pallas_call | solution.py:643
  70.2 3.3 %all-to-all-done.4 = f32[32,8,128]{2,1,0:T(8,128)S(1)} async-done(((f32[32,8,128]{2,1,0:T(8,128)}), f32[32,8,128]{2,1,0:T(8,128)S(1)}, u32[]{:S(2)}, u32[]{:S(2)}) %all-to-all-start.4) | async-done | bytes 131104 | tf_op jit(solution)/shard_map/all_to_all | solution.py:642
  73.5 1.8 %shard_map.91 = f32[32,16,128]{2,1,0:T(8,128)} custom-call(f32[8,4,8,128]{3,2,1,0:T(8,128)S(1)} %bitcast.21, bf16[512,256]{1,0:T(8,128)(2,1)S(1)} %copy-done, bf16[512,256]{1,0:T(8,128)(2,1)S(1)} %copy-done.1, f32[1,128]{1,0:T(1,128)S(1)} %get-tuple-element.55.strength_ref, f32[1,128]{1,0:T(1,128)S(1)} %get-tuple-element.56.mean_ref), custom_call_target="tpu_custom_call" | custom-call | tf_op jit(solution)/shard_map/pallas_call | solution.py:580
  75.3 2.7 %all-to-all-start.5 = ((f32[32,16,128]{2,1,0:T(8,128)}), f32[32,16,128]{2,1,0:T(8,128)S(1)}, u32[]{:S(2)}, u32[]{:S(2)}) async-start(f32[32,16,128]{2,1,0:T(8,128)} %shard_map.91), calls=%async_computation.5 | async-start | bytes 524288 | tf_op jit(solution)/shard_map/all_to_all | solution.py:642
  78.0 7.8 %shard_map.92 = (bf16[8,768,256]{2,1,0:T(8,128)(2,1)}, bf16[8,768,256]{2,1,0:T(8,128)(2,1)}) custom-call(s32[2]{0:T(128)S(1)} %get-tuple-element.92.tm_ref, f32[2,32,16,512]{3,2,1,0:T(8,128)} %retarded_ref.4, f32[2,32,16,512]{3,2,1,0:T(8,128)} %lesser_ref.4, f32[4,8,16,256]{3,2,1,0:T(8,128)} %collective-permute-done.1.others_0_, ...), custom_call_target="tpu_custom_call" | custom-call | tf_op jit(solution)/shard_map/pallas_call | solution.py:643
  85.8 2.4 %all-to-all-done.5 = f32[32,16,128]{2,1,0:T(8,128)S(1)} async-done(((f32[32,16,128]{2,1,0:T(8,128)}), f32[32,16,128]{2,1,0:T(8,128)S(1)}, u32[]{:S(2)}, u32[]{:S(2)}) %all-to-all-start.5) | async-done | bytes 262176 | tf_op jit(solution)/shard_map/all_to_all | solution.py:642
  88.2 0.6 collective-permute-start.5
  88.8 0.0 collective-permute-start.4
  88.9 3.9 %shard_map.93 = (f32[2,32,16,512]{3,2,1,0:T(8,128)}, bf16[8,768,256]{2,1,0:T(8,128)(2,1)S(1)}) custom-call(s32[1]{0:T(128)} %bitcast.1.tm_ref, f32[512,128]{1,0:T(8,128)S(1)} %bitcast.16, f32[2,32,16,16]{3,2,1,0:T(8,128)S(1)} %copy.12.refs_0_.propagator_ref, bf16[8,768,256]{2,1,0:T(8,128)(2,1)} %get-tuple-element.81.ladder_ref, ...), custom_call_target="tpu_custom_call" | custom-call | tf_op jit(solution)/shard_map/pallas_call | solution.py:716
  92.7 0.0 collective-permute-done.5.arrived_ref
  92.8 2.1 %shard_map.94.others_1_ = f32[2,32,16,512]{3,2,1,0:T(8,128)} custom-call(s32[1]{0:T(128)} %bitcast.10.tm_ref, f32[512,128]{1,0:T(8,128)S(1)} %collective-permute-done.5.arrived_ref, f32[2,32,16,16]{3,2,1,0:T(8,128)S(1)} %copy.12.refs_0_.propagator_ref, bf16[8,768,256]{2,1,0:T(8,128)(2,1)S(1)} %get-tuple-element.83.ladder_ref, ...), custom_call_target="tpu_custom_call", output_to_operand_aliasing={{}: (4, {})} | custom-call | tf_op jit(solution)/shard_map/pallas_call | solution.py:716
  94.8 1.9 %collective-permute-done.4.arrived_ref = f32[512,128]{1,0:T(8,128)S(1)} collective-permute-done((f32[512,128]{1,0:T(8,128)S(1)}, f32[512,128]{1,0:T(8,128)S(1)}, u32[]{:S(2)}, u32[]{:S(2)}) %collective-permute-start.4) | collective-permute-done | bytes 262176 | tf_op jit(solution)/shard_map/ppermute | solution.py:728
  96.8 0.8 collective-permute-start.6
  97.6 3.9 %shard_map.95 = (f32[2,32,16,512]{3,2,1,0:T(8,128)}, bf16[8,768,256]{2,1,0:T(8,128)(2,1)S(1)}) custom-call(s32[1]{0:T(128)} %bitcast.12.tm_ref, f32[512,128]{1,0:T(8,128)S(1)} %collective-permute-done.4.arrived_ref, f32[2,32,16,16]{3,2,1,0:T(8,128)S(1)} %copy.12.refs_0_.propagator_ref, ...), custom_call_target="tpu_custom_call", output_to_operand_aliasing={{0}: (5, {})} | custom-call | tf_op jit(solution)/shard_map/pallas_call | solution.py:716
  101.4 0.0 collective-permute-done.6.arrived_ref
  101.4 2.1 %shard_map.96 = f32[2,32,16,512]{3,2,1,0:T(8,128)} custom-call(s32[1]{0:T(128)} %bitcast.tm_ref, f32[512,128]{1,0:T(8,128)S(1)} %collective-permute-done.6.arrived_ref, f32[2,32,16,16]{3,2,1,0:T(8,128)S(1)} %copy.12.refs_0_.propagator_ref, bf16[8,768,256]{2,1,0:T(8,128)(2,1)S(1)} %get-tuple-element.89.ladder_ref, ...), custom_call_target="tpu_custom_call", output_to_operand_aliasing={{}: (4, {})} | custom-call | tf_op jit(solution)/shard_map/pallas_call | solution.py:716
  (1 shorter events, 0.0 us)
Async XLA Ops:
  0.0 15.7 %copy-start.2 = (f32[256]{0:T(256)S(1)}, f32[256]{0:T(256)}, u32[]{:S(2)}) copy-start(f32[256]{0:T(256)} %coupling_ref) | copy-start | bytes 3076
  0.0 15.7 %copy-start.3 = (f32[256]{0:T(256)S(1)}, f32[256]{0:T(256)}, u32[]{:S(2)}) copy-start(f32[256]{0:T(256)} %mf_ref) | copy-start | bytes 3076
  0.0 15.7 %copy-start.4 = (f32[8]{0:T(128)S(1)}, f32[8]{0:T(128)}, u32[]{:S(2)}) copy-start(f32[8]{0:T(128)} %lag_ref) | copy-start | bytes 100
  0.0 21.9 %copy-start = (bf16[512,256]{1,0:T(8,128)(2,1)S(1)}, bf16[512,256]{1,0:T(8,128)(2,1)}, u32[]{:S(2)}) copy-start(bf16[512,256]{1,0:T(8,128)(2,1)} %constant.27.clone.high_ref) | copy-start | bytes 786436
  0.0 21.9 %copy-start.1 = (bf16[512,256]{1,0:T(8,128)(2,1)S(1)}, bf16[512,256]{1,0:T(8,128)(2,1)}, u32[]{:S(2)}) copy-start(bf16[512,256]{1,0:T(8,128)(2,1)} %constant.28.clone.low_ref) | copy-start | bytes 786436
  1.7 1.6 %collective-permute-start = (f32[2,16,16,128]{3,2,1,0:T(8,128)S(1)}, f32[2,16,16,128]{3,2,1,0:T(8,128)S(1)}, u32[]{:S(2)}, u32[]{:S(2)}) collective-permute-start(f32[2,16,16,128]{3,2,1,0:T(8,128)S(1)} %get-tuple-element.48), channel_id=1, source_target_pairs={{0,1},{1,0},{2,3},{3,2},{4,5},{5,4},{6,7},{7,6},{8,9},{9,8},{10,11... | collective-permute-start | bytes 786440 | tf_op jit(solution)/shard_map/ppermute | solution.py:602
  4.5 17.4 %all-to-all-start = ((f32[32,16,128]{2,1,0:T(8,128)}), f32[32,16,128]{2,1,0:T(8,128)S(1)}, u32[]{:S(2)}, u32[]{:S(2)}) async-start(f32[32,16,128]{2,1,0:T(8,128)} %bitcast.2), calls=%async_computation | async-start | bytes 524288 | tf_op jit(solution)/shard_map/all_to_all | solution.py:659
  11.6 14.9 %collective-permute-start.3 = (f32[4,8,16,256]{3,2,1,0:T(8,128)S(1)}, f32[4,8,16,256]{3,2,1,0:T(8,128)}, u32[]{:S(2)}, u32[]{:S(2)}) collective-permute-start(f32[4,8,16,256]{3,2,1,0:T(8,128)S(1)} %get-tuple-element.61), channel_id=1, source_target_pairs={{0,1},{1,0},{2,3},{3,2},{4,5},{5,4},{6,7},{7,6},{8,9},{9,8},{10,11... | collective-permute-start | bytes 1572872 | tf_op jit(solution)/shard_map/ppermute | solution.py:616
  11.9 14.6 %collective-permute-start.1 = (f32[4,8,16,256]{3,2,1,0:T(8,128)S(1)}, f32[4,8,16,256]{3,2,1,0:T(8,128)}, u32[]{:S(2)}, u32[]{:S(2)}) collective-permute-start(f32[4,8,16,256]{3,2,1,0:T(8,128)S(1)} %get-tuple-element.59), channel_id=1, source_target_pairs={{3,0},{0,1},{1,2},{2,3},{7,4},{4,5},{5,6},{6,7},{11,8},{8,9},{9,10... | collective-permute-start | bytes 1572872 | tf_op jit(solution)/shard_map/ppermute | solution.py:611
  13.4 14.8 %collective-permute-start.2 = (f32[4,8,16,256]{3,2,1,0:T(8,128)S(1)}, f32[4,8,16,256]{3,2,1,0:T(8,128)}, u32[]{:S(2)}, u32[]{:S(2)}) collective-permute-start(f32[4,8,16,256]{3,2,1,0:T(8,128)S(1)} %get-tuple-element.60), channel_id=1, source_target_pairs={{3,1},{1,2},{2,3},{0,0},{7,5},{5,6},{6,7},{4,4},{11,9},{9,10},{10,... | collective-permute-start | bytes 1572872 | tf_op jit(solution)/shard_map/ppermute | solution.py:612
  23.6 13.2 %all-to-all-start.1 = ((f32[32,16,128]{2,1,0:T(8,128)}), f32[32,16,128]{2,1,0:T(8,128)S(1)}, u32[]{:S(2)}, u32[]{:S(2)}) async-start(f32[32,16,128]{2,1,0:T(8,128)} %shard_map.85), calls=%async_computation.1 | async-start | bytes 524288 | tf_op jit(solution)/shard_map/all_to_all | solution.py:659
  62.4 11.1 %all-to-all-start.4 = ((f32[32,8,128]{2,1,0:T(8,128)}), f32[32,8,128]{2,1,0:T(8,128)S(1)}, u32[]{:S(2)}, u32[]{:S(2)}) async-start(f32[32,8,128]{2,1,0:T(8,128)} %bitcast.9), calls=%async_computation.4 | async-start | bytes 262144 | tf_op jit(solution)/shard_map/all_to_all | solution.py:642
  75.3 13.0 %all-to-all-start.5 = ((f32[32,16,128]{2,1,0:T(8,128)}), f32[32,16,128]{2,1,0:T(8,128)S(1)}, u32[]{:S(2)}, u32[]{:S(2)}) async-start(f32[32,16,128]{2,1,0:T(8,128)} %shard_map.91), calls=%async_computation.5 | async-start | bytes 524288 | tf_op jit(solution)/shard_map/all_to_all | solution.py:642
  88.2 4.5 %collective-permute-start.5 = (f32[512,128]{1,0:T(8,128)S(1)}, f32[512,128]{1,0:T(8,128)S(1)}, u32[]{:S(2)}, u32[]{:S(2)}) collective-permute-start(f32[512,128]{1,0:T(8,128)S(1)} %bitcast.14), channel_id=1, source_target_pairs={{0,1},{1,0},{2,3},{3,2},{4,5},{5,4},{6,7},{7,6},{8,9},{9,8},{10,11... | collective-permute-start | bytes 786440 | tf_op jit(solution)/shard_map/ppermute | solution.py:728
  88.8 7.9 %collective-permute-start.4 = (f32[512,128]{1,0:T(8,128)S(1)}, f32[512,128]{1,0:T(8,128)S(1)}, u32[]{:S(2)}, u32[]{:S(2)}) collective-permute-start(f32[512,128]{1,0:T(8,128)S(1)} %bitcast.15), channel_id=1, source_target_pairs={{0,2},{1,3},{2,0},{3,1},{4,6},{5,7},{6,4},{7,5},{8,10},{9,11},{10,... | collective-permute-start | bytes 786440 | tf_op jit(solution)/shard_map/ppermute | solution.py:728
  96.8 4.7 %collective-permute-start.6 = (f32[512,128]{1,0:T(8,128)S(1)}, f32[512,128]{1,0:T(8,128)S(1)}, u32[]{:S(2)}, u32[]{:S(2)}) collective-permute-start(f32[512,128]{1,0:T(8,128)S(1)} %collective-permute-done.4.arrived_ref), channel_id=1, source_target_pairs={{0,1},{1,0},{2,3},{3,2},{4,5},{5,4},{6,7},{7,6},{8,9},{9,8},{10,11... | collective-permute-start | bytes 786440 | tf_op jit(solution)/shard_map/ppermute | solution.py:728

commit v9 on v8

--- a/solution.py
+++ b/solution.py
@@ -232,7 +232,7 @@
     for number in range(8):
         part, half, quarter = number // 4, number // 2 % 2, number % 2
         source = ref.at[part, pl.ds((2 * half + quarter) * own, own), :, pl.ds(ref.shape[3] - TILE, TILE)]
-        target = near_ref.at[2 * part + half, :, :, pl.ds(quarter * TILE, TILE)]
+        target = near_ref.at[2 * half + part, :, :, pl.ds(quarter * TILE, TILE)]
         copies.append(pltpu.make_async_copy(source, target, semaphores.at[number]))
     return copies
 
@@ -411,26 +411,30 @@
     low_ref = ladder_ref.at[:, rows_each:]
     own = count // len(outs)
     blocks = len(outs)
-    momenta = pl.ds(tm_ref[1] // blocks * count, count)
-    fetches = start_all(
-        [
+    base = tm_ref[1] // blocks * count
+    chunk = count // 2
+
+    def fetches(number):
+        rows = pl.ds(number * chunk, chunk)
+        return [
             pltpu.make_async_copy(
-                ref.at[:, momenta],
-                region_ref.at[pl.ds(2 * kind, 2), :, :, pl.ds(TILE, ref.shape[3])],
-                arrive.at[kind],
+                ref.at[:, pl.ds(base + number * chunk, chunk)],
+                region_ref.at[pl.ds(2 * kind, 2), rows, :, pl.ds(TILE, ref.shape[3])],
+                arrive.at[kind, number],
             )
             for kind, ref in enumerate((retarded_ref, lesser_ref))
         ]
-    )
+
+    order = [number ^ (tm_ref[1] % blocks) for number in range(2)]
+    start_all(fetches(order[0]))
 
     def rims(second, quarters):
         copies = []
         for kind, ref in enumerate((rim_refs[0], rim_refs[second])):
-            for part in range(2):
-                for number, quarter in enumerate(quarters):
-                    source = ref.at[2 * part + tm_ref[1] // 2, :, :, pl.ds(quarter * TILE, TILE)]
-                    target = region_ref.at[2 * kind + part, pl.ds(number * own, own), :, pl.ds(0, TILE)]
-                    copies.append(pltpu.make_async_copy(source, target, arrive_rim.at[2 * kind + part, number]))
+            for number, quarter in enumerate(quarters):
+                source = ref.at[pl.ds(tm_ref[1] // 2 * 2, 2), :, :, pl.ds(quarter * TILE, TILE)]
+                target = region_ref.at[pl.ds(2 * kind, 2), pl.ds(number * own, own), :, pl.ds(0, TILE)]
+                copies.append(pltpu.make_async_copy(source, target, arrive_rim.at[kind, number]))
         return copies
 
     @pl.when(tm_ref[0] == 0)
@@ -446,9 +450,9 @@
                     act(rims(second, quarters))
 
     each_rims(start_all)
+    start_all(fetches(order[1]))
     meanwhile()
     each_rims(wait_all)
-    wait_all(fetches)
 
     def leaving(block, n):
         k = block * own + n
@@ -477,8 +481,10 @@
         start_all(leaving(block, n))
         return carry
 
-    for block in range(blocks):
-        lax.fori_loop(0, own, functools.partial(one, block), 0)
+    for number in range(2):
+        wait_all(fetches(order[number]))
+        block, first = (number, 0) if blocks == 2 else (0, number * chunk)
+        lax.fori_loop(first, first + chunk, functools.partial(one, block), 0)
     for block in range(blocks):
         lax.fori_loop(0, own, lambda n, c: (wait_all(leaving(block, n)), c)[1], 0)
 
@@ -632,8 +638,8 @@
         return [
             pltpu.VMEM((4, blocks * own, ORB, TILE + columns), jnp.float32),
             pltpu.VMEM((blocks * own, *ladder_shape[1:]), jnp.bfloat16),
-            pltpu.SemaphoreType.DMA((2,)),
-            pltpu.SemaphoreType.DMA((4, 2)),
+            pltpu.SemaphoreType.DMA((2, 2)),
+            pltpu.SemaphoreType.DMA((2, 2)),
             pltpu.SemaphoreType.DMA((blocks * own,)),
         ]
 

time: 104 us -> 104 us (level)
  no operation moved by 1% of the time
where the time goes in v9:
time: 104 us
  Pallas kernels  40.3 us (39%)
  blocking collectives  22.7 us (22%)
  starting transfers between devices  20.8 us (20%)
  waiting for transfers between devices  17.9 us (17%)
  local copies, waits for them, and re-layouts  1.26 us (1%)
    all_to_all x2, blocking collectives, send_alone(): return lax.all_to_all(sent, both_axes, 0, 0, tiled=True)  22.7 us
    pallas_call x2, Pallas kernels, send_beside(): pl.pallas_call(final_ladder_kernel, out_shape=[pltpu.HBM(ladder_shape, jn...  12.4 us
    pallas_call x4, Pallas kernels, finish(): pl.pallas_call(functools.partial(final_kernel, own, fetched, len(followin...  11.9 us
    all_to_all x2, starting transfers between devices, send_alone(): return lax.all_to_all(sent, both_axes, 0, 0, tiled=True)  9.87 us
    all_to_all x2, waiting for transfers between devices, send_alone(): return lax.all_to_all(sent, both_axes, 0, 0, tiled=True)  7.83 us
    pallas_call x6, Pallas kernels, call(): pl.pallas_call(kernel, out_shape=shapes, in_specs=[SMEM if x.dtype == jnp...  7.55 us
    pallas_call x1, Pallas kernels, on_device_tiled(): pl.pallas_call(functools.partial(both_ladders_kernel, own), out_shape=(ru...  6.22 us
    all_to_all x2, waiting for transfers between devices, send_beside(): arrived = lax.all_to_all(sent, both_axes, 0, 0, tiled=True)  6.14 us
  transfers between devices with their start and end apart: 11, of which 7 were waited for; matrix products, arithmetic and copies ran while one was open for 1% of the time, Pallas kernels for 30%

profile of v9, /device:TPU:1, one launch (start us, length us, event | category | flops | bytes accessed | tf_op | source)
XLA Modules:
  0.0 103.6 jit_solution(3756748485517447327)
XLA Ops:
  0.0 0.0 copy-start.2
  0.0 0.0 copy-start.3
  0.0 0.0 copy-start.4
  0.0 0.0 copy-start
  0.0 0.0 copy-start.1
  0.0 1.7 %shard_map.82 = (f32[2,16,16,128]{3,2,1,0:T(8,128)S(1)}, f32[2,16,16,128]{3,2,1,0:T(8,128)S(1)}, f32[4,8,16,256]{3,2,1,0:T(8,128)S(1)}, f32[4,8,16,256]{3,2,1,0:T(8,128)S(1)}, f32[4,8,16,256]{3,2,1,0:T(8,128)S(1)}) custom-call(s32[1]{0:T(128)} %bitcast.1.tm_ref, f32[2,32,16,512]{3,2,1,0:T(8,128)} %retarded_ref.4, f32[2,32,16,512]{3,2,1,0:T(8,128)} %lesser_ref.4), custom_call_target="tpu_custom_call" | custom-call | tf_op jit(solution)/shard_map/pallas_call | solution.py:599
  1.7 0.1 collective-permute-start
  1.8 1.2 %copy.12.refs_0_.propagator_ref = f32[2,32,16,16]{3,2,1,0:T(8,128)S(1)} copy(f32[2,32,16,16]{1,3,2,0:T(8,128)} %param.10) | data formatting | bytes 131072 | tf_op args[2]
  3.0 0.3 collective-permute-done.refs_1_
  3.3 1.2 %shard_map.83 = f32[512,128]{1,0:T(8,128)} custom-call(s32[1]{0:T(128)} %bitcast.1.tm_ref, f32[2,32,16,16]{3,2,1,0:T(8,128)S(1)} %copy.12.refs_0_.propagator_ref, f32[2,16,16,128]{3,2,1,0:T(8,128)S(1)} %collective-permute-done.refs_1_, f32[2,16,16,128]{3,2,1,0:T(8,128)S(1)} %get-tuple-element.49.refs_2_), custom_call_target="tpu_custom_call" | custom-call | tf_op jit(solution)/shard_map/pallas_call | solution.py:586
  4.5 7.1 %all-to-all-start = ((f32[32,16,128]{2,1,0:T(8,128)}), f32[32,16,128]{2,1,0:T(8,128)S(1)}, u32[]{:S(2)}, u32[]{:S(2)}) async-start(f32[32,16,128]{2,1,0:T(8,128)} %bitcast.2), calls=%async_computation | async-start | bytes 524288 | tf_op jit(solution)/shard_map/all_to_all | solution.py:665
  11.6 0.3 collective-permute-start.3
  11.9 1.5 %collective-permute-start.1 = (f32[4,8,16,256]{3,2,1,0:T(8,128)S(1)}, f32[4,8,16,256]{3,2,1,0:T(8,128)}, u32[]{:S(2)}, u32[]{:S(2)}) collective-permute-start(f32[4,8,16,256]{3,2,1,0:T(8,128)S(1)} %get-tuple-element.59), channel_id=1, source_target_pairs={{3,0},{0,1},{1,2},{2,3},{7,4},{4,5},{5,6},{6,7},{11,8},{8,9},{9,10... | collective-permute-start | bytes 1572872 | tf_op jit(solution)/shard_map/ppermute | solution.py:617
  13.4 2.3 %collective-permute-start.2 = (f32[4,8,16,256]{3,2,1,0:T(8,128)S(1)}, f32[4,8,16,256]{3,2,1,0:T(8,128)}, u32[]{:S(2)}, u32[]{:S(2)}) collective-permute-start(f32[4,8,16,256]{3,2,1,0:T(8,128)S(1)} %get-tuple-element.60), channel_id=1, source_target_pairs={{3,1},{1,2},{2,3},{0,0},{7,5},{5,6},{6,7},{4,4},{11,9},{9,10},{10,... | collective-permute-start | bytes 1572872 | tf_op jit(solution)/shard_map/ppermute | solution.py:618
  15.7 0.0 copy-done.2
  15.7 0.0 copy-done.3
  15.7 0.0 copy-done.4
  15.8 0.6 shard_map.84
  16.4 5.5 %all-to-all-done = f32[32,16,128]{2,1,0:T(8,128)S(1)} async-done(((f32[32,16,128]{2,1,0:T(8,128)}), f32[32,16,128]{2,1,0:T(8,128)S(1)}, u32[]{:S(2)}, u32[]{:S(2)}) %all-to-all-start) | async-done | bytes 262176 | tf_op jit(solution)/shard_map/all_to_all | solution.py:665
  21.9 0.0 copy-done
  21.9 0.0 copy-done.1
  21.9 1.8 %shard_map.85 = f32[32,16,128]{2,1,0:T(8,128)} custom-call(f32[8,4,16,128]{3,2,1,0:T(8,128)S(1)} %bitcast.18, bf16[512,256]{1,0:T(8,128)(2,1)S(1)} %copy-done, bf16[512,256]{1,0:T(8,128)(2,1)S(1)} %copy-done.1, f32[1,128]{1,0:T(1,128)S(1)} %get-tuple-element.55.strength_ref, f32[1,128]{1,0:T(1,128)S(1)} %get-tuple-element.56.mean_ref), custom_call_target="tpu_custom_call" | custom-call | tf_op jit(solution)/shard_map/pallas_call | solution.py:586
  23.6 2.8 %all-to-all-start.1 = ((f32[32,16,128]{2,1,0:T(8,128)}), f32[32,16,128]{2,1,0:T(8,128)S(1)}, u32[]{:S(2)}, u32[]{:S(2)}) async-start(f32[32,16,128]{2,1,0:T(8,128)} %shard_map.85), calls=%async_computation.1 | async-start | bytes 524288 | tf_op jit(solution)/shard_map/all_to_all | solution.py:665
  26.4 0.1 pad_add_fusion
  26.5 0.0 collective-permute-done.3.others_2_
  26.5 0.0 collective-permute-done.1.others_0_
  26.5 1.7 %collective-permute-done.2.others_1_ = f32[4,8,16,256]{3,2,1,0:T(8,128)} collective-permute-done((f32[4,8,16,256]{3,2,1,0:T(8,128)S(1)}, f32[4,8,16,256]{3,2,1,0:T(8,128)}, u32[]{:S(2)}, u32[]{:S(2)}) %collective-permute-start.2) | collective-permute-done | bytes 524320 | tf_op jit(solution)/shard_map/ppermute | solution.py:618
  28.3 6.2 %shard_map.86 = (bf16[8,256,256]{2,1,0:T(8,128)(2,1)S(1)}, bf16[8,256,256]{2,1,0:T(8,128)(2,1)S(1)}, bf16[8,768,256]{2,1,0:T(8,128)(2,1)}) custom-call(s32[2]{0:T(128)S(1)} %get-tuple-element.91.tm_ref, f32[2,32,16,512]{3,2,1,0:T(8,128)} %retarded_ref.4, f32[2,32,16,512]{3,2,1,0:T(8,128)} %lesser_ref.4, f32[4,8,16,256]{3,2,1,0:T(8,128)} %collective-permute-done.1.others_0_, ...), custom_call_target="tpu_custom_call" | custom-call | tf_op jit(solution)/shard_map/pallas_call | solution.py:683
  34.5 2.3 %all-to-all-done.1 = f32[32,16,128]{2,1,0:T(8,128)S(1)} async-done(((f32[32,16,128]{2,1,0:T(8,128)}), f32[32,16,128]{2,1,0:T(8,128)S(1)}, u32[]{:S(2)}, u32[]{:S(2)}) %all-to-all-start.1) | async-done | bytes 262176 | tf_op jit(solution)/shard_map/all_to_all | solution.py:665
  36.8 0.5 shard_map.87
  37.4 10.6 %all_to_all.30 = f32[32,8,128]{2,1,0:T(8,128)S(1)} all-to-all(f32[32,8,128]{2,1,0:T(8,128)S(1)} %bitcast.20), channel_id=1, replica_groups=mesh['mom'=8,'tm'=4] {'mom','tm'}, dimensions={0} | all-to-all | bytes 262144 | tf_op jit(solution)/shard_map/all_to_all | solution.py:665
  48.0 1.1 %shard_map.88 = f32[32,16,128]{2,1,0:T(8,128)S(1)} custom-call(f32[8,4,8,128]{3,2,1,0:T(8,128)S(1)} %bitcast.22, bf16[512,256]{1,0:T(8,128)(2,1)S(1)} %copy-done, bf16[512,256]{1,0:T(8,128)(2,1)S(1)} %copy-done.1, f32[1,128]{1,0:T(1,128)S(1)} %get-tuple-element.55.strength_ref, f32[1,128]{1,0:T(1,128)S(1)} %get-tuple-element.56.mean_ref), custom_call_target="tpu_custom_call" | custom-call | tf_op jit(solution)/shard_map/pallas_call | solution.py:586
  49.1 12.1 %all_to_all.31 = f32[32,16,128]{2,1,0:T(8,128)S(1)} all-to-all(f32[32,16,128]{2,1,0:T(8,128)S(1)} %shard_map.88), channel_id=1, replica_groups=mesh['mom'=8,'tm'=4] {'mom','tm'}, dimensions={0} | all-to-all | bytes 524288 | tf_op jit(solution)/shard_map/all_to_all | solution.py:665
  61.2 1.2 %shard_map.89 = f32[256,128]{1,0:T(8,128)} custom-call(f32[512,128]{1,0:T(8,128)S(1)} %bitcast.19, f32[2,8,16,16]{3,2,1,0:T(8,128)S(1)} %constant_dynamic-slice_fusion.propagator_ref, bf16[8,256,256]{2,1,0:T(8,128)(2,1)S(1)} %get-tuple-element.63.high_ref, bf16[8,256,256]{2,1,0:T(8,128)(2,1)S(1)} %get-tuple-element.64.low_ref), custom_call_target="tpu_custom_call" | custom-call | tf_op jit(solution)/shard_map/pallas_call | solution.py:586
  62.4 2.8 %all-to-all-start.4 = ((f32[32,8,128]{2,1,0:T(8,128)}), f32[32,8,128]{2,1,0:T(8,128)S(1)}, u32[]{:S(2)}, u32[]{:S(2)}) async-start(f32[32,8,128]{2,1,0:T(8,128)} %bitcast.9), calls=%async_computation.4 | async-start | bytes 262144 | tf_op jit(solution)/shard_map/all_to_all | solution.py:648
  65.2 0.1 pad_add_fusion.1.tm_ref
  65.2 4.8 %shard_map.90.others_0_ = bf16[8,768,256]{2,1,0:T(8,128)(2,1)} custom-call(s32[2]{0:T(128)S(1)} %pad_add_fusion.1.tm_ref, f32[2,32,16,512]{3,2,1,0:T(8,128)} %retarded_ref.4, f32[2,32,16,512]{3,2,1,0:T(8,128)} %lesser_ref.4, f32[4,8,16,256]{3,2,1,0:T(8,128)} %collective-permute-done.1.others_0_, f32[4,8,16,256]{3,2,1,0:T(8,128)} %collective-permute-done.2.others_1_, ...), custom_call_target="tpu_custom_call" | custom-call | tf_op jit(solution)/shard_map/pallas_call | solution.py:649
  70.1 3.4 %all-to-all-done.4 = f32[32,8,128]{2,1,0:T(8,128)S(1)} async-done(((f32[32,8,128]{2,1,0:T(8,128)}), f32[32,8,128]{2,1,0:T(8,128)S(1)}, u32[]{:S(2)}, u32[]{:S(2)}) %all-to-all-start.4) | async-done | bytes 131104 | tf_op jit(solution)/shard_map/all_to_all | solution.py:648
  73.5 1.8 %shard_map.91 = f32[32,16,128]{2,1,0:T(8,128)} custom-call(f32[8,4,8,128]{3,2,1,0:T(8,128)S(1)} %bitcast.21, bf16[512,256]{1,0:T(8,128)(2,1)S(1)} %copy-done, bf16[512,256]{1,0:T(8,128)(2,1)S(1)} %copy-done.1, f32[1,128]{1,0:T(1,128)S(1)} %get-tuple-element.55.strength_ref, f32[1,128]{1,0:T(1,128)S(1)} %get-tuple-element.56.mean_ref), custom_call_target="tpu_custom_call" | custom-call | tf_op jit(solution)/shard_map/pallas_call | solution.py:586
  75.3 2.6 %all-to-all-start.5 = ((f32[32,16,128]{2,1,0:T(8,128)}), f32[32,16,128]{2,1,0:T(8,128)S(1)}, u32[]{:S(2)}, u32[]{:S(2)}) async-start(f32[32,16,128]{2,1,0:T(8,128)} %shard_map.91), calls=%async_computation.5 | async-start | bytes 524288 | tf_op jit(solution)/shard_map/all_to_all | solution.py:648
  77.8 7.6 %shard_map.92 = (bf16[8,768,256]{2,1,0:T(8,128)(2,1)}, bf16[8,768,256]{2,1,0:T(8,128)(2,1)}) custom-call(s32[2]{0:T(128)S(1)} %get-tuple-element.92.tm_ref, f32[2,32,16,512]{3,2,1,0:T(8,128)} %retarded_ref.4, f32[2,32,16,512]{3,2,1,0:T(8,128)} %lesser_ref.4, f32[4,8,16,256]{3,2,1,0:T(8,128)} %collective-permute-done.1.others_0_, ...), custom_call_target="tpu_custom_call" | custom-call | tf_op jit(solution)/shard_map/pallas_call | solution.py:649
  85.4 2.7 %all-to-all-done.5 = f32[32,16,128]{2,1,0:T(8,128)S(1)} async-done(((f32[32,16,128]{2,1,0:T(8,128)}), f32[32,16,128]{2,1,0:T(8,128)S(1)}, u32[]{:S(2)}, u32[]{:S(2)}) %all-to-all-start.5) | async-done | bytes 262176 | tf_op jit(solution)/shard_map/all_to_all | solution.py:648
  88.2 0.6 collective-permute-start.5
  88.7 0.0 collective-permute-start.4
  88.8 3.9 %shard_map.93 = (f32[2,32,16,512]{3,2,1,0:T(8,128)}, bf16[8,768,256]{2,1,0:T(8,128)(2,1)S(1)}) custom-call(s32[1]{0:T(128)} %bitcast.1.tm_ref, f32[512,128]{1,0:T(8,128)S(1)} %bitcast.16, f32[2,32,16,16]{3,2,1,0:T(8,128)S(1)} %copy.12.refs_0_.propagator_ref, bf16[8,768,256]{2,1,0:T(8,128)(2,1)} %get-tuple-element.81.ladder_ref, ...), custom_call_target="tpu_custom_call" | custom-call | tf_op jit(solution)/shard_map/pallas_call | solution.py:722
  92.7 0.0 collective-permute-done.5.arrived_ref
  92.7 2.1 %shard_map.94.others_1_ = f32[2,32,16,512]{3,2,1,0:T(8,128)} custom-call(s32[1]{0:T(128)} %bitcast.10.tm_ref, f32[512,128]{1,0:T(8,128)S(1)} %collective-permute-done.5.arrived_ref, f32[2,32,16,16]{3,2,1,0:T(8,128)S(1)} %copy.12.refs_0_.propagator_ref, bf16[8,768,256]{2,1,0:T(8,128)(2,1)S(1)} %get-tuple-element.83.ladder_ref, ...), custom_call_target="tpu_custom_call", output_to_operand_aliasing={{}: (4, {})} | custom-call | tf_op jit(solution)/shard_map/pallas_call | solution.py:722
  94.8 1.9 %collective-permute-done.4.arrived_ref = f32[512,128]{1,0:T(8,128)S(1)} collective-permute-done((f32[512,128]{1,0:T(8,128)S(1)}, f32[512,128]{1,0:T(8,128)S(1)}, u32[]{:S(2)}, u32[]{:S(2)}) %collective-permute-start.4) | collective-permute-done | bytes 262176 | tf_op jit(solution)/shard_map/ppermute | solution.py:734
  96.7 0.8 collective-permute-start.6
  97.5 3.9 %shard_map.95 = (f32[2,32,16,512]{3,2,1,0:T(8,128)}, bf16[8,768,256]{2,1,0:T(8,128)(2,1)S(1)}) custom-call(s32[1]{0:T(128)} %bitcast.12.tm_ref, f32[512,128]{1,0:T(8,128)S(1)} %collective-permute-done.4.arrived_ref, f32[2,32,16,16]{3,2,1,0:T(8,128)S(1)} %copy.12.refs_0_.propagator_ref, ...), custom_call_target="tpu_custom_call", output_to_operand_aliasing={{0}: (5, {})} | custom-call | tf_op jit(solution)/shard_map/pallas_call | solution.py:722
  101.3 0.0 collective-permute-done.6.arrived_ref
  101.4 2.1 %shard_map.96 = f32[2,32,16,512]{3,2,1,0:T(8,128)} custom-call(s32[1]{0:T(128)} %bitcast.tm_ref, f32[512,128]{1,0:T(8,128)S(1)} %collective-permute-done.6.arrived_ref, f32[2,32,16,16]{3,2,1,0:T(8,128)S(1)} %copy.12.refs_0_.propagator_ref, bf16[8,768,256]{2,1,0:T(8,128)(2,1)S(1)} %get-tuple-element.89.ladder_ref, ...), custom_call_target="tpu_custom_call", output_to_operand_aliasing={{}: (4, {})} | custom-call | tf_op jit(solution)/shard_map/pallas_call | solution.py:722
  (1 shorter events, 0.0 us)
Async XLA Ops:
  0.0 15.7 %copy-start.2 = (f32[256]{0:T(256)S(1)}, f32[256]{0:T(256)}, u32[]{:S(2)}) copy-start(f32[256]{0:T(256)} %coupling_ref) | copy-start | bytes 3076
  0.0 15.7 %copy-start.3 = (f32[256]{0:T(256)S(1)}, f32[256]{0:T(256)}, u32[]{:S(2)}) copy-start(f32[256]{0:T(256)} %mf_ref) | copy-start | bytes 3076
  0.0 15.7 %copy-start.4 = (f32[8]{0:T(128)S(1)}, f32[8]{0:T(128)}, u32[]{:S(2)}) copy-start(f32[8]{0:T(128)} %lag_ref) | copy-start | bytes 100
  0.0 21.9 %copy-start = (bf16[512,256]{1,0:T(8,128)(2,1)S(1)}, bf16[512,256]{1,0:T(8,128)(2,1)}, u32[]{:S(2)}) copy-start(bf16[512,256]{1,0:T(8,128)(2,1)} %constant.27.clone.high_ref) | copy-start | bytes 786436
  0.0 21.9 %copy-start.1 = (bf16[512,256]{1,0:T(8,128)(2,1)S(1)}, bf16[512,256]{1,0:T(8,128)(2,1)}, u32[]{:S(2)}) copy-start(bf16[512,256]{1,0:T(8,128)(2,1)} %constant.28.clone.low_ref) | copy-start | bytes 786436
  1.7 1.6 %collective-permute-start = (f32[2,16,16,128]{3,2,1,0:T(8,128)S(1)}, f32[2,16,16,128]{3,2,1,0:T(8,128)S(1)}, u32[]{:S(2)}, u32[]{:S(2)}) collective-permute-start(f32[2,16,16,128]{3,2,1,0:T(8,128)S(1)} %get-tuple-element.48), channel_id=1, source_target_pairs={{0,1},{1,0},{2,3},{3,2},{4,5},{5,4},{6,7},{7,6},{8,9},{9,8},{10,11... | collective-permute-start | bytes 786440 | tf_op jit(solution)/shard_map/ppermute | solution.py:608
  4.5 17.4 %all-to-all-start = ((f32[32,16,128]{2,1,0:T(8,128)}), f32[32,16,128]{2,1,0:T(8,128)S(1)}, u32[]{:S(2)}, u32[]{:S(2)}) async-start(f32[32,16,128]{2,1,0:T(8,128)} %bitcast.2), calls=%async_computation | async-start | bytes 524288 | tf_op jit(solution)/shard_map/all_to_all | solution.py:665
  11.6 14.9 %collective-permute-start.3 = (f32[4,8,16,256]{3,2,1,0:T(8,128)S(1)}, f32[4,8,16,256]{3,2,1,0:T(8,128)}, u32[]{:S(2)}, u32[]{:S(2)}) collective-permute-start(f32[4,8,16,256]{3,2,1,0:T(8,128)S(1)} %get-tuple-element.61), channel_id=1, source_target_pairs={{0,1},{1,0},{2,3},{3,2},{4,5},{5,4},{6,7},{7,6},{8,9},{9,8},{10,11... | collective-permute-start | bytes 1572872 | tf_op jit(solution)/shard_map/ppermute | solution.py:622
  11.9 14.6 %collective-permute-start.1 = (f32[4,8,16,256]{3,2,1,0:T(8,128)S(1)}, f32[4,8,16,256]{3,2,1,0:T(8,128)}, u32[]{:S(2)}, u32[]{:S(2)}) collective-permute-start(f32[4,8,16,256]{3,2,1,0:T(8,128)S(1)} %get-tuple-element.59), channel_id=1, source_target_pairs={{3,0},{0,1},{1,2},{2,3},{7,4},{4,5},{5,6},{6,7},{11,8},{8,9},{9,10... | collective-permute-start | bytes 1572872 | tf_op jit(solution)/shard_map/ppermute | solution.py:617
  13.4 14.8 %collective-permute-start.2 = (f32[4,8,16,256]{3,2,1,0:T(8,128)S(1)}, f32[4,8,16,256]{3,2,1,0:T(8,128)}, u32[]{:S(2)}, u32[]{:S(2)}) collective-permute-start(f32[4,8,16,256]{3,2,1,0:T(8,128)S(1)} %get-tuple-element.60), channel_id=1, source_target_pairs={{3,1},{1,2},{2,3},{0,0},{7,5},{5,6},{6,7},{4,4},{11,9},{9,10},{10,... | collective-permute-start | bytes 1572872 | tf_op jit(solution)/shard_map/ppermute | solution.py:618
  23.6 13.2 %all-to-all-start.1 = ((f32[32,16,128]{2,1,0:T(8,128)}), f32[32,16,128]{2,1,0:T(8,128)S(1)}, u32[]{:S(2)}, u32[]{:S(2)}) async-start(f32[32,16,128]{2,1,0:T(8,128)} %shard_map.85), calls=%async_computation.1 | async-start | bytes 524288 | tf_op jit(solution)/shard_map/all_to_all | solution.py:665
  62.4 11.1 %all-to-all-start.4 = ((f32[32,8,128]{2,1,0:T(8,128)}), f32[32,8,128]{2,1,0:T(8,128)S(1)}, u32[]{:S(2)}, u32[]{:S(2)}) async-start(f32[32,8,128]{2,1,0:T(8,128)} %bitcast.9), calls=%async_computation.4 | async-start | bytes 262144 | tf_op jit(solution)/shard_map/all_to_all | solution.py:648
  75.3 12.9 %all-to-all-start.5 = ((f32[32,16,128]{2,1,0:T(8,128)}), f32[32,16,128]{2,1,0:T(8,128)S(1)}, u32[]{:S(2)}, u32[]{:S(2)}) async-start(f32[32,16,128]{2,1,0:T(8,128)} %shard_map.91), calls=%async_computation.5 | async-start | bytes 524288 | tf_op jit(solution)/shard_map/all_to_all | solution.py:648
  88.2 4.5 %collective-permute-start.5 = (f32[512,128]{1,0:T(8,128)S(1)}, f32[512,128]{1,0:T(8,128)S(1)}, u32[]{:S(2)}, u32[]{:S(2)}) collective-permute-start(f32[512,128]{1,0:T(8,128)S(1)} %bitcast.14), channel_id=1, source_target_pairs={{0,1},{1,0},{2,3},{3,2},{4,5},{5,4},{6,7},{7,6},{8,9},{9,8},{10,11... | collective-permute-start | bytes 786440 | tf_op jit(solution)/shard_map/ppermute | solution.py:734
  88.7 7.9 %collective-permute-start.4 = (f32[512,128]{1,0:T(8,128)S(1)}, f32[512,128]{1,0:T(8,128)S(1)}, u32[]{:S(2)}, u32[]{:S(2)}) collective-permute-start(f32[512,128]{1,0:T(8,128)S(1)} %bitcast.15), channel_id=1, source_target_pairs={{0,2},{1,3},{2,0},{3,1},{4,6},{5,7},{6,4},{7,5},{8,10},{9,11},{10,... | collective-permute-start | bytes 786440 | tf_op jit(solution)/shard_map/ppermute | solution.py:734
  96.7 4.7 %collective-permute-start.6 = (f32[512,128]{1,0:T(8,128)S(1)}, f32[512,128]{1,0:T(8,128)S(1)}, u32[]{:S(2)}, u32[]{:S(2)}) collective-permute-start(f32[512,128]{1,0:T(8,128)S(1)} %collective-permute-done.4.arrived_ref), channel_id=1, source_target_pairs={{0,1},{1,0},{2,3},{3,2},{4,5},{5,4},{6,7},{7,6},{8,9},{9,8},{10,11... | collective-permute-start | bytes 786440 | tf_op jit(solution)/shard_map/ppermute | solution.py:734
